TPU v7x, 512 devices: a whole 4x8x8 slice. The times are simulated.
512 devices in a mesh: dom: 32 (over x, z), member: 16 (over y, core).
Axes of the slice: x: 4, y: 8, z: 8, core: 2. Of those that a mesh axis runs over, the one named last changes fastest.
Arguments:
- features: bfloat16 [131072, 256], P(('dom', 'member')), may hold values from -6 to 6
- cotangent: bfloat16 [131072, 256], P(('dom', 'member')), may hold values from -6 to 6
- edge_src: int32 [32, 16, 4096], P('dom', 'member'), may hold values from -1 to 4095, as said below
- edge_dst: int32 [32, 16, 4096], P('dom', 'member'), may hold values from -1 to 4095, as said below
- send_rows: int32 [32, 16, 32, 4], P('dom', 'member'), may hold values from -1 to 255, as said below
- recv_rows: int32 [32, 16, 32, 4], P('dom', 'member'), may hold values from -1 to 193, as said below
- in_degree: int32 [32, 16, 256], P('dom', 'member'), may hold values from 0 to 2097168, as said below
- weight_self: bfloat16 [256, 256], replicated, may hold values from -0.375 to 0.375
- weight_neigh: bfloat16 [256, 256], replicated, may hold values from -0.375 to 0.375
Outputs:
- activated: bfloat16 [131072, 256], P(('dom', 'member'))
- grad_features: bfloat16 [131072, 256], P(('dom', 'member'))
- grad_self: float32 [256, 256], replicated
- grad_neigh: float32 [256, 256], replicated
Inputs may be any that keep to these rules, and one draw needn't show every extreme that they name: Live edge slots of a device form a prefix; edge_src and edge_dst are -1 together exactly on the padding. Some device of every partition has all 4096 slots live. `edge_dst`: same padding as edge_src. `send_rows`: each of a device's 62 mirror rows (its last 62 rows) appears in exactly one slot; no slot to the device's own partition; at most 4 slots to one peer, and exactly 4 to some peer of every device. recv_rows[q, m, p, k] >= 0 exactly where send_rows[p, m, q, k] >= 0; it names a master row (below 194), distinct over k for one q, m, p. `in_degree`: equal at all replicas of a vertex.
All inputs are finite; a program needn't handle non-finite values.
Results may differ from a plain program's by a relative error of at most 0.018.
Values may be sent and summed in bfloat16 or wider, within the bound.
No kernel may reach another device: no remote copies, remote signals or barrier semaphores. Data moves between devices by JAX's collectives and lax.ppermute only.
A program may use at most 64 MiB of HBM per device.

v0:
```python
import jax
import jax.numpy as jnp
from jax import lax
from jax.sharding import PartitionSpec as P

TILE = 128


def body(
    features,
    cotangent,
    edge_src,
    edge_dst,
    send_rows,
    recv_rows,
    in_degree,
    weight_self,
    weight_neigh,
):
    row_count, feat_width = features.shape
    dom_count = lax.axis_size("dom")
    part_rows = row_count * lax.axis_size("member")
    send_list = send_rows.reshape(-1)
    recv_list = recv_rows.reshape(-1)
    columns = lax.broadcasted_iota(jnp.int32, (send_list.shape[0], row_count), 1)
    pick_send = (send_list[:, None] == columns).astype(jnp.bfloat16)
    pick_recv = (recv_list[:, None] == columns).astype(jnp.bfloat16)
    is_mirror = jnp.sum(pick_send.astype(jnp.float32), axis=0) > 0.5
    mirror_col = is_mirror[:, None]
    denominator = in_degree.reshape(-1).astype(jnp.float32)[:, None] + 1.0
    contract_first = (((0,), (0,)), ((), ()))

    def exchange_slots(slots):
        moved = lax.all_to_all(
            slots.reshape(dom_count, -1, feat_width), "dom", split_axis=0, concat_axis=0, tiled=True
        )
        return moved.reshape(-1, feat_width)

    def to_mirrors(values):
        slots = jnp.dot(pick_recv, values, preferred_element_type=jnp.float32).astype(jnp.bfloat16)
        arrived = lax.dot_general(
            pick_send, exchange_slots(slots), contract_first, preferred_element_type=jnp.float32
        )
        return jnp.where(mirror_col, arrived.astype(jnp.bfloat16), values)

    def to_masters(values):
        slots = jnp.dot(
            pick_send, values.astype(jnp.bfloat16), preferred_element_type=jnp.float32
        ).astype(jnp.bfloat16)
        arrived = lax.dot_general(
            pick_recv, exchange_slots(slots), contract_first, preferred_element_type=jnp.float32
        )
        return values + arrived

    def gather_rows(values):
        return lax.all_gather(values, "member", axis=0, tiled=True)

    def member_reduce(partial_rows):
        return lax.psum_scatter(
            partial_rows.astype(jnp.bfloat16), "member", scatter_dimension=0, tiled=True
        ).astype(jnp.float32)

    def edge_pass(source_table, take_rows, place_rows):
        edge_total = take_rows.shape[0]
        block_size = TILE * 4

        def block_step(block_at, accum):
            take_block = lax.dynamic_slice_in_dim(take_rows, block_at * block_size, block_size)
            place_block = lax.dynamic_slice_in_dim(place_rows, block_at * block_size, block_size)
            usable = take_block >= 0
            messages = source_table[jnp.where(usable, take_block, 0)].astype(jnp.float32)
            landing_rows = jnp.where(usable, place_block, part_rows)
            return accum.at[landing_rows].add(messages, mode="drop")

        block_total = edge_total // block_size
        start_acc = jnp.zeros((part_rows, feat_width), jnp.float32)
        return lax.fori_loop(0, block_total, block_step, start_acc)

    source_edges = edge_src.reshape(-1)
    dest_edges = edge_dst.reshape(-1)
    pulled = to_mirrors(features)
    member_total = member_reduce(
        edge_pass(gather_rows(pulled), source_edges, dest_edges)
        .astype(jnp.bfloat16)
        .astype(jnp.float32)
    )
    totals = to_masters(member_total)
    averaged = (totals / denominator).astype(jnp.bfloat16)
    averaged = to_mirrors(averaged)
    pre = jnp.dot(pulled, weight_self, preferred_element_type=jnp.float32) + jnp.dot(
        averaged, weight_neigh, preferred_element_type=jnp.float32
    )
    gate_sig = jax.nn.sigmoid(pre)
    activated = (pre * gate_sig).astype(jnp.bfloat16)
    slope = gate_sig * (1.0 + pre * (1.0 - gate_sig))
    grad_pre = jnp.where(mirror_col, 0.0, cotangent.astype(jnp.float32) * slope).astype(
        jnp.bfloat16
    )
    local_self = lax.dot_general(
        pulled, grad_pre, contract_first, preferred_element_type=jnp.float32
    )
    local_neigh = lax.dot_general(
        averaged, grad_pre, contract_first, preferred_element_type=jnp.float32
    )
    grad_mean = (
        jnp.dot(grad_pre, weight_neigh.T, preferred_element_type=jnp.float32) / denominator
    ).astype(jnp.bfloat16)
    grad_mean = to_mirrors(grad_mean)
    back_total = member_reduce(
        edge_pass(gather_rows(grad_mean), dest_edges, source_edges)
        .astype(jnp.bfloat16)
        .astype(jnp.float32)
    )
    back_sum = to_masters(back_total)
    self_term = jnp.dot(grad_pre, weight_self.T, preferred_element_type=jnp.float32)
    grad_features = jnp.where(mirror_col, 0.0, back_sum + self_term).astype(jnp.bfloat16)
    weight_sums = lax.psum((local_self, local_neigh), ("dom", "member"))
    return (activated, grad_features, weight_sums[0], weight_sums[1])


def solution(mesh):
    placed = (
        P(("dom", "member"), None),
        P(("dom", "member"), None),
        P("dom", "member", None),
        P("dom", "member", None),
        P("dom", "member", None, None),
        P("dom", "member", None, None),
        P("dom", "member", None),
        P(),
        P(),
    )
    return jax.shard_map(
        body,
        mesh=mesh,
        in_specs=placed,
        out_specs=(P(("dom", "member"), None), P(("dom", "member"), None), P(), P()),
        check_vma=False,
    )
```

profile of v0, /device:TPU:1, one launch (start us, length us, event | category | flops | bytes accessed | tf_op | source)
XLA Modules:
  0.0 741.4 jit_solution(7744046046455393651)
XLA Ops:
  9.9 13.7 %all-to-all-start = ((bf16[32,4,256]{2,1,0:T(4,128)(2,1)}), bf16[32,4,256]{2,1,0:T(4,128)(2,1)S(1)}, u32[]{:S(2)}, u32[]{:S(2)}) async-start(bf16[32,4,256]{2,1,0:T(4,128)(2,1)} %reshape.60), calls=%async_computation | async-start | bytes 131072 | tf_op jit(solution)/shard_map/all_to_all | solution.py:34
  34.4 38.7 %all-gather.3.cloned.1.call-done = bf16[4096,256]{1,0:T(8,128)(2,1)} async-done(((bf16[256,256]{1,0:T(8,128)(2,1)}), bf16[4096,256]{1,0:T(8,128)(2,1)}) %all-gather.3.cloned.1.call-update) | async-done | bytes 2097168 | tf_op jit(solution)/shard_map/all_gather | solution.py:56
  75.5 75.1 %while.26 = (s32[]{:T(128)}, f32[4096,256]{1,0:T(8,128)}, s32[4096]{0:T(1024)}, s32[4096]{0:T(1024)}, bf16[4096,256]{1,0:T(8,128)(2,1)S(1)}, /*index=5*/s32[]{:T(128)}, s32[]{:T(128)}, s32[]{:T(128)}, s32[]{:T(128)}) while((s32[]{:T(128)}, f32[4096,256]{1,0:T(8,128)}, s32[4096]{0:T(1024)}, s32[4096]{0:T(1024)}, ...), condition=%wide.region_3.4_spmd, body=%wide.region_1.3_spmd.sunk | while | flops 267782 | bytes 6310039 | solution.py:77
  76.3 8.6 %scatter_custom_fusion.9 = f32[4096,256]{1,0:T(8,128)} fusion(f32[4096,256]{1,0:T(8,128)} %get-tuple-element.302, s32[512]{0:T(512)S(1)} %get-tuple-element.283, bf16[4096,256]{1,0:T(8,128)(2,1)S(1)} %get-tuple-element.314, s32[1024]{0:T(1024)S(1)} %pad_clamp_fusion.4), kind=kCustom, calls=%fused_computation.4.clone.1 | custom fusion | flops 262144 | bytes 6295552 | tf_op jit(solution)/shard_map/while/body/eval_jaxpr/scatter-add | solution.py:73
  85.7 8.6 %scatter_custom_fusion.9 = f32[4096,256]{1,0:T(8,128)} fusion(f32[4096,256]{1,0:T(8,128)} %get-tuple-element.302, s32[512]{0:T(512)S(1)} %get-tuple-element.283, bf16[4096,256]{1,0:T(8,128)(2,1)S(1)} %get-tuple-element.314, s32[1024]{0:T(1024)S(1)} %pad_clamp_fusion.4), kind=kCustom, calls=%fused_computation.4.clone.1 | custom fusion | flops 262144 | bytes 6295552 | tf_op jit(solution)/shard_map/while/body/eval_jaxpr/scatter-add | solution.py:73
  95.1 8.6 %scatter_custom_fusion.9 = f32[4096,256]{1,0:T(8,128)} fusion(f32[4096,256]{1,0:T(8,128)} %get-tuple-element.302, s32[512]{0:T(512)S(1)} %get-tuple-element.283, bf16[4096,256]{1,0:T(8,128)(2,1)S(1)} %get-tuple-element.314, s32[1024]{0:T(1024)S(1)} %pad_clamp_fusion.4), kind=kCustom, calls=%fused_computation.4.clone.1 | custom fusion | flops 262144 | bytes 6295552 | tf_op jit(solution)/shard_map/while/body/eval_jaxpr/scatter-add | solution.py:73
  104.5 8.6 %scatter_custom_fusion.9 = f32[4096,256]{1,0:T(8,128)} fusion(f32[4096,256]{1,0:T(8,128)} %get-tuple-element.302, s32[512]{0:T(512)S(1)} %get-tuple-element.283, bf16[4096,256]{1,0:T(8,128)(2,1)S(1)} %get-tuple-element.314, s32[1024]{0:T(1024)S(1)} %pad_clamp_fusion.4), kind=kCustom, calls=%fused_computation.4.clone.1 | custom fusion | flops 262144 | bytes 6295552 | tf_op jit(solution)/shard_map/while/body/eval_jaxpr/scatter-add | solution.py:73
  113.9 8.6 %scatter_custom_fusion.9 = f32[4096,256]{1,0:T(8,128)} fusion(f32[4096,256]{1,0:T(8,128)} %get-tuple-element.302, s32[512]{0:T(512)S(1)} %get-tuple-element.283, bf16[4096,256]{1,0:T(8,128)(2,1)S(1)} %get-tuple-element.314, s32[1024]{0:T(1024)S(1)} %pad_clamp_fusion.4), kind=kCustom, calls=%fused_computation.4.clone.1 | custom fusion | flops 262144 | bytes 6295552 | tf_op jit(solution)/shard_map/while/body/eval_jaxpr/scatter-add | solution.py:73
  123.3 8.6 %scatter_custom_fusion.9 = f32[4096,256]{1,0:T(8,128)} fusion(f32[4096,256]{1,0:T(8,128)} %get-tuple-element.302, s32[512]{0:T(512)S(1)} %get-tuple-element.283, bf16[4096,256]{1,0:T(8,128)(2,1)S(1)} %get-tuple-element.314, s32[1024]{0:T(1024)S(1)} %pad_clamp_fusion.4), kind=kCustom, calls=%fused_computation.4.clone.1 | custom fusion | flops 262144 | bytes 6295552 | tf_op jit(solution)/shard_map/while/body/eval_jaxpr/scatter-add | solution.py:73
  142.0 8.6 %scatter_custom_fusion.9 = f32[4096,256]{1,0:T(8,128)} fusion(f32[4096,256]{1,0:T(8,128)} %get-tuple-element.302, s32[512]{0:T(512)S(1)} %get-tuple-element.283, bf16[4096,256]{1,0:T(8,128)(2,1)S(1)} %get-tuple-element.314, s32[1024]{0:T(1024)S(1)} %pad_clamp_fusion.4), kind=kCustom, calls=%fused_computation.4.clone.1 | custom fusion | flops 262144 | bytes 6295552 | tf_op jit(solution)/shard_map/while/body/eval_jaxpr/scatter-add | solution.py:73
  154.5 58.5 %reduce-scatter.3.cloned.1.call-done = bf16[256,256]{1,0:T(8,128)(2,1)} async-done(((bf16[4096,256]{1,0:T(8,128)(2,1)}), bf16[256,256]{1,0:T(8,128)(2,1)}) %reduce-scatter.3.cloned.1.call-update) | async-done | bytes 131088 | tf_op jit(solution)/shard_map/reduce_scatter | solution.py:59
  214.7 8.9 %all-to-all-start.1 = ((bf16[32,4,256]{2,1,0:T(4,128)(2,1)}), bf16[32,4,256]{2,1,0:T(4,128)(2,1)S(1)}, u32[]{:S(2)}, u32[]{:S(2)}) async-start(bf16[32,4,256]{2,1,0:T(4,128)(2,1)} %reshape.64), calls=%async_computation.2 | async-start | bytes 131072 | tf_op jit(solution)/shard_map/all_to_all | solution.py:34
  223.7 8.8 %all-to-all-done.1 = bf16[32,4,256]{2,1,0:T(4,128)(2,1)S(1)} async-done(((bf16[32,4,256]{2,1,0:T(4,128)(2,1)}), bf16[32,4,256]{2,1,0:T(4,128)(2,1)S(1)}, u32[]{:S(2)}, u32[]{:S(2)}) %all-to-all-start.1) | async-done | bytes 65568 | tf_op jit(solution)/shard_map/all_to_all | solution.py:34
  238.7 8.6 %all-to-all-done.2 = bf16[32,4,256]{2,1,0:T(4,128)(2,1)S(1)} async-done(((bf16[32,4,256]{2,1,0:T(4,128)(2,1)}), bf16[32,4,256]{2,1,0:T(4,128)(2,1)S(1)}, u32[]{:S(2)}, u32[]{:S(2)}) %all-to-all-start.2) | async-done | bytes 65568 | tf_op jit(solution)/shard_map/all_to_all | solution.py:34
  249.1 11.8 %all_to_all.25 = bf16[32,4,256]{2,1,0:T(4,128)(2,1)S(1)} all-to-all(bf16[32,4,256]{2,1,0:T(4,128)(2,1)S(1)} %reshape.68), channel_id=1, replica_groups=mesh['dom'=32,'member'=16] {'dom'}, dimensions={0} | all-to-all | bytes 131072 | tf_op jit(solution)/shard_map/all_to_all | solution.py:34
  262.1 41.1 %all-gather.5.cloned.1.call-done = bf16[4096,256]{1,0:T(8,128)(2,1)} async-done(((bf16[256,256]{1,0:T(8,128)(2,1)}), bf16[4096,256]{1,0:T(8,128)(2,1)}) %all-gather.5.cloned.1.call-update) | async-done | bytes 2097168 | tf_op jit(solution)/shard_map/all_gather | solution.py:56
  305.7 75.1 %while.27 = (s32[]{:T(128)}, f32[4096,256]{1,0:T(8,128)}, s32[4096]{0:T(1024)}, s32[4096]{0:T(1024)}, bf16[4096,256]{1,0:T(8,128)(2,1)S(1)}, /*index=5*/s32[]{:T(128)}, s32[]{:T(128)}, s32[]{:T(128)}, s32[]{:T(128)}) while((s32[]{:T(128)}, f32[4096,256]{1,0:T(8,128)}, s32[4096]{0:T(1024)}, s32[4096]{0:T(1024)}, ...), condition=%wide.region_7.8_spmd, body=%wide.region_5.7_spmd.sunk | while | flops 267782 | bytes 6310039 | solution.py:77
  344.0 8.6 %scatter_custom_fusion.11 = f32[4096,256]{1,0:T(8,128)} fusion(f32[4096,256]{1,0:T(8,128)} %get-tuple-element.329, s32[512]{0:T(512)S(1)} %get-tuple-element.290, bf16[4096,256]{1,0:T(8,128)(2,1)S(1)} %get-tuple-element.341, s32[1024]{0:T(1024)S(1)} %pad_clamp_fusion.5), kind=kCustom, calls=%fused_computation.12.clone.1 | custom fusion | flops 262144 | bytes 6295552 | tf_op jit(solution)/shard_map/while/body/eval_jaxpr/scatter-add | solution.py:73
  353.4 8.6 %scatter_custom_fusion.11 = f32[4096,256]{1,0:T(8,128)} fusion(f32[4096,256]{1,0:T(8,128)} %get-tuple-element.329, s32[512]{0:T(512)S(1)} %get-tuple-element.290, bf16[4096,256]{1,0:T(8,128)(2,1)S(1)} %get-tuple-element.341, s32[1024]{0:T(1024)S(1)} %pad_clamp_fusion.5), kind=kCustom, calls=%fused_computation.12.clone.1 | custom fusion | flops 262144 | bytes 6295552 | tf_op jit(solution)/shard_map/while/body/eval_jaxpr/scatter-add | solution.py:73
  362.8 8.6 %scatter_custom_fusion.11 = f32[4096,256]{1,0:T(8,128)} fusion(f32[4096,256]{1,0:T(8,128)} %get-tuple-element.329, s32[512]{0:T(512)S(1)} %get-tuple-element.290, bf16[4096,256]{1,0:T(8,128)(2,1)S(1)} %get-tuple-element.341, s32[1024]{0:T(1024)S(1)} %pad_clamp_fusion.5), kind=kCustom, calls=%fused_computation.12.clone.1 | custom fusion | flops 262144 | bytes 6295552 | tf_op jit(solution)/shard_map/while/body/eval_jaxpr/scatter-add | solution.py:73
  372.2 8.6 %scatter_custom_fusion.11 = f32[4096,256]{1,0:T(8,128)} fusion(f32[4096,256]{1,0:T(8,128)} %get-tuple-element.329, s32[512]{0:T(512)S(1)} %get-tuple-element.290, bf16[4096,256]{1,0:T(8,128)(2,1)S(1)} %get-tuple-element.341, s32[1024]{0:T(1024)S(1)} %pad_clamp_fusion.5), kind=kCustom, calls=%fused_computation.12.clone.1 | custom fusion | flops 262144 | bytes 6295552 | tf_op jit(solution)/shard_map/while/body/eval_jaxpr/scatter-add | solution.py:73
  385.5 57.6 %reduce-scatter.5.cloned.1.call-done = bf16[256,256]{1,0:T(8,128)(2,1)} async-done(((bf16[4096,256]{1,0:T(8,128)(2,1)}), bf16[256,256]{1,0:T(8,128)(2,1)}) %reduce-scatter.5.cloned.1.call-update) | async-done | bytes 131088 | tf_op jit(solution)/shard_map/reduce_scatter | solution.py:59
  444.8 8.9 %all-to-all-start.4 = ((bf16[32,4,256]{2,1,0:T(4,128)(2,1)}), bf16[32,4,256]{2,1,0:T(4,128)(2,1)S(1)}, u32[]{:S(2)}, u32[]{:S(2)}) async-start(bf16[32,4,256]{2,1,0:T(4,128)(2,1)} %reshape.70), calls=%async_computation.6 | async-start | bytes 131072 | tf_op jit(solution)/shard_map/all_to_all | solution.py:34
  464.7 266.8 %all-reduce.3.cloned.1.call-done = (f32[256,256]{1,0:T(8,128)}, f32[256,256]{1,0:T(8,128)}) async-done(((f32[256,256]{1,0:T(8,128)}, f32[256,256]{1,0:T(8,128)}), (f32[256,256]{1,0:T(8,128)}, f32[256,256]{1,0:T(8,128)})) %all-reduce.3.cloned.1.call-update) | async-done | bytes 524304 | tf_op jit(solution)/shard_map/psum | solution.py:117
  (103 shorter events, 109.3 us)
Async XLA Ops:
  7.2 240.5 %copy-start = (bf16[256,256]{1,0:T(8,128)(2,1)S(1)}, bf16[256,256]{1,0:T(8,128)(2,1)}, u32[]{:S(2)}) copy-start(bf16[256,256]{1,0:T(8,128)(2,1)} %param.21) | copy-start | bytes 393220
  9.9 22.6 %all-to-all-start = ((bf16[32,4,256]{2,1,0:T(4,128)(2,1)}), bf16[32,4,256]{2,1,0:T(4,128)(2,1)S(1)}, u32[]{:S(2)}, u32[]{:S(2)}) async-start(bf16[32,4,256]{2,1,0:T(4,128)(2,1)} %reshape.60), calls=%async_computation | async-start | bytes 131072 | tf_op jit(solution)/shard_map/all_to_all | solution.py:34
  23.6 49.5 %all-gather.3.cloned.1.call-start = ((), (), s32[]{:S(2)}) async-start(), calls=%async_computation.7 | async-start | bytes 2228224 | tf_op jit(solution)/shard_map/all_gather | solution.py:56
  34.3 178.6 %reduce-scatter.3.cloned.1.call-start = ((), (), s32[]{:S(2)}) async-start(), calls=%async_computation.8 | async-start | bytes 2228224 | tf_op jit(solution)/shard_map/reduce_scatter | solution.py:59
  73.1 2.4 copy-start.2
  150.6 73.0 %copy-start.5 = (s32[1,1,256]{2,1,0:T(1,128)S(1)}, s32[1,1,256]{2,1,0:T(1,128)}, u32[]{:S(2)}) copy-start(s32[1,1,256]{2,1,0:T(1,128)} %param.19) | copy-start | bytes 3076
  150.6 87.9 %copy-start.3 = (bf16[256,256]{1,0:T(8,128)(2,1)S(1)}, bf16[256,256]{1,0:T(8,128)(2,1)}, u32[]{:S(2)}) copy-start(bf16[256,256]{1,0:T(8,128)(2,1)} %fusion.11) | copy-start | bytes 393220
  150.6 87.9 %copy-start.4 = (bf16[256,256]{1,0:T(8,128)(2,1)S(1)}, bf16[256,256]{1,0:T(8,128)(2,1)}, u32[]{:S(2)}) copy-start(bf16[256,256]{1,0:T(8,128)(2,1)} %param.20) | copy-start | bytes 393220
  154.4 93.2 %copy-start.6 = (bf16[256,256]{1,0:T(8,128)(2,1)S(1)}, bf16[256,256]{1,0:T(8,128)(2,1)}, u32[]{:S(2)}) copy-start(bf16[256,256]{1,0:T(8,128)(2,1)} %param.14) | copy-start | bytes 393220
  214.7 17.8 %all-to-all-start.1 = ((bf16[32,4,256]{2,1,0:T(4,128)(2,1)}), bf16[32,4,256]{2,1,0:T(4,128)(2,1)S(1)}, u32[]{:S(2)}, u32[]{:S(2)}) async-start(bf16[32,4,256]{2,1,0:T(4,128)(2,1)} %reshape.64), calls=%async_computation.2 | async-start | bytes 131072 | tf_op jit(solution)/shard_map/all_to_all | solution.py:34
  234.6 12.7 %all-to-all-start.2 = ((bf16[32,4,256]{2,1,0:T(4,128)(2,1)}), bf16[32,4,256]{2,1,0:T(4,128)(2,1)S(1)}, u32[]{:S(2)}, u32[]{:S(2)}) async-start(bf16[32,4,256]{2,1,0:T(4,128)(2,1)} %reshape.66), calls=%async_computation.3 | async-start | bytes 131072 | tf_op jit(solution)/shard_map/all_to_all | solution.py:34
  238.5 64.8 %all-gather.5.cloned.1.call-start = ((), (), s32[]{:S(2)}) async-start(), calls=%async_computation.9 | async-start | bytes 2228224 | tf_op jit(solution)/shard_map/all_gather | solution.py:56
  261.9 181.1 %reduce-scatter.5.cloned.1.call-start = ((), (), s32[]{:S(2)}) async-start(), calls=%async_computation.10 | async-start | bytes 2228224 | tf_op jit(solution)/shard_map/reduce_scatter | solution.py:59
  303.2 2.4 copy-start.1
  444.8 17.8 %all-to-all-start.4 = ((bf16[32,4,256]{2,1,0:T(4,128)(2,1)}), bf16[32,4,256]{2,1,0:T(4,128)(2,1)S(1)}, u32[]{:S(2)}, u32[]{:S(2)}) async-start(bf16[32,4,256]{2,1,0:T(4,128)(2,1)} %reshape.70), calls=%async_computation.6 | async-start | bytes 131072 | tf_op jit(solution)/shard_map/all_to_all | solution.py:34
  453.8 277.7 %all-reduce.3.cloned.1.call-start = ((), (), s32[]{:S(2)}) async-start(), calls=%async_computation.11 | async-start | bytes 1048576 | tf_op jit(solution)/shard_map/psum | solution.py:117
Sparse Core Ops, SparseCore 0:
  34.5 38.5 all-gather.2
  154.6 58.3 reduce-scatter.2
  262.0 41.1 all-gather.4
  384.7 58.3 reduce-scatter.4
  460.0 271.4 all-reduce.2
where the time goes:
time: 743 us; the launch traced here: 741 us
  waiting for transfers between devices  496 us (67%)
  other arithmetic  158 us (21%)
  starting transfers between devices  35.8 us (5%)
  between operations  13.9 us (2%)
  matrix products  13.3 us (2%)
  local copies, waits for them, and re-layouts  12.8 us (2%)
  blocking collectives  11.8 us (2%)
    psum x1, waiting for transfers between devices, body(): weight_sums = lax.psum((local_self, local_neigh), ('dom', 'member'))  267 us
    scatter-add x16, other arithmetic, block_step(): return accum.at[landing_rows].add(messages, mode='drop')  138 us
    reduce_scatter x2, waiting for transfers between devices, member_reduce(): lax.psum_scatter(partial_rows.astype(jnp.bfloat16), 'member', scatter_dim...  116 us
    all_gather x2, waiting for transfers between devices, gather_rows(): return lax.all_gather(values, 'member', axis=0, tiled=True)  79.8 us
    all_to_all x4, starting transfers between devices, exchange_slots(): lax.all_to_all(slots.reshape(dom_count, -1, feat_width), 'dom', split_axi...  35.4 us
    all_to_all x4, waiting for transfers between devices, exchange_slots(): lax.all_to_all(slots.reshape(dom_count, -1, feat_width), 'dom', split_axi...  33.1 us
  transfers between devices with their start and end apart: 9, of which 9 were waited for; matrix products, arithmetic and copies ran while one was open for 1% of the time, Pallas kernels for 0%

commit v1 on v0

v1 whole, which is shorter than its diff:
```python
import functools

import jax
import jax.numpy as jnp
from jax import lax
from jax.experimental import pallas as pl
from jax.experimental.pallas import tpu as pltpu
from jax.sharding import Mesh, PartitionSpec as P

MIRR = 62
LATE = 64
UNROLL = 16
ACCS = 4
CHUNK = 128


def edge_kernel(
    take_high, counts_ref, packed_ref, early_ref, late_ref, early_out, late_out, table, *accs
):
    early_rows, late_rows = early_ref.shape[0], late_ref.shape[0]
    rows = early_rows + late_rows
    pad = table.shape[0] - rows

    def load(ref, base):
        def step(i, _):
            at = pl.multiple_of(i * CHUNK, CHUNK)
            table[pl.ds(base + at, CHUNK), :] = ref[pl.ds(at, CHUNK), :].astype(jnp.float32)
            for acc in accs:
                acc[pl.ds(base + at, CHUNK), :] = jnp.zeros((CHUNK, ref.shape[1]), jnp.float32)
            return 0

        lax.fori_loop(0, ref.shape[0] // CHUNK, step, 0)

    load(early_ref, 0)
    load(late_ref, early_rows)
    table[pl.ds(rows, pad), :] = jnp.zeros((pad, table.shape[1]), jnp.float32)

    for which in range(2):

        def step(i, _):
            for group in range(UNROLL // ACCS):
                takes, places = [], []
                for k in range(ACCS):
                    word = packed_ref[which, i * UNROLL + group * ACCS + k]
                    low, high = word & 0xFFFF, word >> 16
                    takes.append(high if take_high else low)
                    places.append(low if take_high else high)
                sums = [
                    accs[k][pl.ds(places[k], 1), :] + table[pl.ds(takes[k], 1), :]
                    for k in range(ACCS)
                ]
                for k in range(ACCS):
                    accs[k][pl.ds(places[k], 1), :] = sums[k]
            return 0

        lax.fori_loop(0, counts_ref[which], step, 0)

    def store(ref, base):
        def step(i, _):
            at = pl.multiple_of(i * CHUNK, CHUNK)
            total = accs[0][pl.ds(base + at, CHUNK), :]
            for acc in accs[1:]:
                total = total + acc[pl.ds(base + at, CHUNK), :]
            ref[pl.ds(at, CHUNK), :] = total.astype(ref.dtype)
            return 0

        lax.fori_loop(0, ref.shape[0] // CHUNK, step, 0)

    store(early_out, 0)
    store(late_out, early_rows)


def edge_sums(take_high, counts, packed, early, late):
    rows, width = early.shape[0] + late.shape[0], early.shape[1]
    smem = pl.BlockSpec(memory_space=pltpu.SMEM)
    vmem = pl.BlockSpec(memory_space=pltpu.VMEM)
    return pl.pallas_call(
        functools.partial(edge_kernel, take_high),
        out_shape=(
            jax.ShapeDtypeStruct(early.shape, jnp.bfloat16),
            jax.ShapeDtypeStruct(late.shape, jnp.bfloat16),
        ),
        in_specs=[smem, smem, vmem, vmem],
        out_specs=(vmem, vmem),
        scratch_shapes=[pltpu.VMEM((rows + 8, width), jnp.float32)] * (1 + ACCS),
        compiler_params=pltpu.CompilerParams(vmem_limit_bytes=40 * 1024 * 1024),
        cost_estimate=pl.CostEstimate(
            flops=16384 * width, bytes_accessed=4 * rows * width, transcendentals=0
        ),
        name="edge_sums",
    )(counts, packed, early, late)


def body(
    features,
    cotangent,
    edge_src,
    edge_dst,
    send_rows,
    recv_rows,
    in_degree,
    weight_self,
    weight_neigh,
):
    rows, width = features.shape
    half = width // 2
    early = rows - LATE
    dom_count = lax.axis_size("dom")
    chips = lax.axis_size("y")
    core = lax.axis_index("core")
    part_rows = rows * chips * 2
    contract_first = (((0,), (0,)), ((), ()))
    f32, bf16 = jnp.float32, jnp.bfloat16

    send_list = send_rows.reshape(-1)
    recv_list = recv_rows.reshape(-1)
    slot_count = send_list.shape[0]
    columns = lax.broadcasted_iota(jnp.int32, (slot_count, rows), 1)
    late_columns = lax.broadcasted_iota(jnp.int32, (slot_count, LATE), 1) + early
    pick_send = (send_list[:, None] == late_columns).astype(bf16)
    pick_recv = (recv_list[:, None] == columns).astype(bf16)
    is_mirror = lax.broadcasted_iota(jnp.int32, (rows, 1), 0) >= rows - MIRR
    late_mirror = is_mirror[early:]
    denominator = in_degree.reshape(-1).astype(f32)[:, None] + 1.0

    def over_dom(slots):
        return lax.all_to_all(slots, "dom", split_axis=0, concat_axis=0, tiled=True)

    def from_masters(values):
        slots = jnp.dot(pick_recv, values, preferred_element_type=f32).astype(bf16)
        return slots.reshape(dom_count, -1, values.shape[1])

    def at_mirrors(slots, values):
        arrived = lax.dot_general(
            pick_send, slots.reshape(slot_count, -1), contract_first, preferred_element_type=f32
        )
        return jnp.where(late_mirror, arrived.astype(bf16), values[early:])

    def mirrors_to_masters(late_values):
        slots = jnp.dot(pick_send, late_values, preferred_element_type=f32).astype(bf16)
        moved = over_dom(slots.reshape(dom_count, -1, width)).reshape(slot_count, width)
        return lax.dot_general(pick_recv, moved, contract_first, preferred_element_type=f32)

    def twin(values):
        return lax.ppermute(values, "core", [(0, 1), (1, 0)])

    def halves(values):
        mine = lax.dynamic_slice_in_dim(values, core * half, half, 1)
        other = lax.dynamic_slice_in_dim(values, (1 - core) * half, half, 1)
        return mine, other

    def chip_block(values):
        mine, other = halves(values)
        return jnp.concatenate([mine, twin(other)], axis=0)

    def gather(block):
        return lax.all_gather(block, "y", axis=0, tiled=True)

    def scatter(partial):
        return lax.psum_scatter(partial, "y", scatter_dimension=0, tiled=True)

    def whole_rows(block):
        count = block.shape[0] // 2
        mine = block[:count]
        other = twin(block[count:])
        return jnp.where(
            core == 0,
            jnp.concatenate([mine, other], axis=1),
            jnp.concatenate([other, mine], axis=1),
        )

    src, dst = edge_src.reshape(-1), edge_dst.reshape(-1)
    own_words = jnp.where(src >= 0, (dst << 16) | src, -1)
    words = jnp.stack([own_words, twin(own_words)])

    def table_row(row):
        member, within = (row // rows) ^ core, row % rows
        return jnp.where(
            within < early,
            member * early + within,
            (part_rows // rows) * early + member * LATE + within - early,
        )

    live = words >= 0
    counts = (jnp.sum(live.astype(jnp.int32), axis=1) + UNROLL - 1) // UNROLL
    packed = jnp.where(
        live,
        (table_row(words >> 16) << 16) | table_row(words & 0xFFFF),
        (part_rows << 16) | part_rows,
    )

    def edge_pass(take_high, early_table, late_table):
        return edge_sums(take_high, counts, packed, early_table, late_table)

    def partition_sums(early_part, late_part):
        late_block = scatter(late_part)
        late_block, early_part = lax.optimization_barrier((late_block, early_part))
        early_block = scatter(early_part)
        late_total = whole_rows(late_block)
        arrived = mirrors_to_masters(late_total)
        arrived, early_block = lax.optimization_barrier((arrived, early_block))
        totals = jnp.concatenate([whole_rows(early_block), late_total], axis=0).astype(f32)
        return totals + arrived

    early_block, sent = lax.optimization_barrier((chip_block(features[:early]), features))
    early_table = gather(early_block)
    late_rows = at_mirrors(over_dom(from_masters(sent)), features)
    early_table, late_rows = lax.optimization_barrier((early_table, late_rows))
    late_table = gather(chip_block(late_rows))
    early_part, late_part = edge_pass(False, early_table, late_table)
    totals = partition_sums(early_part, late_part)
    averaged = (totals / denominator).astype(bf16)

    pre = jnp.dot(features, weight_self, preferred_element_type=f32) + jnp.dot(
        averaged, weight_neigh, preferred_element_type=f32
    )
    gate_sig = jax.nn.sigmoid(pre)
    activated = (pre * gate_sig).astype(bf16)
    slope = gate_sig * (1.0 + pre * (1.0 - gate_sig))
    grad_pre = jnp.where(is_mirror, 0.0, cotangent.astype(f32) * slope).astype(bf16)
    grad_mean = (
        jnp.dot(grad_pre, weight_neigh.T, preferred_element_type=f32) / denominator
    ).astype(bf16)
    back_block, activated = lax.optimization_barrier((chip_block(grad_mean[:early]), activated))
    back_early = gather(back_block)
    local_self = lax.dot_general(features, grad_pre, contract_first, preferred_element_type=f32)
    local_neigh = lax.dot_general(averaged, grad_pre, contract_first, preferred_element_type=f32)
    self_term = jnp.dot(grad_pre, weight_self.T, preferred_element_type=f32)

    local_weights = jnp.concatenate([local_self, local_neigh], axis=1).astype(bf16)
    share = local_weights.reshape(dom_count, -1, 2 * width)
    slots = from_masters(jnp.concatenate([grad_mean, activated], axis=1))
    cap = slots.shape[1]
    moved = over_dom(jnp.concatenate([slots, share], axis=1))
    arrived = moved[:, :cap]
    late_rows = at_mirrors(arrived[:, :, :width], grad_mean)
    back_early, late_rows = lax.optimization_barrier((back_early, late_rows))
    back_late = gather(chip_block(late_rows))
    activated_late = at_mirrors(arrived[:, :, width:], activated)
    activated = jnp.concatenate([activated[:early], activated_late], axis=0)

    weight_sum = jnp.sum(moved[:, cap:].astype(f32), axis=0)
    back_late, weight_sum = lax.optimization_barrier((back_late, weight_sum))
    by_member = lax.all_gather(weight_sum, ("y", "core"), axis=0, tiled=False)

    early_part, late_part = edge_pass(True, back_early, back_late)
    weight_sum = jnp.sum(by_member, axis=0)
    weight_sums = over_dom(
        jnp.broadcast_to(weight_sum[None], (dom_count,) + weight_sum.shape)
    ).reshape(-1, 2 * width)
    back_sum = partition_sums(early_part, late_part)
    grad_features = jnp.where(is_mirror, 0.0, back_sum + self_term).astype(bf16)
    return activated, grad_features, weight_sums[:, :width], weight_sums[:, width:]


def solution(mesh):
    devices = mesh.devices
    split = Mesh(
        devices.reshape(devices.shape[0], devices.shape[1] // 2, 2), ("dom", "y", "core")
    )
    every = ("dom", "y", "core")
    member = ("y", "core")
    placed = (
        P(every, None),
        P(every, None),
        P("dom", member, None),
        P("dom", member, None),
        P("dom", member, None, None),
        P("dom", member, None, None),
        P("dom", member, None),
        P(),
        P(),
    )
    return jax.shard_map(
        body,
        mesh=split,
        in_specs=placed,
        out_specs=(P(every, None), P(every, None), P(), P()),
        check_vma=False,
    )
```

time: 743 us -> 399 us (0.54)
  waiting for transfers between devices: 496 us -> 120 us
  other arithmetic: 158 us -> 3.24 us
  blocking collectives: 11.8 us -> 97.3 us
  starting transfers between devices: 35.8 us -> 101 us
  Pallas kernels: 0 us -> 46.3 us
  matrix products: 13.3 us -> 4.26 us
    psum x1 -> x0, waiting for transfers between devices: 267 us -> none  [body(): weight_sums = lax.psum((local_self, local_neigh), ('dom', 'member'))]
    scatter-add x16 -> x0, other arithmetic: 138 us -> none  [block_step(): return accum.at[landing_rows].add(messages, mode='drop')]
    all_gather x0 -> x5, blocking collectives: none -> 97.3 us  [the longest x4 80.2 us: gather(): return lax.all_gather(block, 'y', axis=0, tiled=True)]
    all_gather x2 -> x0, waiting for transfers between devices: 79.8 us -> none  [gather_rows(): return lax.all_gather(values, 'member', axis=0, tiled=True)]
    ppermute x0 -> x9, starting transfers between devices: none -> 53.7 us  [twin(): return lax.ppermute(values, 'core', [(0, 1), (1, 0)])]
    pallas_call x0 -> x2, Pallas kernels: none -> 46.3 us  [edge_sums(): pl.pallas_call(functools.partial(edge_kernel, take_high), out_shape=(jax....]
    reduce_scatter x2 -> x4, waiting for transfers between devices: 116 us -> 96.2 us  [scatter(): return lax.psum_scatter(partial, 'y', scatter_dimension=0, tiled=True)]
    all_to_all x4 -> x5, waiting for transfers between devices: 33.1 us -> 19.2 us  [over_dom(): return lax.all_to_all(slots, 'dom', split_axis=0, concat_axis=0, tiled=True)]
  transfers between devices with their start and end apart: 9 -> 18, of which waited for: 9 -> 11; matrix products, arithmetic and copies ran while one was open for 1% -> 2% of each run, Pallas kernels for 0% -> 0%
where the time goes in v1:
time: 399 us; the launch traced here: 396 us
  waiting for transfers between devices  120 us (30%)
  starting transfers between devices  101 us (25%)
  blocking collectives  97.3 us (24%)
  Pallas kernels  46.3 us (12%)
  between operations  14.2 us (4%)
  local copies, waits for them, and re-layouts  10.1 us (3%)
  matrix products  4.26 us (1%)
    reduce_scatter x4, waiting for transfers between devices, scatter(): return lax.psum_scatter(partial, 'y', scatter_dimension=0, tiled=True)  96.2 us
    all_gather x4, blocking collectives, gather(): return lax.all_gather(block, 'y', axis=0, tiled=True)  80.2 us
    ppermute x9, starting transfers between devices, twin(): return lax.ppermute(values, 'core', [(0, 1), (1, 0)])  53.7 us
    all_to_all x5, starting transfers between devices, over_dom(): return lax.all_to_all(slots, 'dom', split_axis=0, concat_axis=0, tiled=True)  47.2 us
    pallas_call x2, Pallas kernels, edge_sums(): pl.pallas_call(functools.partial(edge_kernel, take_high), out_shape=(jax....  46.3 us
    all_to_all x5, waiting for transfers between devices, over_dom(): return lax.all_to_all(slots, 'dom', split_axis=0, concat_axis=0, tiled=True)  19.2 us
    all_gather x1, blocking collectives, body(): by_member = lax.all_gather(weight_sum, ('y', 'core'), axis=0, tiled=False)  17.2 us
  transfers between devices with their start and end apart: 18, of which 11 were waited for; matrix products, arithmetic and copies ran while one was open for 2% of the time, Pallas kernels for 0%

profile of v1, /device:TPU:1, one launch (start us, length us, event | category | flops | bytes accessed | tf_op | source)
XLA Modules:
  0.0 396.4 jit_solution(7806204563803487336)
XLA Ops:
  8.0 8.8 %collective-permute-start = (s32[4096]{0:T(1024)S(1)}, s32[4096]{0:T(1024)S(1)}, u32[]{:S(2)}, u32[]{:S(2)}) collective-permute-start(s32[4096]{0:T(1024)S(1)} %bitcast.40), channel_id=1, source_target_pairs={{0,1},{1,0},{2,3},{3,2},{4,5},{5,4},{6,7},{7,6},{8,9},{9,8},{10,11... | collective-permute-start | bytes 49160 | tf_op jit(solution)/shard_map/ppermute | solution.py:145
  22.4 7.5 %all-to-all-start = ((bf16[32,4,256]{2,1,0:T(4,128)(2,1)}), bf16[32,4,256]{2,1,0:T(4,128)(2,1)S(1)}, u32[]{:S(2)}, u32[]{:S(2)}) async-start(bf16[32,4,256]{2,1,0:T(4,128)(2,1)} %reshape.114), calls=%async_computation | async-start | bytes 131072 | tf_op jit(solution)/shard_map/all_to_all | solution.py:127
  30.0 22.2 %all_gather.18.early_ref = bf16[3072,128]{1,0:T(8,128)(2,1)S(1)} all-gather(bf16[384,128]{1,0:T(8,128)(2,1)S(1)} %pad_maximum_fusion.1), channel_id=1, replica_groups=mesh['dom'=32,'y'=8,'core'=2] {'y'}, dimensions={0}, use_global_device_ids=true | all-gather | bytes 884736 | tf_op jit(solution)/shard_map/all_gather | solution.py:157
  52.5 8.3 %collective-permute-start.2 = (bf16[64,128]{1,0:T(8,128)(2,1)S(1)}, bf16[64,128]{1,0:T(8,128)(2,1)S(1)}, u32[]{:S(2)}, u32[]{:S(2)}) collective-permute-start(bf16[64,128]{1,0:T(8,128)(2,1)S(1)} %get-tuple-element.69), channel_id=1, source_target_pairs={{0,1},{1,0},{2,3},{3,2},{4,5},{5,4},{6,7},{7,6},{8,9},{9,8},{10,11... | collective-permute-start | bytes 49160 | tf_op jit(solution)/shard_map/ppermute | solution.py:145
  61.6 18.4 %all_gather.19.late_ref = bf16[1024,128]{1,0:T(8,128)(2,1)S(1)} all-gather(bf16[128,128]{1,0:T(8,128)(2,1)S(1)} %pad_maximum_fusion.3), channel_id=1, replica_groups=mesh['dom'=32,'y'=8,'core'=2] {'y'}, dimensions={0}, use_global_device_ids=true | all-gather | bytes 294912 | tf_op jit(solution)/shard_map/all_gather | solution.py:157
  80.0 23.1 %edge_sums.2 = (bf16[3072,128]{1,0:T(8,128)(2,1)}, bf16[1024,128]{1,0:T(8,128)(2,1)}) custom-call(s32[2]{0:T(128)S(1)} %and_select_fusion.4.counts_ref, s32[2,4096]{1,0:T(2,128)S(1)} %get-tuple-element.70.packed_ref, bf16[3072,128]{1,0:T(8,128)(2,1)S(1)} %all_gather.18.early_ref, bf16[1024,128]{1,0:T(8,128)(2,1)S(1)} %all_gather.19.late_ref), custom_call_target="tpu_custom_call" | custom-call | flops 2097152 | bytes 2097152 | tf_op jit(solution)/shard_map/edge_sums/pallas_call | solution.py:77
  103.2 41.2 %reduce-scatter.5.cloned.1.call-done = bf16[128,128]{1,0:T(8,128)(2,1)} async-done(((bf16[1024,128]{1,0:T(8,128)(2,1)}), bf16[128,128]{1,0:T(8,128)(2,1)}) %reduce-scatter.5.cloned.1.call-update) | async-done | bytes 32784 | tf_op jit(solution)/shard_map/reduce_scatter | solution.py:160
  145.2 8.0 %collective-permute-start.3 = (bf16[64,128]{1,0:T(8,128)(2,1)S(1)}, bf16[64,128]{1,0:T(8,128)(2,1)S(1)}, u32[]{:S(2)}, u32[]{:S(2)}) collective-permute-start(bf16[64,128]{1,0:T(8,128)(2,1)S(1)} %get-tuple-element.67), channel_id=1, source_target_pairs={{0,1},{1,0},{2,3},{3,2},{4,5},{5,4},{6,7},{7,6},{8,9},{9,8},{10,11... | collective-permute-start | bytes 49160 | tf_op jit(solution)/shard_map/ppermute | solution.py:145
  154.9 10.0 %all-to-all-start.1 = ((bf16[32,4,256]{2,1,0:T(4,128)(2,1)}), bf16[32,4,256]{2,1,0:T(4,128)(2,1)S(1)}, u32[]{:S(2)}, u32[]{:S(2)}) async-start(bf16[32,4,256]{2,1,0:T(4,128)(2,1)} %reshape.116), calls=%async_computation.2 | async-start | bytes 131072 | tf_op jit(solution)/shard_map/all_to_all | solution.py:127
  165.0 8.9 %all-to-all-done.1 = bf16[32,4,256]{2,1,0:T(4,128)(2,1)S(1)} async-done(((bf16[32,4,256]{2,1,0:T(4,128)(2,1)}), bf16[32,4,256]{2,1,0:T(4,128)(2,1)S(1)}, u32[]{:S(2)}, u32[]{:S(2)}) %all-to-all-start.1) | async-done | bytes 65568 | tf_op jit(solution)/shard_map/all_to_all | solution.py:127
  174.2 14.0 %reduce-scatter.7.cloned.1.call-done = bf16[384,128]{1,0:T(8,128)(2,1)} async-done(((bf16[3072,128]{1,0:T(8,128)(2,1)}), bf16[384,128]{1,0:T(8,128)(2,1)}) %reduce-scatter.7.cloned.1.call-update) | async-done | bytes 98320 | tf_op jit(solution)/shard_map/reduce_scatter | solution.py:160
  189.1 6.5 %collective-permute-start.4 = (bf16[192,128]{1,0:T(8,128)(2,1)S(1)}, bf16[192,128]{1,0:T(8,128)(2,1)S(1)}, u32[]{:S(2)}, u32[]{:S(2)}) collective-permute-start(bf16[192,128]{1,0:T(8,128)(2,1)S(1)} %get-tuple-element.59), channel_id=1, source_target_pairs={{0,1},{1,0},{2,3},{3,2},{4,5},{5,4},{6,7},{7,6},{8,9},{9,8},{10,11... | collective-permute-start | bytes 147464 | tf_op jit(solution)/shard_map/ppermute | solution.py:145
  202.6 9.9 %all-to-all-start.2 = ((bf16[32,12,512]{2,1,0:T(8,128)(2,1)}), bf16[32,12,512]{2,1,0:T(8,128)(2,1)S(1)}, u32[]{:S(2)}, u32[]{:S(2)}) async-start(bf16[32,12,512]{2,1,0:T(8,128)(2,1)} %maximum_maximum_fusion), calls=%async_computation.4 | async-start | bytes 1048576 | tf_op jit(solution)/shard_map/all_to_all | solution.py:127
  212.6 20.8 %all_gather.20.early_ref = bf16[3072,128]{1,0:T(8,128)(2,1)S(1)} all-gather(bf16[384,128]{1,0:T(8,128)(2,1)S(1)} %pad_maximum_fusion.2), channel_id=1, replica_groups=mesh['dom'=32,'y'=8,'core'=2] {'y'}, dimensions={0}, use_global_device_ids=true | all-gather | bytes 884736 | tf_op jit(solution)/shard_map/all_gather | solution.py:157
  233.7 7.9 %collective-permute-start.6 = (bf16[64,128]{1,0:T(8,128)(2,1)S(1)}, bf16[64,128]{1,0:T(8,128)(2,1)S(1)}, u32[]{:S(2)}, u32[]{:S(2)}) collective-permute-start(bf16[64,128]{1,0:T(8,128)(2,1)S(1)} %get-tuple-element.65), channel_id=1, source_target_pairs={{0,1},{1,0},{2,3},{3,2},{4,5},{5,4},{6,7},{7,6},{8,9},{9,8},{10,11... | collective-permute-start | bytes 49160 | tf_op jit(solution)/shard_map/ppermute | solution.py:145
  242.4 18.8 %all_gather.21.late_ref = bf16[1024,128]{1,0:T(8,128)(2,1)S(1)} all-gather(bf16[128,128]{1,0:T(8,128)(2,1)S(1)} %pad_maximum_fusion.4), channel_id=1, replica_groups=mesh['dom'=32,'y'=8,'core'=2] {'y'}, dimensions={0}, use_global_device_ids=true | all-gather | bytes 294912 | tf_op jit(solution)/shard_map/all_gather | solution.py:157
  261.2 23.1 %edge_sums.3 = (bf16[3072,128]{1,0:T(8,128)(2,1)}, bf16[1024,128]{1,0:T(8,128)(2,1)}) custom-call(s32[2]{0:T(128)S(1)} %and_select_fusion.4.counts_ref, s32[2,4096]{1,0:T(2,128)S(1)} %get-tuple-element.70.packed_ref, bf16[3072,128]{1,0:T(8,128)(2,1)S(1)} %all_gather.20.early_ref, bf16[1024,128]{1,0:T(8,128)(2,1)S(1)} %all_gather.21.late_ref), custom_call_target="tpu_custom_call" | custom-call | flops 2097152 | bytes 2097152 | tf_op jit(solution)/shard_map/edge_sums/pallas_call | solution.py:77
  284.4 40.9 %reduce-scatter.9.cloned.1.call-done = bf16[128,128]{1,0:T(8,128)(2,1)} async-done(((bf16[1024,128]{1,0:T(8,128)(2,1)}), bf16[128,128]{1,0:T(8,128)(2,1)}) %reduce-scatter.9.cloned.1.call-update) | async-done | bytes 32784 | tf_op jit(solution)/shard_map/reduce_scatter | solution.py:160
  326.1 7.7 %collective-permute-start.7 = (bf16[64,128]{1,0:T(8,128)(2,1)S(1)}, bf16[64,128]{1,0:T(8,128)(2,1)S(1)}, u32[]{:S(2)}, u32[]{:S(2)}) collective-permute-start(bf16[64,128]{1,0:T(8,128)(2,1)S(1)} %get-tuple-element.63), channel_id=1, source_target_pairs={{0,1},{1,0},{2,3},{3,2},{4,5},{5,4},{6,7},{7,6},{8,9},{9,8},{10,11... | collective-permute-start | bytes 49160 | tf_op jit(solution)/shard_map/ppermute | solution.py:145
  335.5 9.9 %all-to-all-start.3 = ((bf16[32,4,256]{2,1,0:T(4,128)(2,1)}), bf16[32,4,256]{2,1,0:T(4,128)(2,1)S(1)}, u32[]{:S(2)}, u32[]{:S(2)}) async-start(bf16[32,4,256]{2,1,0:T(4,128)(2,1)} %reshape.121), calls=%async_computation.6 | async-start | bytes 131072 | tf_op jit(solution)/shard_map/all_to_all | solution.py:127
  345.4 17.2 %all-gather = f32[128,512]{1,0:T(8,128)S(1)} all-gather(f32[8,512]{1,0:T(8,128)S(1)} %convert_reduce_fusion), channel_id=2, replica_groups=mesh['dom'=32,'y'=8,'core'=2] {'y','core'}, dimensions={0}, use_global_device_ids=true | all-gather | bytes 278528 | tf_op jit(solution)/shard_map/all_gather | solution.py:244
  363.5 9.9 %all-to-all-start.4 = ((f32[32,8,512]{2,1,0:T(8,128)}), f32[32,8,512]{2,1,0:T(8,128)S(1)}, u32[]{:S(2)}, u32[]{:S(2)}) async-start(f32[32,8,512]{2,1,0:T(8,128)} %broadcast_in_dim.63), calls=%async_computation.8 | async-start | bytes 1048576 | tf_op jit(solution)/shard_map/all_to_all | solution.py:127
  375.5 2.3 collective-permute-start.8
  377.9 10.3 %all-to-all-done.4 = f32[32,8,512]{2,1,0:T(8,128)S(1)} async-done(((f32[32,8,512]{2,1,0:T(8,128)}), f32[32,8,512]{2,1,0:T(8,128)S(1)}, u32[]{:S(2)}, u32[]{:S(2)}) %all-to-all-start.4) | async-done | bytes 524320 | tf_op jit(solution)/shard_map/all_to_all | solution.py:127
  (104 shorter events, 26.5 us)
Async XLA Ops:
  7.2 189.5 %copy-start = (bf16[256,256]{1,0:T(8,128)(2,1)S(1)}, bf16[256,256]{1,0:T(8,128)(2,1)}, u32[]{:S(2)}) copy-start(bf16[256,256]{1,0:T(8,128)(2,1)} %param.17) | copy-start | bytes 393220
  8.0 12.7 %collective-permute-start = (s32[4096]{0:T(1024)S(1)}, s32[4096]{0:T(1024)S(1)}, u32[]{:S(2)}, u32[]{:S(2)}) collective-permute-start(s32[4096]{0:T(1024)S(1)} %bitcast.40), channel_id=1, source_target_pairs={{0,1},{1,0},{2,3},{3,2},{4,5},{5,4},{6,7},{7,6},{8,9},{9,8},{10,11... | collective-permute-start | bytes 49160 | tf_op jit(solution)/shard_map/ppermute | solution.py:145
  17.7 2.0 copy-start.5
  17.7 3.4 collective-permute-start.1
  20.6 0.9 copy-start.1
  22.4 29.7 %all-to-all-start = ((bf16[32,4,256]{2,1,0:T(4,128)(2,1)}), bf16[32,4,256]{2,1,0:T(4,128)(2,1)S(1)}, u32[]{:S(2)}, u32[]{:S(2)}) async-start(bf16[32,4,256]{2,1,0:T(4,128)(2,1)} %reshape.114), calls=%async_computation | async-start | bytes 131072 | tf_op jit(solution)/shard_map/all_to_all | solution.py:127
  29.9 114.5 %reduce-scatter.5.cloned.1.call-start = ((), (), s32[]{:S(2)}) async-start(), calls=%async_computation.9 | async-start | bytes 294912 | tf_op jit(solution)/shard_map/reduce_scatter | solution.py:160
  52.5 9.1 %collective-permute-start.2 = (bf16[64,128]{1,0:T(8,128)(2,1)S(1)}, bf16[64,128]{1,0:T(8,128)(2,1)S(1)}, u32[]{:S(2)}, u32[]{:S(2)}) collective-permute-start(bf16[64,128]{1,0:T(8,128)(2,1)S(1)} %get-tuple-element.69), channel_id=1, source_target_pairs={{0,1},{1,0},{2,3},{3,2},{4,5},{5,4},{6,7},{7,6},{8,9},{9,8},{10,11... | collective-permute-start | bytes 49160 | tf_op jit(solution)/shard_map/ppermute | solution.py:145
  103.2 85.1 %reduce-scatter.7.cloned.1.call-start = ((), (), s32[]{:S(2)}) async-start(), calls=%async_computation.10 | async-start | bytes 884736 | tf_op jit(solution)/shard_map/reduce_scatter | solution.py:160
  144.4 8.8 %copy-start.2 = (bf16[256,256]{1,0:T(8,128)(2,1)S(1)}, bf16[256,256]{1,0:T(8,128)(2,1)}, u32[]{:S(2)}) copy-start(bf16[256,256]{1,0:T(8,128)(2,1)} %param.16) | copy-start | bytes 393220
  145.2 8.8 %collective-permute-start.3 = (bf16[64,128]{1,0:T(8,128)(2,1)S(1)}, bf16[64,128]{1,0:T(8,128)(2,1)S(1)}, u32[]{:S(2)}, u32[]{:S(2)}) collective-permute-start(bf16[64,128]{1,0:T(8,128)(2,1)S(1)} %get-tuple-element.67), channel_id=1, source_target_pairs={{0,1},{1,0},{2,3},{3,2},{4,5},{5,4},{6,7},{7,6},{8,9},{9,8},{10,11... | collective-permute-start | bytes 49160 | tf_op jit(solution)/shard_map/ppermute | solution.py:145
  154.9 10.0 %copy-start.7 = (s32[1,1,256]{2,1,0:T(1,128)S(1)}, s32[1,1,256]{2,1,0:T(1,128)}, u32[]{:S(2)}) copy-start(s32[1,1,256]{2,1,0:T(1,128)} %param.15) | copy-start | bytes 3076
  154.9 19.0 %all-to-all-start.1 = ((bf16[32,4,256]{2,1,0:T(4,128)(2,1)}), bf16[32,4,256]{2,1,0:T(4,128)(2,1)S(1)}, u32[]{:S(2)}, u32[]{:S(2)}) async-start(bf16[32,4,256]{2,1,0:T(4,128)(2,1)} %reshape.116), calls=%async_computation.2 | async-start | bytes 131072 | tf_op jit(solution)/shard_map/all_to_all | solution.py:127
  189.1 7.4 %collective-permute-start.4 = (bf16[192,128]{1,0:T(8,128)(2,1)S(1)}, bf16[192,128]{1,0:T(8,128)(2,1)S(1)}, u32[]{:S(2)}, u32[]{:S(2)}) collective-permute-start(bf16[192,128]{1,0:T(8,128)(2,1)S(1)} %get-tuple-element.59), channel_id=1, source_target_pairs={{0,1},{1,0},{2,3},{3,2},{4,5},{5,4},{6,7},{7,6},{8,9},{9,8},{10,11... | collective-permute-start | bytes 147464 | tf_op jit(solution)/shard_map/ppermute | solution.py:145
  196.5 0.9 copy-start.8
  198.2 3.1 collective-permute-start.5
  202.6 30.7 %all-to-all-start.2 = ((bf16[32,12,512]{2,1,0:T(8,128)(2,1)}), bf16[32,12,512]{2,1,0:T(8,128)(2,1)S(1)}, u32[]{:S(2)}, u32[]{:S(2)}) async-start(bf16[32,12,512]{2,1,0:T(8,128)(2,1)} %maximum_maximum_fusion), calls=%async_computation.4 | async-start | bytes 1048576 | tf_op jit(solution)/shard_map/all_to_all | solution.py:127
  212.5 112.8 %reduce-scatter.9.cloned.1.call-start = ((), (), s32[]{:S(2)}) async-start(), calls=%async_computation.11 | async-start | bytes 294912 | tf_op jit(solution)/shard_map/reduce_scatter | solution.py:160
  233.7 8.7 %collective-permute-start.6 = (bf16[64,128]{1,0:T(8,128)(2,1)S(1)}, bf16[64,128]{1,0:T(8,128)(2,1)S(1)}, u32[]{:S(2)}, u32[]{:S(2)}) collective-permute-start(bf16[64,128]{1,0:T(8,128)(2,1)S(1)} %get-tuple-element.65), channel_id=1, source_target_pairs={{0,1},{1,0},{2,3},{3,2},{4,5},{5,4},{6,7},{7,6},{8,9},{9,8},{10,11... | collective-permute-start | bytes 49160 | tf_op jit(solution)/shard_map/ppermute | solution.py:145
  284.4 90.3 %reduce-scatter.11.cloned.1.call-start = ((), (), s32[]{:S(2)}) async-start(), calls=%async_computation.12 | async-start | bytes 884736 | tf_op jit(solution)/shard_map/reduce_scatter | solution.py:160
  326.1 8.5 %collective-permute-start.7 = (bf16[64,128]{1,0:T(8,128)(2,1)S(1)}, bf16[64,128]{1,0:T(8,128)(2,1)S(1)}, u32[]{:S(2)}, u32[]{:S(2)}) collective-permute-start(bf16[64,128]{1,0:T(8,128)(2,1)S(1)} %get-tuple-element.63), channel_id=1, source_target_pairs={{0,1},{1,0},{2,3},{3,2},{4,5},{5,4},{6,7},{7,6},{8,9},{9,8},{10,11... | collective-permute-start | bytes 49160 | tf_op jit(solution)/shard_map/ppermute | solution.py:145
  335.5 27.1 %all-to-all-start.3 = ((bf16[32,4,256]{2,1,0:T(4,128)(2,1)}), bf16[32,4,256]{2,1,0:T(4,128)(2,1)S(1)}, u32[]{:S(2)}, u32[]{:S(2)}) async-start(bf16[32,4,256]{2,1,0:T(4,128)(2,1)} %reshape.121), calls=%async_computation.6 | async-start | bytes 131072 | tf_op jit(solution)/shard_map/all_to_all | solution.py:127
  363.5 24.7 %all-to-all-start.4 = ((f32[32,8,512]{2,1,0:T(8,128)}), f32[32,8,512]{2,1,0:T(8,128)S(1)}, u32[]{:S(2)}, u32[]{:S(2)}) async-start(f32[32,8,512]{2,1,0:T(8,128)} %broadcast_in_dim.63), calls=%async_computation.8 | async-start | bytes 1048576 | tf_op jit(solution)/shard_map/all_to_all | solution.py:127
  375.5 13.5 %collective-permute-start.8 = (bf16[192,128]{1,0:T(8,128)(2,1)S(1)}, bf16[192,128]{1,0:T(8,128)(2,1)S(1)}, u32[]{:S(2)}, u32[]{:S(2)}) collective-permute-start(bf16[192,128]{1,0:T(8,128)(2,1)S(1)} %get-tuple-element.55), channel_id=1, source_target_pairs={{0,1},{1,0},{2,3},{3,2},{4,5},{5,4},{6,7},{7,6},{8,9},{9,8},{10,11... | collective-permute-start | bytes 147464 | tf_op jit(solution)/shard_map/ppermute | solution.py:145
  (4 other events, 3.1 us)
Sparse Core Ops, SparseCore 0:
  103.3 41.1 reduce-scatter.4
  147.5 40.7 reduce-scatter.6
  284.5 40.7 reduce-scatter.8
  328.2 40.7 reduce-scatter.10

commit v2 on v1

v2 whole, which is shorter than its diff:
```python
import functools

import jax
import jax.numpy as jnp
from jax import lax
from jax.experimental import pallas as pl
from jax.experimental.pallas import tpu as pltpu
from jax.sharding import PartitionSpec as P

MIRR = 62
LATE = 64
UNROLL = 16
ACCS = 4
CHUNK = 128


def edge_kernel(
    take_high, counts_ref, packed_ref, early_ref, late_ref, early_out, late_out, table, *accs
):
    early_rows, late_rows = early_ref.shape[0], late_ref.shape[0]
    rows = early_rows + late_rows
    pad = table.shape[0] - rows

    def load(ref, base):
        def step(i, _):
            at = pl.multiple_of(i * CHUNK, CHUNK)
            table[pl.ds(base + at, CHUNK), :] = ref[pl.ds(at, CHUNK), :].astype(jnp.float32)
            for acc in accs:
                acc[pl.ds(base + at, CHUNK), :] = jnp.zeros((CHUNK, ref.shape[1]), jnp.float32)
            return 0

        lax.fori_loop(0, ref.shape[0] // CHUNK, step, 0)

    load(early_ref, 0)
    load(late_ref, early_rows)
    table[pl.ds(rows, pad), :] = jnp.zeros((pad, table.shape[1]), jnp.float32)

    one_row = (rows + pad, 1, table.shape[1])
    table_rows = table.reshape(one_row)
    acc_rows = [acc.reshape(one_row) for acc in accs]
    for which in range(2):

        def step(i, _):
            for group in range(UNROLL // ACCS):
                takes, places = [], []
                for k in range(ACCS):
                    word = packed_ref[which, i * UNROLL + group * ACCS + k]
                    low, high = word & 0xFFFF, word >> 16
                    takes.append(high if take_high else low)
                    places.append(low if take_high else high)
                sums = [acc_rows[k][places[k]] + table_rows[takes[k]] for k in range(ACCS)]
                for k in range(ACCS):
                    acc_rows[k][places[k]] = sums[k]
            return 0

        lax.fori_loop(0, counts_ref[which], step, 0)

    def store(ref, base):
        def step(i, _):
            at = pl.multiple_of(i * CHUNK, CHUNK)
            total = accs[0][pl.ds(base + at, CHUNK), :]
            for acc in accs[1:]:
                total = total + acc[pl.ds(base + at, CHUNK), :]
            ref[pl.ds(at, CHUNK), :] = total.astype(ref.dtype)
            return 0

        lax.fori_loop(0, ref.shape[0] // CHUNK, step, 0)

    store(early_out, 0)
    store(late_out, early_rows)


def edge_sums(take_high, counts, packed, early, late):
    rows, width = early.shape[0] + late.shape[0], early.shape[1]
    smem = pl.BlockSpec(memory_space=pltpu.SMEM)
    vmem = pl.BlockSpec(memory_space=pltpu.VMEM)
    return pl.pallas_call(
        functools.partial(edge_kernel, take_high),
        out_shape=(
            jax.ShapeDtypeStruct(early.shape, jnp.bfloat16),
            jax.ShapeDtypeStruct(late.shape, jnp.bfloat16),
        ),
        in_specs=[smem, smem, vmem, vmem],
        out_specs=(vmem, vmem),
        scratch_shapes=[pltpu.VMEM((rows + 8, width), jnp.float32)] * (1 + ACCS),
        compiler_params=pltpu.CompilerParams(vmem_limit_bytes=40 * 1024 * 1024),
        cost_estimate=pl.CostEstimate(
            flops=16384 * width, bytes_accessed=4 * rows * width, transcendentals=0
        ),
        name="edge_sums",
    )(counts, packed, early, late)


def body(
    features,
    cotangent,
    edge_src,
    edge_dst,
    send_rows,
    recv_rows,
    in_degree,
    weight_self,
    weight_neigh,
):
    rows, width = features.shape
    half = width // 2
    early = rows - LATE
    dom_count = lax.axis_size("dom")
    members = lax.axis_size("member")
    part_rows = rows * members
    contract_first = (((0,), (0,)), ((), ()))
    f32, bf16 = jnp.float32, jnp.bfloat16

    send_list = send_rows.reshape(-1)
    recv_list = recv_rows.reshape(-1)
    slot_count = send_list.shape[0]
    cap = slot_count // dom_count
    columns = lax.broadcasted_iota(jnp.int32, (slot_count, rows), 1)
    late_columns = lax.broadcasted_iota(jnp.int32, (slot_count, LATE), 1) + early
    pick_send = (send_list[:, None] == late_columns).astype(bf16)
    pick_recv = (recv_list[:, None] == columns).astype(bf16)
    is_mirror = lax.broadcasted_iota(jnp.int32, (rows, 1), 0) >= rows - MIRR
    late_mirror = is_mirror[early:]
    denominator = in_degree.reshape(-1).astype(f32)[:, None] + 1.0

    def over_dom(slots):
        return lax.all_to_all(slots, "dom", split_axis=0, concat_axis=0, tiled=True)

    def from_masters(values):
        slots = jnp.dot(pick_recv, values, preferred_element_type=f32).astype(bf16)
        return slots.reshape(dom_count, -1, values.shape[1])

    def at_mirrors(slots, values):
        arrived = lax.dot_general(
            pick_send, slots.reshape(slot_count, -1), contract_first, preferred_element_type=f32
        )
        return jnp.where(late_mirror, arrived.astype(bf16), values[early:])

    def over_member(blocks):
        return lax.all_to_all(blocks, "member", split_axis=0, concat_axis=0, tiled=True)

    def copies(values):
        halves = jnp.stack([values[:, :half], values[:, half:]])
        every = jnp.broadcast_to(halves[None], (members // 2,) + halves.shape)
        return every.reshape(members, -1, half)

    def gather(values):
        return over_member(copies(values)).reshape(-1, half)

    def member_sum(arrived):
        by_core = arrived.reshape((members // 2, 2) + arrived.shape[1:]).astype(f32)
        return jnp.concatenate([jnp.sum(by_core[:, core], axis=0) for core in (0, 1)], axis=1)

    src, dst = edge_src.reshape(-1), edge_dst.reshape(-1)

    def table_row(row):
        member, within = row // rows, row % rows
        return jnp.where(
            within < early, member * early + within, members * early + member * LATE + within - early
        )

    own_words = jnp.where(
        src >= 0, (table_row(dst) << 16) | table_row(src), (part_rows << 16) | part_rows
    )
    pairs = [(m, m ^ 1) for m in range(members)]
    packed = jnp.stack([own_words, lax.ppermute(own_words, "member", pairs)])
    live = packed < (part_rows << 16)
    counts = (jnp.sum(live.astype(jnp.int32), axis=1) + UNROLL - 1) // UNROLL

    def edge_pass(take_high, early_table, late_table):
        return edge_sums(take_high, counts, packed, early_table, late_table)

    def partition_sums(early_part, late_part, weight_sum=None):
        late_part = late_part.reshape(members, LATE, half)
        if weight_sum is not None:
            share = weight_sum.astype(bf16).reshape(-1, half)
            share = jnp.broadcast_to(share[None], (members,) + share.shape)
            late_part = jnp.concatenate([late_part, share], axis=1)
        late_arrived = over_member(late_part)
        late_arrived, early_part = lax.optimization_barrier((late_arrived, early_part))
        early_arrived = over_member(early_part.reshape(members, early, half))
        late_total = member_sum(late_arrived[:, :LATE])
        slots = jnp.dot(pick_send, late_total.astype(bf16), preferred_element_type=f32)
        slots = slots.astype(bf16).reshape(dom_count, -1, width)
        weight_sums = None
        if weight_sum is not None:
            share = jnp.sum(late_arrived[:, LATE:].astype(f32), axis=0).astype(bf16)
            share = share.reshape(-1, width)
            share = jnp.broadcast_to(share[None], (dom_count,) + share.shape)
            slots = jnp.concatenate([slots, share], axis=1)
        moved = over_dom(slots)
        if weight_sum is not None:
            weight_sums = moved[:, cap:].reshape(-1, 2 * width).astype(f32)
        arrived = lax.dot_general(
            pick_recv,
            moved[:, :cap].reshape(slot_count, width),
            contract_first,
            preferred_element_type=f32,
        )
        arrived, early_arrived = lax.optimization_barrier((arrived, early_arrived))
        totals = jnp.concatenate([member_sum(early_arrived), late_total], axis=0)
        return totals + arrived, weight_sums

    early_copies, sent = lax.optimization_barrier((copies(features[:early]), features))
    early_table = over_member(early_copies).reshape(-1, half)
    late_rows = at_mirrors(over_dom(from_masters(sent)), features)
    early_table, late_rows = lax.optimization_barrier((early_table, late_rows))
    late_table = gather(late_rows)
    early_part, late_part = edge_pass(False, early_table, late_table)
    totals, _ = partition_sums(early_part, late_part)
    averaged = (totals / denominator).astype(bf16)

    pre = jnp.dot(features, weight_self, preferred_element_type=f32) + jnp.dot(
        averaged, weight_neigh, preferred_element_type=f32
    )
    gate_sig = jax.nn.sigmoid(pre)
    activated = (pre * gate_sig).astype(bf16)
    slope = gate_sig * (1.0 + pre * (1.0 - gate_sig))
    grad_pre = jnp.where(is_mirror, 0.0, cotangent.astype(f32) * slope).astype(bf16)
    grad_mean = (
        jnp.dot(grad_pre, weight_neigh.T, preferred_element_type=f32) / denominator
    ).astype(bf16)
    early_copies, activated = lax.optimization_barrier((copies(grad_mean[:early]), activated))
    back_early = over_member(early_copies).reshape(-1, half)
    local_self = lax.dot_general(features, grad_pre, contract_first, preferred_element_type=f32)
    local_neigh = lax.dot_general(averaged, grad_pre, contract_first, preferred_element_type=f32)
    self_term = jnp.dot(grad_pre, weight_self.T, preferred_element_type=f32)

    local_weights = jnp.concatenate([local_self, local_neigh], axis=1).astype(bf16)
    share = local_weights.reshape(dom_count, -1, 2 * width)
    slots = from_masters(jnp.concatenate([grad_mean, activated], axis=1))
    moved = over_dom(jnp.concatenate([slots, share], axis=1))
    arrived = moved[:, :cap]
    late_rows = at_mirrors(arrived[:, :, :width], grad_mean)
    back_early, late_rows = lax.optimization_barrier((back_early, late_rows))
    back_late = gather(late_rows)
    activated_late = at_mirrors(arrived[:, :, width:], activated)
    activated = jnp.concatenate([activated[:early], activated_late], axis=0)

    weight_sum = jnp.sum(moved[:, cap:].astype(f32), axis=0)
    early_part, late_part = edge_pass(True, back_early, back_late)
    back_sum, weight_sums = partition_sums(early_part, late_part, weight_sum)
    grad_features = jnp.where(is_mirror, 0.0, back_sum + self_term).astype(bf16)
    return activated, grad_features, weight_sums[:, :width], weight_sums[:, width:]


def solution(mesh):
    placed = (
        P(("dom", "member"), None),
        P(("dom", "member"), None),
        P("dom", "member", None),
        P("dom", "member", None),
        P("dom", "member", None, None),
        P("dom", "member", None, None),
        P("dom", "member", None),
        P(),
        P(),
    )
    return jax.shard_map(
        body,
        mesh=mesh,
        in_specs=placed,
        out_specs=(P(("dom", "member"), None), P(("dom", "member"), None), P(), P()),
        check_vma=False,
    )
```

time: 399 us -> 316 us (0.79)
  starting transfers between devices: 101 us -> 31.6 us
  between operations: 14.2 us -> 1.1 us
  waiting for transfers between devices: 120 us -> 107 us
  blocking collectives: 97.3 us -> 106 us
  Pallas kernels: 46.3 us -> 54.1 us
    all_to_all x0 -> x6, blocking collectives: none -> 106 us  [the longest x4 76 us: over_dom(): return lax.all_to_all(slots, 'dom', split_axis=0, concat_axis=0, tiled=True)]
    all_gather x5 -> x0, blocking collectives: 97.3 us -> none  [the longest x4 80.2 us: gather(): return lax.all_gather(block, 'y', axis=0, tiled=True)]
    reduce_scatter x4 -> x0, waiting for transfers between devices: 96.2 us -> none  [scatter(): return lax.psum_scatter(partial, 'y', scatter_dimension=0, tiled=True)]
    all_to_all x5 -> x6, waiting for transfers between devices: 19.2 us -> 107 us  [over_member(): lax.all_to_all(blocks, 'member', split_axis=0, concat_axis=0, tiled=True)]
    ppermute x9 -> x1, starting transfers between devices: 53.7 us -> 2.01 us  [body(): packed = jnp.stack([own_words, lax.ppermute(own_words, 'member', pairs)])]
    all_to_all x5 -> x6, starting transfers between devices: 47.2 us -> 29.6 us  [over_member(): lax.all_to_all(blocks, 'member', split_axis=0, concat_axis=0, tiled=True)]
    pallas_call x2, Pallas kernels: 46.3 us -> 54.1 us  [edge_sums(): pl.pallas_call(functools.partial(edge_kernel, take_high), out_shape=(jax....]
    ppermute x9 -> x1, waiting for transfers between devices: 4.43 us -> 0.01 us  [body(): packed = jnp.stack([own_words, lax.ppermute(own_words, 'member', pairs)])]
  transfers between devices with their start and end apart: 18 -> 7, of which waited for: 11 -> 6; matrix products, arithmetic and copies ran while one was open for 2% -> 2% of each run, Pallas kernels for 0% -> 0%
where the time goes in v2:
time: 316 us
  waiting for transfers between devices  107 us (34%)
  blocking collectives  106 us (34%)
  Pallas kernels  54.1 us (17%)
  starting transfers between devices  31.6 us (10%)
  local copies, waits for them, and re-layouts  7.6 us (2%)
  matrix products  5.17 us (2%)
    all_to_all x6, waiting for transfers between devices, over_member(): lax.all_to_all(blocks, 'member', split_axis=0, concat_axis=0, tiled=True)  107 us
    all_to_all x4, blocking collectives, over_dom(): return lax.all_to_all(slots, 'dom', split_axis=0, concat_axis=0, tiled=True)  76 us
    pallas_call x2, Pallas kernels, edge_sums(): pl.pallas_call(functools.partial(edge_kernel, take_high), out_shape=(jax....  54.1 us
    all_to_all x2, blocking collectives, over_member(): lax.all_to_all(blocks, 'member', split_axis=0, concat_axis=0, tiled=True)  30.3 us
    all_to_all x6, starting transfers between devices, over_member(): lax.all_to_all(blocks, 'member', split_axis=0, concat_axis=0, tiled=True)  29.6 us
  transfers between devices with their start and end apart: 7, of which 6 were waited for; matrix products, arithmetic and copies ran while one was open for 2% of the time, Pallas kernels for 0%

profile of v2, /device:TPU:1, one launch (start us, length us, event | category | flops | bytes accessed | tf_op | source)
XLA Modules:
  0.0 315.5 jit_solution(10751858342100580775)
XLA Ops:
  1.6 1.0 broadcast_in_dim.91
  3.5 1.1 convolution_convert_fusion.5
  4.6 22.4 %all_to_all.60 = bf16[32,4,256]{2,1,0:T(4,128)(2,1)S(1)} all-to-all(bf16[32,4,256]{2,1,0:T(4,128)(2,1)S(1)} %reshape.391), channel_id=1, replica_groups=mesh['dom'=32,'member'=16] {'dom'}, dimensions={0} | all-to-all | bytes 131072 | tf_op jit(solution)/shard_map/all_to_all | solution.py:127
  27.0 9.2 %all-to-all-start = ((bf16[16,192,128]{2,1,0:T(8,128)(2,1)}), bf16[16,192,128]{2,1,0:T(8,128)(2,1)S(1)}, u32[]{:S(2)}, u32[]{:S(2)}) async-start(bf16[16,192,128]{2,1,0:T(8,128)(2,1)} %bitcast.7), calls=%async_computation | async-start | bytes 1572864 | tf_op jit(solution)/shard_map/all_to_all | solution.py:140
  36.3 2.0 collective-permute-start
  38.9 20.0 %all-to-all-done = bf16[16,192,128]{2,1,0:T(8,128)(2,1)S(1)} async-done(((bf16[16,192,128]{2,1,0:T(8,128)(2,1)}), bf16[16,192,128]{2,1,0:T(8,128)(2,1)S(1)}, u32[]{:S(2)}, u32[]{:S(2)}) %all-to-all-start) | async-done | bytes 786464 | tf_op jit(solution)/shard_map/all_to_all | solution.py:140
  59.7 3.4 %all-to-all-start.2 = ((bf16[16,64,128]{2,1,0:T(8,128)(2,1)}), bf16[16,64,128]{2,1,0:T(8,128)(2,1)S(1)}, u32[]{:S(2)}, u32[]{:S(2)}) async-start(bf16[16,64,128]{2,1,0:T(8,128)(2,1)} %bitcast.12), calls=%async_computation.2 | async-start | bytes 524288 | tf_op jit(solution)/shard_map/all_to_all | solution.py:140
  63.6 11.0 %all-to-all-done.2 = bf16[16,64,128]{2,1,0:T(8,128)(2,1)S(1)} async-done(((bf16[16,64,128]{2,1,0:T(8,128)(2,1)}), bf16[16,64,128]{2,1,0:T(8,128)(2,1)S(1)}, u32[]{:S(2)}, u32[]{:S(2)}) %all-to-all-start.2) | async-done | bytes 262176 | tf_op jit(solution)/shard_map/all_to_all | solution.py:140
  74.6 27.0 %edge_sums.2 = (bf16[3072,128]{1,0:T(8,128)(2,1)}, bf16[1024,128]{1,0:T(8,128)(2,1)S(1)}) custom-call(s32[2]{0:T(128)S(1)} %and_select_fusion.4.counts_ref, s32[2,4096]{1,0:T(2,128)S(1)} %get-tuple-element.53.packed_ref, bf16[3072,128]{1,0:T(8,128)(2,1)S(1)} %bitcast.103, bf16[1024,128]{1,0:T(8,128)(2,1)S(1)} %bitcast.105), custom_call_target="tpu_custom_call" | custom-call | flops 2097152 | bytes 2097152 | tf_op jit(solution)/shard_map/edge_sums/pallas_call | solution.py:77
  101.6 13.6 %all_to_all.61 = bf16[16,64,128]{2,1,0:T(8,128)(2,1)S(1)} all-to-all(bf16[16,64,128]{2,1,0:T(8,128)(2,1)S(1)} %bitcast.108), channel_id=1, replica_groups=mesh['dom'=32,'member'=16] {'member'}, dimensions={0} | all-to-all | bytes 524288 | tf_op jit(solution)/shard_map/all_to_all | solution.py:140
  115.6 13.4 %all_to_all.62 = bf16[32,4,256]{2,1,0:T(4,128)(2,1)S(1)} all-to-all(bf16[32,4,256]{2,1,0:T(4,128)(2,1)S(1)} %reshape.396), channel_id=1, replica_groups=mesh['dom'=32,'member'=16] {'dom'}, dimensions={0} | all-to-all | bytes 131072 | tf_op jit(solution)/shard_map/all_to_all | solution.py:127
  129.0 4.9 %all-to-all-start.5 = ((bf16[16,192,128]{2,1,0:T(8,128)(2,1)}), bf16[16,192,128]{2,1,0:T(8,128)(2,1)S(1)}, u32[]{:S(2)}, u32[]{:S(2)}) async-start(bf16[16,192,128]{2,1,0:T(8,128)(2,1)} %bitcast.17), calls=%async_computation.5 | async-start | bytes 1572864 | tf_op jit(solution)/shard_map/all_to_all | solution.py:140
  134.5 22.2 %all-to-all-done.5 = bf16[16,192,128]{2,1,0:T(8,128)(2,1)S(1)} async-done(((bf16[16,192,128]{2,1,0:T(8,128)(2,1)}), bf16[16,192,128]{2,1,0:T(8,128)(2,1)S(1)}, u32[]{:S(2)}, u32[]{:S(2)}) %all-to-all-start.5) | async-done | bytes 786464 | tf_op jit(solution)/shard_map/all_to_all | solution.py:140
  158.7 1.0 broadcast_in_dim.95
  160.2 18.6 %all_to_all.63 = bf16[32,12,512]{2,1,0:T(8,128)(2,1)S(1)} all-to-all(bf16[32,12,512]{2,1,0:T(8,128)(2,1)S(1)} %maximum_maximum_fusion), channel_id=1, replica_groups=mesh['dom'=32,'member'=16] {'dom'}, dimensions={0} | all-to-all | bytes 786432 | tf_op jit(solution)/shard_map/all_to_all | solution.py:127
  178.8 4.8 %all-to-all-start.7 = ((bf16[16,192,128]{2,1,0:T(8,128)(2,1)}), bf16[16,192,128]{2,1,0:T(8,128)(2,1)S(1)}, u32[]{:S(2)}, u32[]{:S(2)}) async-start(bf16[16,192,128]{2,1,0:T(8,128)(2,1)} %bitcast.23), calls=%async_computation.7 | async-start | bytes 1572864 | tf_op jit(solution)/shard_map/all_to_all | solution.py:140
  184.0 22.3 %all-to-all-done.7 = bf16[16,192,128]{2,1,0:T(8,128)(2,1)S(1)} async-done(((bf16[16,192,128]{2,1,0:T(8,128)(2,1)}), bf16[16,192,128]{2,1,0:T(8,128)(2,1)S(1)}, u32[]{:S(2)}, u32[]{:S(2)}) %all-to-all-start.7) | async-done | bytes 786464 | tf_op jit(solution)/shard_map/all_to_all | solution.py:140
  207.1 3.4 %all-to-all-start.8 = ((bf16[16,64,128]{2,1,0:T(8,128)(2,1)}), bf16[16,64,128]{2,1,0:T(8,128)(2,1)S(1)}, u32[]{:S(2)}, u32[]{:S(2)}) async-start(bf16[16,64,128]{2,1,0:T(8,128)(2,1)} %bitcast.30), calls=%async_computation.8 | async-start | bytes 524288 | tf_op jit(solution)/shard_map/all_to_all | solution.py:140
  210.6 11.4 %all-to-all-done.8 = bf16[16,64,128]{2,1,0:T(8,128)(2,1)S(1)} async-done(((bf16[16,64,128]{2,1,0:T(8,128)(2,1)}), bf16[16,64,128]{2,1,0:T(8,128)(2,1)S(1)}, u32[]{:S(2)}, u32[]{:S(2)}) %all-to-all-start.8) | async-done | bytes 262176 | tf_op jit(solution)/shard_map/all_to_all | solution.py:140
  222.0 27.0 %edge_sums.3 = (bf16[3072,128]{1,0:T(8,128)(2,1)}, bf16[1024,128]{1,0:T(8,128)(2,1)S(1)}) custom-call(s32[2]{0:T(128)S(1)} %and_select_fusion.4.counts_ref, s32[2,4096]{1,0:T(2,128)S(1)} %get-tuple-element.53.packed_ref, bf16[3072,128]{1,0:T(8,128)(2,1)S(1)} %bitcast.104, bf16[1024,128]{1,0:T(8,128)(2,1)S(1)} %bitcast.106), custom_call_target="tpu_custom_call" | custom-call | flops 2097152 | bytes 2097152 | tf_op jit(solution)/shard_map/edge_sums/pallas_call | solution.py:77
  249.1 16.6 %all_to_all.64 = bf16[16,96,128]{2,1,0:T(8,128)(2,1)S(1)} all-to-all(bf16[16,96,128]{2,1,0:T(8,128)(2,1)S(1)} %pad_maximum_fusion), channel_id=1, replica_groups=mesh['dom'=32,'member'=16] {'member'}, dimensions={0} | all-to-all | bytes 786432 | tf_op jit(solution)/shard_map/all_to_all | solution.py:140
  266.3 21.6 %all_to_all.65 = bf16[32,20,256]{2,1,0:T(8,128)(2,1)S(1)} all-to-all(bf16[32,20,256]{2,1,0:T(8,128)(2,1)S(1)} %pad_maximum_fusion.1), channel_id=1, replica_groups=mesh['dom'=32,'member'=16] {'dom'}, dimensions={0} | all-to-all | bytes 655360 | tf_op jit(solution)/shard_map/all_to_all | solution.py:127
  287.9 3.8 %all-to-all-start.11 = ((bf16[16,192,128]{2,1,0:T(8,128)(2,1)}), bf16[16,192,128]{2,1,0:T(8,128)(2,1)S(1)}, u32[]{:S(2)}, u32[]{:S(2)}) async-start(bf16[16,192,128]{2,1,0:T(8,128)(2,1)} %bitcast.35), calls=%async_computation.11 | async-start | bytes 1572864 | tf_op jit(solution)/shard_map/all_to_all | solution.py:140
  294.1 20.3 %all-to-all-done.11 = bf16[16,192,128]{2,1,0:T(8,128)(2,1)S(1)} async-done(((bf16[16,192,128]{2,1,0:T(8,128)(2,1)}), bf16[16,192,128]{2,1,0:T(8,128)(2,1)S(1)}, u32[]{:S(2)}, u32[]{:S(2)}) %all-to-all-start.11) | async-done | bytes 786464 | tf_op jit(solution)/shard_map/all_to_all | solution.py:140
  (87 shorter events, 12.0 us)
Async XLA Ops:
  0.6 156.4 %copy-start = (bf16[256,256]{1,0:T(8,128)(2,1)S(1)}, bf16[256,256]{1,0:T(8,128)(2,1)}, u32[]{:S(2)}) copy-start(bf16[256,256]{1,0:T(8,128)(2,1)} %param.17) | copy-start | bytes 393220
  1.5 34.7 %copy-start.3 = (s32[1,1,4096]{2,1,0:T(1,128)S(1)}, s32[1,1,4096]{2,1,0:T(1,128)}, u32[]{:S(2)}) copy-start(s32[1,1,4096]{2,1,0:T(1,128)} %param.12) | copy-start | bytes 49156
  1.5 34.7 %copy-start.4 = (s32[1,1,4096]{2,1,0:T(1,128)S(1)}, s32[1,1,4096]{2,1,0:T(1,128)}, u32[]{:S(2)}) copy-start(s32[1,1,4096]{2,1,0:T(1,128)} %param.11) | copy-start | bytes 49156
  1.5 36.8 %copy-start.5 = (s32[1,1,32,4]{2,3,1,0:T(4,128)S(1)}, s32[1,1,32,4]{2,3,1,0:T(4,128)}, u32[]{:S(2)}) copy-start(s32[1,1,32,4]{2,3,1,0:T(4,128)} %param.13) | copy-start | bytes 1540
  1.6 37.0 %copy-start.1 = (bf16[256,256]{1,0:T(8,128)(2,1)S(1)}, bf16[256,256]{1,0:T(8,128)(2,1)}, u32[]{:S(2)}) copy-start(bf16[256,256]{1,0:T(8,128)(2,1)} %param.9) | copy-start | bytes 393220
  27.0 31.9 %all-to-all-start = ((bf16[16,192,128]{2,1,0:T(8,128)(2,1)}), bf16[16,192,128]{2,1,0:T(8,128)(2,1)S(1)}, u32[]{:S(2)}, u32[]{:S(2)}) async-start(bf16[16,192,128]{2,1,0:T(8,128)(2,1)} %bitcast.7), calls=%async_computation | async-start | bytes 1572864 | tf_op jit(solution)/shard_map/all_to_all | solution.py:140
  36.3 27.1 %collective-permute-start = (s32[4096]{0:T(1024)S(1)}, s32[4096]{0:T(1024)S(1)}, u32[]{:S(2)}, u32[]{:S(2)}) collective-permute-start(s32[4096]{0:T(1024)S(1)} %or_select_fusion), channel_id=1, source_target_pairs={{0,1},{1,0},{2,3},{3,2},{4,5},{5,4},{6,7},{7,6},{8,9},{9,8},{10,11... | collective-permute-start | bytes 49160 | tf_op jit(solution)/shard_map/ppermute | solution.py:166
  59.7 14.9 %all-to-all-start.2 = ((bf16[16,64,128]{2,1,0:T(8,128)(2,1)}), bf16[16,64,128]{2,1,0:T(8,128)(2,1)S(1)}, u32[]{:S(2)}, u32[]{:S(2)}) async-start(bf16[16,64,128]{2,1,0:T(8,128)(2,1)} %bitcast.12), calls=%async_computation.2 | async-start | bytes 524288 | tf_op jit(solution)/shard_map/all_to_all | solution.py:140
  115.3 18.6 %copy-start.6 = (s32[1,1,256]{2,1,0:T(1,128)S(1)}, s32[1,1,256]{2,1,0:T(1,128)}, u32[]{:S(2)}) copy-start(s32[1,1,256]{2,1,0:T(1,128)} %param.15) | copy-start | bytes 3076
  115.3 18.7 %copy-start.2 = (bf16[256,256]{1,0:T(8,128)(2,1)S(1)}, bf16[256,256]{1,0:T(8,128)(2,1)}, u32[]{:S(2)}) copy-start(bf16[256,256]{1,0:T(8,128)(2,1)} %param.16) | copy-start | bytes 393220
  129.0 27.6 %all-to-all-start.5 = ((bf16[16,192,128]{2,1,0:T(8,128)(2,1)}), bf16[16,192,128]{2,1,0:T(8,128)(2,1)S(1)}, u32[]{:S(2)}, u32[]{:S(2)}) async-start(bf16[16,192,128]{2,1,0:T(8,128)(2,1)} %bitcast.17), calls=%async_computation.5 | async-start | bytes 1572864 | tf_op jit(solution)/shard_map/all_to_all | solution.py:140
  156.8 0.9 copy-start.7
  178.8 27.5 %all-to-all-start.7 = ((bf16[16,192,128]{2,1,0:T(8,128)(2,1)}), bf16[16,192,128]{2,1,0:T(8,128)(2,1)S(1)}, u32[]{:S(2)}, u32[]{:S(2)}) async-start(bf16[16,192,128]{2,1,0:T(8,128)(2,1)} %bitcast.23), calls=%async_computation.7 | async-start | bytes 1572864 | tf_op jit(solution)/shard_map/all_to_all | solution.py:140
  207.1 14.9 %all-to-all-start.8 = ((bf16[16,64,128]{2,1,0:T(8,128)(2,1)}), bf16[16,64,128]{2,1,0:T(8,128)(2,1)S(1)}, u32[]{:S(2)}, u32[]{:S(2)}) async-start(bf16[16,64,128]{2,1,0:T(8,128)(2,1)} %bitcast.30), calls=%async_computation.8 | async-start | bytes 524288 | tf_op jit(solution)/shard_map/all_to_all | solution.py:140
  287.9 26.5 %all-to-all-start.11 = ((bf16[16,192,128]{2,1,0:T(8,128)(2,1)}), bf16[16,192,128]{2,1,0:T(8,128)(2,1)S(1)}, u32[]{:S(2)}, u32[]{:S(2)}) async-start(bf16[16,192,128]{2,1,0:T(8,128)(2,1)} %bitcast.35), calls=%async_computation.11 | async-start | bytes 1572864 | tf_op jit(solution)/shard_map/all_to_all | solution.py:140

commit v3 on v2

v3 whole, which is shorter than its diff:
```python
import functools

import jax
import jax.numpy as jnp
from jax import lax
from jax.experimental import pallas as pl
from jax.experimental.pallas import tpu as pltpu
from jax.sharding import PartitionSpec as P

MIRR = 62
LATE = 64
UNROLL = 16
ACCS = 4
CHUNK = 128


def edge_kernel(take_high, bounds_ref, words_ref, table_ref, out_ref, words, table, *rest):
    accs, sems = rest[:-1], rest[-1]
    rows, width = table_ref.shape
    pad = table.shape[0] - rows
    lists = sems.shape[0]
    length = words.shape[0] // lists

    def copy(m):
        span = pl.ds(m * length, length)
        return pltpu.make_async_copy(words_ref.at[span], words.at[span], sems.at[m])

    for m in range(lists):

        @pl.when(bounds_ref[1, m] > bounds_ref[0, m])
        def _():
            copy(m).start()

    def load(i, _):
        span = pl.ds(pl.multiple_of(i * CHUNK, CHUNK), CHUNK)
        table[span, :] = table_ref[span, :].astype(jnp.float32)
        for acc in accs:
            acc[span, :] = jnp.zeros((CHUNK, width), jnp.float32)
        return 0

    lax.fori_loop(0, rows // CHUNK, load, 0)
    table[pl.ds(rows, pad), :] = jnp.zeros((pad, width), jnp.float32)

    one_row = (rows + pad, 1, width)
    table_rows = table.reshape(one_row)
    acc_rows = [acc.reshape(one_row) for acc in accs]
    for m in range(lists):

        def step(i, _):
            for group in range(UNROLL // ACCS):
                takes, places = [], []
                for k in range(ACCS):
                    word = words[m * length + i * UNROLL + group * ACCS + k]
                    low, high = word & 0xFFFF, word >> 16
                    takes.append(high if take_high else low)
                    places.append(low if take_high else high)
                sums = [acc_rows[k][places[k]] + table_rows[takes[k]] for k in range(ACCS)]
                for k in range(ACCS):
                    acc_rows[k][places[k]] = sums[k]
            return 0

        @pl.when(bounds_ref[1, m] > bounds_ref[0, m])
        def _():
            copy(m).wait()
            lax.fori_loop(bounds_ref[0, m], bounds_ref[1, m], step, 0)

    def store(i, _):
        span = pl.ds(pl.multiple_of(i * CHUNK, CHUNK), CHUNK)
        total = accs[0][span, :]
        for acc in accs[1:]:
            total = total + acc[span, :]
        out_ref[span, :] = total.astype(out_ref.dtype)
        return 0

    lax.fori_loop(0, rows // CHUNK, store, 0)


def edge_sums(take_high, bounds, words, table):
    rows, width = table.shape
    lists = bounds.shape[1]
    vmem = pl.BlockSpec(memory_space=pltpu.VMEM)
    return pl.pallas_call(
        functools.partial(edge_kernel, take_high),
        out_shape=jax.ShapeDtypeStruct((rows, width), jnp.bfloat16),
        in_specs=[
            pl.BlockSpec(memory_space=pltpu.SMEM),
            pl.BlockSpec(memory_space=pl.ANY),
            vmem,
        ],
        out_specs=vmem,
        scratch_shapes=[pltpu.SMEM(words.shape, jnp.int32)]
        + [pltpu.VMEM((rows + 8, width), jnp.float32)] * (1 + ACCS)
        + [pltpu.SemaphoreType.DMA((lists,))],
        compiler_params=pltpu.CompilerParams(vmem_limit_bytes=40 * 1024 * 1024),
        cost_estimate=pl.CostEstimate(
            flops=16384 * width, bytes_accessed=4 * rows * width, transcendentals=0
        ),
        name="edge_sums",
    )(bounds, words, table)


def body(
    features,
    cotangent,
    edge_src,
    edge_dst,
    send_rows,
    recv_rows,
    in_degree,
    weight_self,
    weight_neigh,
):
    rows, width = features.shape
    half = width // 2
    early = rows - LATE
    dom_count = lax.axis_size("dom")
    members = lax.axis_size("member")
    part_rows = rows * members
    contract_first = (((0,), (0,)), ((), ()))
    f32, bf16 = jnp.float32, jnp.bfloat16

    send_list = send_rows.reshape(-1)
    recv_list = recv_rows.reshape(-1)
    slot_count = send_list.shape[0]
    cap = slot_count // dom_count
    columns = lax.broadcasted_iota(jnp.int32, (slot_count, rows), 1)
    late_columns = lax.broadcasted_iota(jnp.int32, (slot_count, LATE), 1) + early
    pick_send = (send_list[:, None] == late_columns).astype(bf16)
    pick_recv = (recv_list[:, None] == columns).astype(bf16)
    is_mirror = lax.broadcasted_iota(jnp.int32, (rows, 1), 0) >= rows - MIRR
    late_mirror = is_mirror[early:]
    denominator = in_degree.reshape(-1).astype(f32)[:, None] + 1.0

    def over_dom(slots):
        return lax.all_to_all(slots, "dom", split_axis=0, concat_axis=0, tiled=True)

    def from_masters(values):
        slots = jnp.dot(pick_recv, values, preferred_element_type=f32).astype(bf16)
        return slots.reshape(dom_count, -1, values.shape[1])

    def at_mirrors(slots, values):
        arrived = lax.dot_general(
            pick_send, slots.reshape(slot_count, -1), contract_first, preferred_element_type=f32
        )
        return jnp.where(late_mirror, arrived.astype(bf16), values[early:])

    def over_member(blocks):
        return lax.all_to_all(blocks, "member", split_axis=0, concat_axis=0, tiled=True)

    def gather(values):
        halves = jnp.stack([values[:, :half], values[:, half:]])
        every = jnp.broadcast_to(halves[None], (members // 2,) + halves.shape)
        return over_member(every.reshape(members, rows, half)).reshape(-1, half)

    def member_sum(arrived):
        by_core = arrived.reshape((members // 2, 2) + arrived.shape[1:]).astype(f32)
        return jnp.concatenate([jnp.sum(by_core[:, core], axis=0) for core in (0, 1)], axis=1)

    src, dst = edge_src.reshape(-1), edge_dst.reshape(-1)
    words = jnp.where(src >= 0, (dst << 16) | src, (part_rows << 16) | part_rows)
    mine = words.reshape(1, -1)
    index = lax.axis_index("member")
    bit = 1
    while bit < members:
        theirs = lax.ppermute(mine, "member", [(m, m ^ bit) for m in range(members)])
        low = (index & bit) == 0
        mine = jnp.concatenate([jnp.where(low, mine, theirs), jnp.where(low, theirs, mine)])
        bit *= 2
    blocks = jnp.sum((mine < (part_rows << 16)).astype(jnp.int32), axis=1)
    blocks = (blocks + UNROLL - 1) // UNROLL
    before = jnp.sum(
        jnp.where(
            lax.broadcasted_iota(jnp.int32, (members, members), 1)
            < lax.broadcasted_iota(jnp.int32, (members, members), 0),
            blocks[None, :],
            0,
        ),
        axis=1,
    )
    total = jnp.sum(blocks)
    chips = members // 2
    chip = index >> 1
    bounds = jnp.stack(
        [jnp.clip(lax.div(total * at, chips) - before, 0, blocks) for at in (chip, chip + 1)]
    )
    words = mine.reshape(-1)

    def partition_sums(table, take_high, weight_sum=None):
        part = edge_sums(take_high, bounds, words, table).reshape(members, rows, half)
        if weight_sum is not None:
            share = weight_sum.astype(bf16).reshape(-1, half)
            share = jnp.broadcast_to(share[None], (members,) + share.shape)
            part = jnp.concatenate([part, share], axis=1)
        arrived = over_member(part)
        totals = member_sum(arrived[:, :rows])
        slots = jnp.dot(pick_send, totals[early:].astype(bf16), preferred_element_type=f32)
        slots = slots.astype(bf16).reshape(dom_count, -1, width)
        weight_sums = None
        if weight_sum is not None:
            share = jnp.sum(arrived[:, rows:].astype(f32), axis=0).astype(bf16)
            share = share.reshape(-1, width)
            share = jnp.broadcast_to(share[None], (dom_count,) + share.shape)
            slots = jnp.concatenate([slots, share], axis=1)
        moved = over_dom(slots)
        if weight_sum is not None:
            weight_sums = moved[:, cap:].reshape(-1, 2 * width).astype(f32)
        from_mirrors = lax.dot_general(
            pick_recv,
            moved[:, :cap].reshape(slot_count, width),
            contract_first,
            preferred_element_type=f32,
        )
        return totals + from_mirrors, weight_sums

    late_rows = at_mirrors(over_dom(from_masters(features)), features)
    table = gather(jnp.concatenate([features[:early], late_rows], axis=0))
    totals, _ = partition_sums(table, False)
    averaged = (totals / denominator).astype(bf16)

    pre = jnp.dot(features, weight_self, preferred_element_type=f32) + jnp.dot(
        averaged, weight_neigh, preferred_element_type=f32
    )
    gate_sig = jax.nn.sigmoid(pre)
    activated = (pre * gate_sig).astype(bf16)
    slope = gate_sig * (1.0 + pre * (1.0 - gate_sig))
    grad_pre = jnp.where(is_mirror, 0.0, cotangent.astype(f32) * slope).astype(bf16)
    grad_mean = (
        jnp.dot(grad_pre, weight_neigh.T, preferred_element_type=f32) / denominator
    ).astype(bf16)
    local_self = lax.dot_general(features, grad_pre, contract_first, preferred_element_type=f32)
    local_neigh = lax.dot_general(averaged, grad_pre, contract_first, preferred_element_type=f32)
    self_term = jnp.dot(grad_pre, weight_self.T, preferred_element_type=f32)

    local_weights = jnp.concatenate([local_self, local_neigh], axis=1).astype(bf16)
    share = local_weights.reshape(dom_count, -1, 2 * width)
    slots = from_masters(jnp.concatenate([grad_mean, activated], axis=1))
    moved = over_dom(jnp.concatenate([slots, share], axis=1))
    arrived = moved[:, :cap]
    late_rows = at_mirrors(arrived[:, :, :width], grad_mean)
    table = gather(jnp.concatenate([grad_mean[:early], late_rows], axis=0))
    activated_late = at_mirrors(arrived[:, :, width:], activated)
    activated = jnp.concatenate([activated[:early], activated_late], axis=0)

    weight_sum = jnp.sum(moved[:, cap:].astype(f32), axis=0)
    back_sum, weight_sums = partition_sums(table, True, weight_sum)
    grad_features = jnp.where(is_mirror, 0.0, back_sum + self_term).astype(bf16)
    return activated, grad_features, weight_sums[:, :width], weight_sums[:, width:]


def solution(mesh):
    placed = (
        P(("dom", "member"), None),
        P(("dom", "member"), None),
        P("dom", "member", None),
        P("dom", "member", None),
        P("dom", "member", None, None),
        P("dom", "member", None, None),
        P("dom", "member", None),
        P(),
        P(),
    )
    return jax.shard_map(
        body,
        mesh=mesh,
        in_specs=placed,
        out_specs=(P(("dom", "member"), None), P(("dom", "member"), None), P(), P()),
        check_vma=False,
    )
```

time: 316 us -> 275 us (0.87)
  blocking collectives: 106 us -> 34.9 us
  starting transfers between devices: 31.6 us -> 70.5 us
  Pallas kernels: 54.1 us -> 26.6 us
  waiting for transfers between devices: 107 us -> 119 us
    all_to_all x4 -> x0, blocking collectives: 76 us -> none  [over_dom(): return lax.all_to_all(slots, 'dom', split_axis=0, concat_axis=0, tiled=True)]
    all_to_all x6 -> x3, waiting for transfers between devices: 107 us -> 55.5 us  [over_member(): lax.all_to_all(blocks, 'member', split_axis=0, concat_axis=0, tiled=True)]
    all_to_all x0 -> x4, waiting for transfers between devices: none -> 37.7 us  [over_dom(): return lax.all_to_all(slots, 'dom', split_axis=0, concat_axis=0, tiled=True)]
    pallas_call x2, Pallas kernels: 54.1 us -> 26.6 us  [edge_sums(): pl.pallas_call(functools.partial(edge_kernel, take_high), out_shape=jax.S...]
    all_to_all x0 -> x4, starting transfers between devices: none -> 26.9 us  [over_dom(): return lax.all_to_all(slots, 'dom', split_axis=0, concat_axis=0, tiled=True)]
    ppermute x1 -> x4, waiting for transfers between devices: 0.01 us -> 26.2 us  [body(): lax.ppermute(mine, 'member', [(m, m ^ bit) for m in range(members)])]
    ppermute x1 -> x4, starting transfers between devices: 2.01 us -> 23.4 us  [body(): lax.ppermute(mine, 'member', [(m, m ^ bit) for m in range(members)])]
    all_to_all x6 -> x3, starting transfers between devices: 29.6 us -> 20.2 us  [over_member(): lax.all_to_all(blocks, 'member', split_axis=0, concat_axis=0, tiled=True)]
  transfers between devices with their start and end apart: 7 -> 11, of which waited for: 6 -> 7; matrix products, arithmetic and copies ran while one was open for 2% -> 3% of each run, Pallas kernels for 0% -> 0%
where the time goes in v3:
time: 275 us; the launch traced here: 273 us
  waiting for transfers between devices  119 us (43%)
  starting transfers between devices  70.5 us (26%)
  blocking collectives  34.9 us (13%)
  Pallas kernels  26.6 us (10%)
  local copies, waits for them, and re-layouts  7.69 us (3%)
  matrix products  5.94 us (2%)
  other arithmetic  5.43 us (2%)
    all_to_all x3, waiting for transfers between devices, over_member(): lax.all_to_all(blocks, 'member', split_axis=0, concat_axis=0, tiled=True)  55.5 us
    all_to_all x4, waiting for transfers between devices, over_dom(): return lax.all_to_all(slots, 'dom', split_axis=0, concat_axis=0, tiled=True)  37.7 us
    all_to_all x1, blocking collectives, over_member(): lax.all_to_all(blocks, 'member', split_axis=0, concat_axis=0, tiled=True)  34.9 us
    all_to_all x4, starting transfers between devices, over_dom(): return lax.all_to_all(slots, 'dom', split_axis=0, concat_axis=0, tiled=True)  26.9 us
    pallas_call x2, Pallas kernels, edge_sums(): pl.pallas_call(functools.partial(edge_kernel, take_high), out_shape=jax.S...  26.6 us
    ppermute x4, waiting for transfers between devices, body(): lax.ppermute(mine, 'member', [(m, m ^ bit) for m in range(members)])  26.2 us
    ppermute x4, starting transfers between devices, body(): lax.ppermute(mine, 'member', [(m, m ^ bit) for m in range(members)])  23.4 us
    all_to_all x3, starting transfers between devices, over_member(): lax.all_to_all(blocks, 'member', split_axis=0, concat_axis=0, tiled=True)  20.2 us
  transfers between devices with their start and end apart: 11, of which 7 were waited for; matrix products, arithmetic and copies ran while one was open for 3% of the time, Pallas kernels for 0%

profile of v3, /device:TPU:1, one launch (start us, length us, event | category | flops | bytes accessed | tf_op | source)
XLA Modules:
  0.0 273.0 jit_solution(1406732725016622250)
XLA Ops:
  1.4 8.8 %collective-permute-start = (s32[1,4096]{1,0:T(1,128)S(1)}, s32[1,4096]{1,0:T(1,128)S(1)}, u32[]{:S(2)}, u32[]{:S(2)}) collective-permute-start(s32[1,4096]{1,0:T(1,128)S(1)} %fusion.45), channel_id=1, source_target_pairs={{0,1},{1,0},{2,3},{3,2},{4,5},{5,4},{6,7},{7,6},{8,9},{9,8},{10,11... | collective-permute-start | bytes 49160 | tf_op jit(solution)/shard_map/ppermute | solution.py:165
  11.1 1.1 convolution_convert_fusion.5
  12.9 7.5 %all-to-all-start = ((bf16[32,4,256]{2,1,0:T(4,128)(2,1)}), bf16[32,4,256]{2,1,0:T(4,128)(2,1)S(1)}, u32[]{:S(2)}, u32[]{:S(2)}) async-start(bf16[32,4,256]{2,1,0:T(4,128)(2,1)} %reshape.233), calls=%async_computation | async-start | bytes 131072 | tf_op jit(solution)/shard_map/all_to_all | solution.py:135
  20.5 3.2 %collective-permute-start.1 = (s32[2,4096]{1,0:T(2,128)S(1)}, s32[2,4096]{1,0:T(2,128)S(1)}, u32[]{:S(2)}, u32[]{:S(2)}) collective-permute-start(s32[2,4096]{1,0:T(2,128)S(1)} %pad_add_fusion.3), channel_id=1, source_target_pairs={{0,2},{1,3},{2,0},{3,1},{4,6},{5,7},{6,4},{7,5},{8,10},{9,11},{10,... | collective-permute-start | bytes 98312 | tf_op jit(solution)/shard_map/ppermute | solution.py:165
  25.6 4.2 %collective-permute-start.2 = (s32[4,4096]{1,0:T(4,128)S(1)}, s32[4,4096]{1,0:T(4,128)S(1)}, u32[]{:S(2)}, u32[]{:S(2)}) collective-permute-start(s32[4,4096]{1,0:T(4,128)S(1)} %pad_add_fusion.2), channel_id=1, source_target_pairs={{0,4},{1,5},{2,6},{3,7},{4,0},{5,1},{6,2},{7,3},{8,12},{9,13},{10,... | collective-permute-start | bytes 196616 | tf_op jit(solution)/shard_map/ppermute | solution.py:165
  29.8 1.7 collective-permute-done.2
  32.7 1.2 broadcast_in_dim.91
  33.8 10.1 %all-to-all-start.1 = ((bf16[16,256,128]{2,1,0:T(8,128)(2,1)}), bf16[16,256,128]{2,1,0:T(8,128)(2,1)S(1)}, u32[]{:S(2)}, u32[]{:S(2)}) async-start(bf16[16,256,128]{2,1,0:T(8,128)(2,1)} %bitcast.7), calls=%async_computation.1 | async-start | bytes 2097152 | tf_op jit(solution)/shard_map/all_to_all | solution.py:148
  43.9 7.2 %collective-permute-start.3 = (s32[8,4096]{1,0:T(8,128)S(1)}, s32[8,4096]{1,0:T(8,128)S(1)}, u32[]{:S(2)}, u32[]{:S(2)}) collective-permute-start(s32[8,4096]{1,0:T(8,128)S(1)} %pad_add_fusion.1), channel_id=1, source_target_pairs={{0,8},{1,9},{2,10},{3,11},{4,12},{5,13},{6,14},{7,15},{8,0},{9,1},... | collective-permute-start | bytes 393224 | tf_op jit(solution)/shard_map/ppermute | solution.py:165
  51.1 24.5 %collective-permute-done.3 = s32[8,4096]{1,0:T(8,128)S(1)} collective-permute-done((s32[8,4096]{1,0:T(8,128)S(1)}, s32[8,4096]{1,0:T(8,128)S(1)}, u32[]{:S(2)}, u32[]{:S(2)}) %collective-permute-start.3) | collective-permute-done | bytes 131104 | tf_op jit(solution)/shard_map/ppermute | solution.py:165
  78.0 13.8 %edge_sums.2 = bf16[4096,128]{1,0:T(8,128)(2,1)} custom-call(s32[2,16]{1,0:T(2,128)S(1)} %pad_add_fusion.4.bounds_ref, s32[65536]{0:T(1024)S(1)} %bitcast.75, bf16[4096,128]{1,0:T(8,128)(2,1)S(1)} %bitcast.72), custom_call_target="tpu_custom_call" | custom-call | flops 2097152 | bytes 2097152 | tf_op jit(solution)/shard_map/edge_sums/pallas_call | solution.py:82
  91.8 5.5 %all-to-all-start.2 = ((bf16[16,256,128]{2,1,0:T(8,128)(2,1)}), bf16[16,256,128]{2,1,0:T(8,128)(2,1)S(1)}, u32[]{:S(2)}, u32[]{:S(2)}) async-start(bf16[16,256,128]{2,1,0:T(8,128)(2,1)} %bitcast.9), calls=%async_computation.2 | async-start | bytes 2097152 | tf_op jit(solution)/shard_map/all_to_all | solution.py:148
  97.6 27.7 %all-to-all-done.2 = bf16[16,256,128]{2,1,0:T(8,128)(2,1)S(1)} async-done(((bf16[16,256,128]{2,1,0:T(8,128)(2,1)}), bf16[16,256,128]{2,1,0:T(8,128)(2,1)S(1)}, u32[]{:S(2)}, u32[]{:S(2)}) %all-to-all-start.2) | async-done | bytes 1048608 | tf_op jit(solution)/shard_map/all_to_all | solution.py:148
  126.5 9.4 %all-to-all-start.3 = ((bf16[32,4,256]{2,1,0:T(4,128)(2,1)}), bf16[32,4,256]{2,1,0:T(4,128)(2,1)S(1)}, u32[]{:S(2)}, u32[]{:S(2)}) async-start(bf16[32,4,256]{2,1,0:T(4,128)(2,1)} %reshape.238), calls=%async_computation.3 | async-start | bytes 131072 | tf_op jit(solution)/shard_map/all_to_all | solution.py:135
  135.9 9.1 %all-to-all-done.3 = bf16[32,4,256]{2,1,0:T(4,128)(2,1)S(1)} async-done(((bf16[32,4,256]{2,1,0:T(4,128)(2,1)}), bf16[32,4,256]{2,1,0:T(4,128)(2,1)S(1)}, u32[]{:S(2)}, u32[]{:S(2)}) %all-to-all-start.3) | async-done | bytes 65568 | tf_op jit(solution)/shard_map/all_to_all | solution.py:135
  147.7 3.9 %all-to-all-start.4 = ((bf16[32,12,512]{2,1,0:T(8,128)(2,1)}), bf16[32,12,512]{2,1,0:T(8,128)(2,1)S(1)}, u32[]{:S(2)}, u32[]{:S(2)}) async-start(bf16[32,12,512]{2,1,0:T(8,128)(2,1)} %maximum_maximum_fusion), calls=%async_computation.4 | async-start | bytes 1048576 | tf_op jit(solution)/shard_map/all_to_all | solution.py:135
  151.6 16.5 %all-to-all-done.4 = bf16[32,12,512]{2,1,0:T(8,128)(2,1)S(1)} async-done(((bf16[32,12,512]{2,1,0:T(8,128)(2,1)}), bf16[32,12,512]{2,1,0:T(8,128)(2,1)S(1)}, u32[]{:S(2)}, u32[]{:S(2)}) %all-to-all-start.4) | async-done | bytes 393248 | tf_op jit(solution)/shard_map/all_to_all | solution.py:135
  168.4 1.2 broadcast_in_dim.94
  169.6 4.7 %all-to-all-start.5 = ((bf16[16,256,128]{2,1,0:T(8,128)(2,1)}), bf16[16,256,128]{2,1,0:T(8,128)(2,1)S(1)}, u32[]{:S(2)}, u32[]{:S(2)}) async-start(bf16[16,256,128]{2,1,0:T(8,128)(2,1)} %bitcast.18), calls=%async_computation.5 | async-start | bytes 2097152 | tf_op jit(solution)/shard_map/all_to_all | solution.py:148
  174.3 27.8 %all-to-all-done.5 = bf16[16,256,128]{2,1,0:T(8,128)(2,1)S(1)} async-done(((bf16[16,256,128]{2,1,0:T(8,128)(2,1)}), bf16[16,256,128]{2,1,0:T(8,128)(2,1)S(1)}, u32[]{:S(2)}, u32[]{:S(2)}) %all-to-all-start.5) | async-done | bytes 1048608 | tf_op jit(solution)/shard_map/all_to_all | solution.py:148
  202.2 12.8 %edge_sums.3 = bf16[4096,128]{1,0:T(8,128)(2,1)S(1)} custom-call(s32[2,16]{1,0:T(2,128)S(1)} %pad_add_fusion.4.bounds_ref, s32[65536]{0:T(1024)S(1)} %bitcast.76, bf16[4096,128]{1,0:T(8,128)(2,1)S(1)} %bitcast.73), custom_call_target="tpu_custom_call" | custom-call | flops 2097152 | bytes 2097152 | tf_op jit(solution)/shard_map/edge_sums/pallas_call | solution.py:82
  215.1 34.9 %all_to_all.40 = bf16[16,288,128]{2,1,0:T(8,128)(2,1)S(1)} all-to-all(bf16[16,288,128]{2,1,0:T(8,128)(2,1)S(1)} %pad_maximum_fusion), channel_id=1, replica_groups=mesh['dom'=32,'member'=16] {'member'}, dimensions={0} | all-to-all | bytes 2359296 | tf_op jit(solution)/shard_map/all_to_all | solution.py:148
  251.5 6.1 %all-to-all-start.7 = ((bf16[32,20,256]{2,1,0:T(8,128)(2,1)}), bf16[32,20,256]{2,1,0:T(8,128)(2,1)S(1)}, u32[]{:S(2)}, u32[]{:S(2)}) async-start(bf16[32,20,256]{2,1,0:T(8,128)(2,1)} %pad_maximum_fusion.1), calls=%async_computation.7 | async-start | bytes 786432 | tf_op jit(solution)/shard_map/all_to_all | solution.py:135
  258.6 12.1 %all-to-all-done.7 = bf16[32,20,256]{2,1,0:T(8,128)(2,1)S(1)} async-done(((bf16[32,20,256]{2,1,0:T(8,128)(2,1)}), bf16[32,20,256]{2,1,0:T(8,128)(2,1)S(1)}, u32[]{:S(2)}, u32[]{:S(2)}) %all-to-all-start.7) | async-done | bytes 327712 | tf_op jit(solution)/shard_map/all_to_all | solution.py:135
  (85 shorter events, 15.6 us)
Async XLA Ops:
  0.6 144.8 %copy-start = (bf16[256,256]{1,0:T(8,128)(2,1)S(1)}, bf16[256,256]{1,0:T(8,128)(2,1)}, u32[]{:S(2)}) copy-start(bf16[256,256]{1,0:T(8,128)(2,1)} %param.17) | copy-start | bytes 393220
  1.4 19.0 %collective-permute-start = (s32[1,4096]{1,0:T(1,128)S(1)}, s32[1,4096]{1,0:T(1,128)S(1)}, u32[]{:S(2)}, u32[]{:S(2)}) collective-permute-start(s32[1,4096]{1,0:T(1,128)S(1)} %fusion.45), channel_id=1, source_target_pairs={{0,1},{1,0},{2,3},{3,2},{4,5},{5,4},{6,7},{7,6},{8,9},{9,8},{10,11... | collective-permute-start | bytes 49160 | tf_op jit(solution)/shard_map/ppermute | solution.py:165
  12.9 18.7 %all-to-all-start = ((bf16[32,4,256]{2,1,0:T(4,128)(2,1)}), bf16[32,4,256]{2,1,0:T(4,128)(2,1)S(1)}, u32[]{:S(2)}, u32[]{:S(2)}) async-start(bf16[32,4,256]{2,1,0:T(4,128)(2,1)} %reshape.233), calls=%async_computation | async-start | bytes 131072 | tf_op jit(solution)/shard_map/all_to_all | solution.py:135
  20.5 5.0 %collective-permute-start.1 = (s32[2,4096]{1,0:T(2,128)S(1)}, s32[2,4096]{1,0:T(2,128)S(1)}, u32[]{:S(2)}, u32[]{:S(2)}) collective-permute-start(s32[2,4096]{1,0:T(2,128)S(1)} %pad_add_fusion.3), channel_id=1, source_target_pairs={{0,2},{1,3},{2,0},{3,1},{4,6},{5,7},{6,4},{7,5},{8,10},{9,11},{10,... | collective-permute-start | bytes 98312 | tf_op jit(solution)/shard_map/ppermute | solution.py:165
  25.6 5.9 %collective-permute-start.2 = (s32[4,4096]{1,0:T(4,128)S(1)}, s32[4,4096]{1,0:T(4,128)S(1)}, u32[]{:S(2)}, u32[]{:S(2)}) collective-permute-start(s32[4,4096]{1,0:T(4,128)S(1)} %pad_add_fusion.2), channel_id=1, source_target_pairs={{0,4},{1,5},{2,6},{3,7},{4,0},{5,1},{6,2},{7,3},{8,12},{9,13},{10,... | collective-permute-start | bytes 196616 | tf_op jit(solution)/shard_map/ppermute | solution.py:165
  33.8 44.2 %all-to-all-start.1 = ((bf16[16,256,128]{2,1,0:T(8,128)(2,1)}), bf16[16,256,128]{2,1,0:T(8,128)(2,1)S(1)}, u32[]{:S(2)}, u32[]{:S(2)}) async-start(bf16[16,256,128]{2,1,0:T(8,128)(2,1)} %bitcast.7), calls=%async_computation.1 | async-start | bytes 2097152 | tf_op jit(solution)/shard_map/all_to_all | solution.py:148
  43.9 31.7 %collective-permute-start.3 = (s32[8,4096]{1,0:T(8,128)S(1)}, s32[8,4096]{1,0:T(8,128)S(1)}, u32[]{:S(2)}, u32[]{:S(2)}) collective-permute-start(s32[8,4096]{1,0:T(8,128)S(1)} %pad_add_fusion.1), channel_id=1, source_target_pairs={{0,8},{1,9},{2,10},{3,11},{4,12},{5,13},{6,14},{7,15},{8,0},{9,1},... | collective-permute-start | bytes 393224 | tf_op jit(solution)/shard_map/ppermute | solution.py:165
  78.0 19.4 %copy-start.1 = (bf16[256,256]{1,0:T(8,128)(2,1)S(1)}, bf16[256,256]{1,0:T(8,128)(2,1)}, u32[]{:S(2)}) copy-start(bf16[256,256]{1,0:T(8,128)(2,1)} %param.9) | copy-start | bytes 393220
  78.0 19.3 %copy-start.2 = (bf16[256,256]{1,0:T(8,128)(2,1)S(1)}, bf16[256,256]{1,0:T(8,128)(2,1)}, u32[]{:S(2)}) copy-start(bf16[256,256]{1,0:T(8,128)(2,1)} %param.16) | copy-start | bytes 393220
  91.8 33.5 %all-to-all-start.2 = ((bf16[16,256,128]{2,1,0:T(8,128)(2,1)}), bf16[16,256,128]{2,1,0:T(8,128)(2,1)S(1)}, u32[]{:S(2)}, u32[]{:S(2)}) async-start(bf16[16,256,128]{2,1,0:T(8,128)(2,1)} %bitcast.9), calls=%async_computation.2 | async-start | bytes 2097152 | tf_op jit(solution)/shard_map/all_to_all | solution.py:148
  125.5 10.4 %copy-start.3 = (s32[1,1,256]{2,1,0:T(1,128)S(1)}, s32[1,1,256]{2,1,0:T(1,128)}, u32[]{:S(2)}) copy-start(s32[1,1,256]{2,1,0:T(1,128)} %param.15) | copy-start | bytes 3076
  125.5 19.9 %copy-start.4 = (bf16[256,256]{1,0:T(8,128)(2,1)S(1)}, bf16[256,256]{1,0:T(8,128)(2,1)}, u32[]{:S(2)}) copy-start(bf16[256,256]{1,0:T(8,128)(2,1)} %param.10) | copy-start | bytes 393220
  126.5 18.5 %all-to-all-start.3 = ((bf16[32,4,256]{2,1,0:T(4,128)(2,1)}), bf16[32,4,256]{2,1,0:T(4,128)(2,1)S(1)}, u32[]{:S(2)}, u32[]{:S(2)}) async-start(bf16[32,4,256]{2,1,0:T(4,128)(2,1)} %reshape.238), calls=%async_computation.3 | async-start | bytes 131072 | tf_op jit(solution)/shard_map/all_to_all | solution.py:135
  147.7 20.4 %all-to-all-start.4 = ((bf16[32,12,512]{2,1,0:T(8,128)(2,1)}), bf16[32,12,512]{2,1,0:T(8,128)(2,1)S(1)}, u32[]{:S(2)}, u32[]{:S(2)}) async-start(bf16[32,12,512]{2,1,0:T(8,128)(2,1)} %maximum_maximum_fusion), calls=%async_computation.4 | async-start | bytes 1048576 | tf_op jit(solution)/shard_map/all_to_all | solution.py:135
  169.6 32.6 %all-to-all-start.5 = ((bf16[16,256,128]{2,1,0:T(8,128)(2,1)}), bf16[16,256,128]{2,1,0:T(8,128)(2,1)S(1)}, u32[]{:S(2)}, u32[]{:S(2)}) async-start(bf16[16,256,128]{2,1,0:T(8,128)(2,1)} %bitcast.18), calls=%async_computation.5 | async-start | bytes 2097152 | tf_op jit(solution)/shard_map/all_to_all | solution.py:148
  251.5 19.2 %all-to-all-start.7 = ((bf16[32,20,256]{2,1,0:T(8,128)(2,1)}), bf16[32,20,256]{2,1,0:T(8,128)(2,1)S(1)}, u32[]{:S(2)}, u32[]{:S(2)}) async-start(bf16[32,20,256]{2,1,0:T(8,128)(2,1)} %pad_maximum_fusion.1), calls=%async_computation.7 | async-start | bytes 786432 | tf_op jit(solution)/shard_map/all_to_all | solution.py:135

commit v4 on v3

--- a/solution.py
+++ b/solution.py
@@ -5,20 +5,37 @@
 from jax import lax
 from jax.experimental import pallas as pl
 from jax.experimental.pallas import tpu as pltpu
-from jax.sharding import PartitionSpec as P
+from jax.sharding import Mesh, PartitionSpec as P
 
 MIRR = 62
 LATE = 64
+FIRST = 128
 UNROLL = 16
 ACCS = 4
-CHUNK = 128
-
-
-def edge_kernel(take_high, bounds_ref, words_ref, table_ref, out_ref, words, table, *rest):
+CHUNK = 64
+
+
+def edge_kernel(
+    take_high,
+    bounds_ref,
+    words_ref,
+    early_ref,
+    late_ref,
+    first_out,
+    last_out,
+    words,
+    table,
+    *rest,
+):
     accs, sems = rest[:-1], rest[-1]
-    rows, width = table_ref.shape
+    lists = sems.shape[0]
+    width = late_ref.shape[1]
+    early, late = early_ref.shape[0] // lists, late_ref.shape[0] // lists
+    first = first_out.shape[0] // lists
+    last = early + late - first
+    rows = lists * (early + late)
     pad = table.shape[0] - rows
-    lists = sems.shape[0]
+    column = pl.multiple_of(bounds_ref[2, 0] * width, width)
     length = words.shape[0] // lists
 
     def copy(m):
@@ -31,14 +48,28 @@
         def _():
             copy(m).start()
 
-    def load(i, _):
-        span = pl.ds(pl.multiple_of(i * CHUNK, CHUNK), CHUNK)
-        table[span, :] = table_ref[span, :].astype(jnp.float32)
-        for acc in accs:
-            acc[span, :] = jnp.zeros((CHUNK, width), jnp.float32)
+    def load(m, _):
+        def put(target, count, source):
+            for at in range(0, count, CHUNK):
+                span = pl.ds(pl.multiple_of(target + at, CHUNK), CHUNK)
+                table[span, :] = source(at).astype(jnp.float32)
+                for acc in accs:
+                    acc[span, :] = jnp.zeros((CHUNK, width), jnp.float32)
+
+        def from_early(at):
+            return early_ref[
+                pl.ds(pl.multiple_of(m * early + at, CHUNK), CHUNK), pl.ds(column, width)
+            ]
+
+        def from_late(at):
+            return late_ref[pl.ds(pl.multiple_of(m * late + at, CHUNK), CHUNK), :]
+
+        put(m * first, first, from_early)
+        put(lists * first + m * last, early - first, lambda at: from_early(first + at))
+        put(lists * first + m * last + early - first, late, from_late)
         return 0
 
-    lax.fori_loop(0, rows // CHUNK, load, 0)
+    lax.fori_loop(0, lists, load, 0)
     table[pl.ds(rows, pad), :] = jnp.zeros((pad, width), jnp.float32)
 
     one_row = (rows + pad, 1, width)
@@ -64,30 +95,34 @@
             copy(m).wait()
             lax.fori_loop(bounds_ref[0, m], bounds_ref[1, m], step, 0)
 
-    def store(i, _):
-        span = pl.ds(pl.multiple_of(i * CHUNK, CHUNK), CHUNK)
-        total = accs[0][span, :]
-        for acc in accs[1:]:
-            total = total + acc[span, :]
-        out_ref[span, :] = total.astype(out_ref.dtype)
-        return 0
-
-    lax.fori_loop(0, rows // CHUNK, store, 0)
-
-
-def edge_sums(take_high, bounds, words, table):
-    rows, width = table.shape
-    lists = bounds.shape[1]
+    def store(ref, base):
+        def step(i, _):
+            at = pl.multiple_of(i * CHUNK, CHUNK)
+            total = accs[0][pl.ds(base + at, CHUNK), :]
+            for acc in accs[1:]:
+                total = total + acc[pl.ds(base + at, CHUNK), :]
+            ref[pl.ds(at, CHUNK), :] = total.astype(ref.dtype)
+            return 0
+
+        lax.fori_loop(0, ref.shape[0] // CHUNK, step, 0)
+
+    store(first_out, 0)
+    store(last_out, first_out.shape[0])
+
+
+def edge_sums(take_high, bounds, words, early, late):
+    lists, width = bounds.shape[1], late.shape[1]
+    rows = early.shape[0] + late.shape[0]
+    smem = pl.BlockSpec(memory_space=pltpu.SMEM)
     vmem = pl.BlockSpec(memory_space=pltpu.VMEM)
     return pl.pallas_call(
         functools.partial(edge_kernel, take_high),
-        out_shape=jax.ShapeDtypeStruct((rows, width), jnp.bfloat16),
-        in_specs=[
-            pl.BlockSpec(memory_space=pltpu.SMEM),
-            pl.BlockSpec(memory_space=pl.ANY),
-            vmem,
-        ],
-        out_specs=vmem,
+        out_shape=(
+            jax.ShapeDtypeStruct((lists * FIRST, width), jnp.bfloat16),
+            jax.ShapeDtypeStruct((rows - lists * FIRST, width), jnp.bfloat16),
+        ),
+        in_specs=[smem, pl.BlockSpec(memory_space=pl.ANY), vmem, vmem],
+        out_specs=(vmem, vmem),
         scratch_shapes=[pltpu.SMEM(words.shape, jnp.int32)]
         + [pltpu.VMEM((rows + 8, width), jnp.float32)] * (1 + ACCS)
         + [pltpu.SemaphoreType.DMA((lists,))],
@@ -96,7 +131,7 @@
             flops=16384 * width, bytes_accessed=4 * rows * width, transcendentals=0
         ),
         name="edge_sums",
-    )(bounds, words, table)
+    )(bounds, words, early, late)
 
 
 def body(
@@ -114,7 +149,10 @@
     half = width // 2
     early = rows - LATE
     dom_count = lax.axis_size("dom")
-    members = lax.axis_size("member")
+    member = ("y", "core")
+    chips = lax.axis_size("y")
+    members = 2 * chips
+    core = lax.axis_index("core")
     part_rows = rows * members
     contract_first = (((0,), (0,)), ((), ()))
     f32, bf16 = jnp.float32, jnp.bfloat16
@@ -145,26 +183,53 @@
         return jnp.where(late_mirror, arrived.astype(bf16), values[early:])
 
     def over_member(blocks):
-        return lax.all_to_all(blocks, "member", split_axis=0, concat_axis=0, tiled=True)
+        return lax.all_to_all(blocks, member, split_axis=0, concat_axis=0, tiled=True)
 
     def gather(values):
         halves = jnp.stack([values[:, :half], values[:, half:]])
         every = jnp.broadcast_to(halves[None], (members // 2,) + halves.shape)
-        return over_member(every.reshape(members, rows, half)).reshape(-1, half)
+        return over_member(every.reshape(members, -1, half)).reshape(-1, half)
+
+    def twin(values):
+        return lax.ppermute(values, "core", [(0, 1), (1, 0)])
+
+    def whole_rows(block):
+        count = block.shape[0] // 2
+        mine = lax.dynamic_slice_in_dim(block, core * count, count, 0)
+        other = twin(lax.dynamic_slice_in_dim(block, (1 - core) * count, count, 0))
+        return jnp.where(
+            core == 0,
+            jnp.concatenate([mine, other], axis=1),
+            jnp.concatenate([other, mine], axis=1),
+        )
 
     def member_sum(arrived):
         by_core = arrived.reshape((members // 2, 2) + arrived.shape[1:]).astype(f32)
         return jnp.concatenate([jnp.sum(by_core[:, core], axis=0) for core in (0, 1)], axis=1)
 
     src, dst = edge_src.reshape(-1), edge_dst.reshape(-1)
-    words = jnp.where(src >= 0, (dst << 16) | src, (part_rows << 16) | part_rows)
+    def table_row(row):
+        at, within = row // rows, row % rows
+        return jnp.where(
+            within < FIRST,
+            at * FIRST + within,
+            members * FIRST + at * (rows - FIRST) + within - FIRST,
+        )
+
+    words = jnp.where(
+        src >= 0, (table_row(dst) << 16) | table_row(src), (part_rows << 16) | part_rows
+    )
+    chip = lax.axis_index("y")
+
+    def both(mine, theirs, low):
+        return jnp.concatenate([jnp.where(low, mine, theirs), jnp.where(low, theirs, mine)])
+
     mine = words.reshape(1, -1)
-    index = lax.axis_index("member")
+    mine = both(mine, twin(mine), core == 0)
     bit = 1
-    while bit < members:
-        theirs = lax.ppermute(mine, "member", [(m, m ^ bit) for m in range(members)])
-        low = (index & bit) == 0
-        mine = jnp.concatenate([jnp.where(low, mine, theirs), jnp.where(low, theirs, mine)])
+    while bit < chips:
+        theirs = lax.ppermute(mine, "y", [(y, y ^ bit) for y in range(chips)])
+        mine = both(mine, theirs, (chip & bit) == 0)
         bit *= 2
     blocks = jnp.sum((mine < (part_rows << 16)).astype(jnp.int32), axis=1)
     blocks = (blocks + UNROLL - 1) // UNROLL
@@ -178,26 +243,28 @@
         axis=1,
     )
     total = jnp.sum(blocks)
-    chips = members // 2
-    chip = index >> 1
     bounds = jnp.stack(
         [jnp.clip(lax.div(total * at, chips) - before, 0, blocks) for at in (chip, chip + 1)]
+        + [jnp.broadcast_to(core, blocks.shape)]
     )
     words = mine.reshape(-1)
 
-    def partition_sums(table, take_high, weight_sum=None):
-        part = edge_sums(take_high, bounds, words, table).reshape(members, rows, half)
+    def partition_sums(early_table, late_table, take_high, weight_sum=None):
+        first, part = edge_sums(take_high, bounds, words, early_table, late_table)
+        first_block = lax.psum_scatter(first, "y", scatter_dimension=0, tiled=True)
+        part = part.reshape(members, -1, half)
+        last = part.shape[1]
         if weight_sum is not None:
             share = weight_sum.astype(bf16).reshape(-1, half)
             share = jnp.broadcast_to(share[None], (members,) + share.shape)
             part = jnp.concatenate([part, share], axis=1)
         arrived = over_member(part)
-        totals = member_sum(arrived[:, :rows])
-        slots = jnp.dot(pick_send, totals[early:].astype(bf16), preferred_element_type=f32)
+        last_total = member_sum(arrived[:, :last])
+        slots = jnp.dot(pick_send, last_total[-LATE:].astype(bf16), preferred_element_type=f32)
         slots = slots.astype(bf16).reshape(dom_count, -1, width)
         weight_sums = None
         if weight_sum is not None:
-            share = jnp.sum(arrived[:, rows:].astype(f32), axis=0).astype(bf16)
+            share = jnp.sum(arrived[:, last:].astype(f32), axis=0).astype(bf16)
             share = share.reshape(-1, width)
             share = jnp.broadcast_to(share[None], (dom_count,) + share.shape)
             slots = jnp.concatenate([slots, share], axis=1)
@@ -210,11 +277,13 @@
             contract_first,
             preferred_element_type=f32,
         )
+        from_mirrors, first_block = lax.optimization_barrier((from_mirrors, first_block))
+        totals = jnp.concatenate([whole_rows(first_block), last_total], axis=0)
         return totals + from_mirrors, weight_sums
 
+    early_table = lax.all_gather(features[:early], member, axis=0, tiled=True)
     late_rows = at_mirrors(over_dom(from_masters(features)), features)
-    table = gather(jnp.concatenate([features[:early], late_rows], axis=0))
-    totals, _ = partition_sums(table, False)
+    totals, _ = partition_sums(early_table, gather(late_rows), False)
     averaged = (totals / denominator).astype(bf16)
 
     pre = jnp.dot(features, weight_self, preferred_element_type=f32) + jnp.dot(
@@ -227,6 +296,7 @@
     grad_mean = (
         jnp.dot(grad_pre, weight_neigh.T, preferred_element_type=f32) / denominator
     ).astype(bf16)
+    early_table = lax.all_gather(grad_mean[:early], member, axis=0, tiled=True)
     local_self = lax.dot_general(features, grad_pre, contract_first, preferred_element_type=f32)
     local_neigh = lax.dot_general(averaged, grad_pre, contract_first, preferred_element_type=f32)
     self_term = jnp.dot(grad_pre, weight_self.T, preferred_element_type=f32)
@@ -237,32 +307,38 @@
     moved = over_dom(jnp.concatenate([slots, share], axis=1))
     arrived = moved[:, :cap]
     late_rows = at_mirrors(arrived[:, :, :width], grad_mean)
-    table = gather(jnp.concatenate([grad_mean[:early], late_rows], axis=0))
+    late_table = gather(late_rows)
     activated_late = at_mirrors(arrived[:, :, width:], activated)
     activated = jnp.concatenate([activated[:early], activated_late], axis=0)
 
     weight_sum = jnp.sum(moved[:, cap:].astype(f32), axis=0)
-    back_sum, weight_sums = partition_sums(table, True, weight_sum)
+    back_sum, weight_sums = partition_sums(early_table, late_table, True, weight_sum)
     grad_features = jnp.where(is_mirror, 0.0, back_sum + self_term).astype(bf16)
     return activated, grad_features, weight_sums[:, :width], weight_sums[:, width:]
 
 
 def solution(mesh):
+    devices = mesh.devices
+    split = Mesh(
+        devices.reshape(devices.shape[0], devices.shape[1] // 2, 2), ("dom", "y", "core")
+    )
+    every = ("dom", "y", "core")
+    member = ("y", "core")
     placed = (
-        P(("dom", "member"), None),
-        P(("dom", "member"), None),
-        P("dom", "member", None),
-        P("dom", "member", None),
-        P("dom", "member", None, None),
-        P("dom", "member", None, None),
-        P("dom", "member", None),
+        P(every, None),
+        P(every, None),
+        P("dom", member, None),
+        P("dom", member, None),
+        P("dom", member, None, None),
+        P("dom", member, None, None),
+        P("dom", member, None),
         P(),
         P(),
     )
     return jax.shard_map(
         body,
-        mesh=mesh,
+        mesh=split,
         in_specs=placed,
-        out_specs=(P(("dom", "member"), None), P(("dom", "member"), None), P(), P()),
+        out_specs=(P(every, None), P(every, None), P(), P()),
         check_vma=False,
     )

time: 275 us -> 294 us (1.069)
  waiting for transfers between devices: 119 us -> 95.4 us
  starting transfers between devices: 70.5 us -> 85.6 us
  between operations: 2.5 us -> 15.6 us
  blocking collectives: 34.9 us -> 47.2 us
  local copies, waits for them, and re-layouts: 7.69 us -> 12.6 us
    ppermute x4 -> x6, waiting for transfers between devices: 26.2 us -> 3.29 us  [the longest x3 2.45 us: body(): theirs = lax.ppermute(mine, 'y', [(y, y ^ bit) for y in range(chips)])]
    reduce_scatter x0 -> x2, waiting for transfers between devices: none -> 22.9 us  [partition_sums(): first_block = lax.psum_scatter(first, 'y', scatter_dimension=0, tiled=True)]
    all_to_all x4 -> x3, waiting for transfers between devices: 37.7 us -> 20.6 us  [over_dom(): return lax.all_to_all(slots, 'dom', split_axis=0, concat_axis=0, tiled=True)]
    all_to_all x3, waiting for transfers between devices: 55.5 us -> 39.4 us  [over_member(): lax.all_to_all(blocks, member, split_axis=0, concat_axis=0, tiled=True)]
    ppermute x4 -> x6, starting transfers between devices: 23.4 us -> 39.3 us  [the longest x3 23.7 us: twin(): return lax.ppermute(values, 'core', [(0, 1), (1, 0)])]
    all_to_all x1 -> x2, blocking collectives: 34.9 us -> 47.2 us  [the longest x1 23.8 us: over_dom(): return lax.all_to_all(slots, 'dom', split_axis=0, concat_axis=0, tiled=True)]
    all_gather x0 -> x2, waiting for transfers between devices: none -> 8.25 us  [the longest x1 8.25 us: body(): early_table = lax.all_gather(features[:early], member, axis=0, tiled=True)]
    all_to_all x4 -> x3, starting transfers between devices: 26.9 us -> 27.5 us  [over_dom(): return lax.all_to_all(slots, 'dom', split_axis=0, concat_axis=0, tiled=True)]
  transfers between devices with their start and end apart: 11 -> 16, of which waited for: 7 -> 11; matrix products, arithmetic and copies ran while one was open for 3% -> 5% of each run, Pallas kernels for 0% -> 0%
where the time goes in v4:
time: 294 us; the launch traced here: 293 us
  waiting for transfers between devices  95.4 us (32%)
  starting transfers between devices  85.6 us (29%)
  blocking collectives  47.2 us (16%)
  Pallas kernels  26.9 us (9%)
  between operations  15.6 us (5%)
  local copies, waits for them, and re-layouts  12.6 us (4%)
  matrix products  5.17 us (2%)
  other arithmetic  4.76 us (2%)
    all_to_all x3, waiting for transfers between devices, over_member(): lax.all_to_all(blocks, member, split_axis=0, concat_axis=0, tiled=True)  39.4 us
    all_to_all x3, starting transfers between devices, over_dom(): return lax.all_to_all(slots, 'dom', split_axis=0, concat_axis=0, tiled=True)  27.5 us
    pallas_call x2, Pallas kernels, edge_sums(): pl.pallas_call(functools.partial(edge_kernel, take_high), out_shape=(jax....  26.9 us
    all_to_all x1, blocking collectives, over_dom(): return lax.all_to_all(slots, 'dom', split_axis=0, concat_axis=0, tiled=True)  23.8 us
    ppermute x3, starting transfers between devices, twin(): return lax.ppermute(values, 'core', [(0, 1), (1, 0)])  23.7 us
    all_to_all x1, blocking collectives, over_member(): lax.all_to_all(blocks, member, split_axis=0, concat_axis=0, tiled=True)  23.4 us
    reduce_scatter x2, waiting for transfers between devices, partition_sums(): first_block = lax.psum_scatter(first, 'y', scatter_dimension=0, tiled=True)  22.9 us
    all_to_all x3, waiting for transfers between devices, over_dom(): return lax.all_to_all(slots, 'dom', split_axis=0, concat_axis=0, tiled=True)  20.6 us
  transfers between devices with their start and end apart: 16, of which 11 were waited for; matrix products, arithmetic and copies ran while one was open for 5% of the time, Pallas kernels for 0%

profile of v4, /device:TPU:1, one launch (start us, length us, event | category | flops | bytes accessed | tf_op | source)
XLA Modules:
  0.0 293.2 jit_solution(15484894236794764575)
XLA Ops:
  8.3 8.8 %collective-permute-start = (s32[1,4096]{1,0:T(1,128)S(1)}, s32[1,4096]{1,0:T(1,128)S(1)}, u32[]{:S(2)}, u32[]{:S(2)}) collective-permute-start(s32[1,4096]{1,0:T(1,128)S(1)} %compare_select_fusion.2), channel_id=1, source_target_pairs={{0,1},{1,0},{2,3},{3,2},{4,5},{5,4},{6,7},{7,6},{8,9},{9,8},{10,11... | collective-permute-start | bytes 49160 | tf_op jit(solution)/shard_map/ppermute | solution.py:194
  19.7 7.5 %all-to-all-start = ((bf16[32,4,256]{2,1,0:T(4,128)(2,1)}), bf16[32,4,256]{2,1,0:T(4,128)(2,1)S(1)}, u32[]{:S(2)}, u32[]{:S(2)}) async-start(bf16[32,4,256]{2,1,0:T(4,128)(2,1)} %reshape.450), calls=%async_computation | async-start | bytes 131072 | tf_op jit(solution)/shard_map/all_to_all | solution.py:173
  28.9 3.2 %collective-permute-start.1 = (s32[2,4096]{1,0:T(2,128)S(1)}, s32[2,4096]{1,0:T(2,128)S(1)}, u32[]{:S(2)}, u32[]{:S(2)}) collective-permute-start(s32[2,4096]{1,0:T(2,128)S(1)} %pad_add_fusion.3), channel_id=1, source_target_pairs={{0,2},{2,0},{4,6},{6,4},{8,10},{10,8},{12,14},{14,12},{1,3},{3,1},... | collective-permute-start | bytes 98312 | tf_op jit(solution)/shard_map/ppermute | solution.py:231
  34.0 4.2 %collective-permute-start.2 = (s32[4,4096]{1,0:T(4,128)S(1)}, s32[4,4096]{1,0:T(4,128)S(1)}, u32[]{:S(2)}, u32[]{:S(2)}) collective-permute-start(s32[4,4096]{1,0:T(4,128)S(1)} %pad_add_fusion.2), channel_id=1, source_target_pairs={{0,4},{2,6},{4,0},{6,2},{8,12},{10,14},{12,8},{14,10},{1,5},{3,7},... | collective-permute-start | bytes 196616 | tf_op jit(solution)/shard_map/ppermute | solution.py:231
  40.0 8.2 %collective-permute-start.3 = (s32[8,4096]{1,0:T(8,128)S(1)}, s32[8,4096]{1,0:T(8,128)S(1)}, u32[]{:S(2)}, u32[]{:S(2)}) collective-permute-start(s32[8,4096]{1,0:T(8,128)S(1)} %pad_add_fusion.1), channel_id=1, source_target_pairs={{0,8},{2,10},{4,12},{6,14},{8,0},{10,2},{12,4},{14,6},{1,9},{3,11}... | collective-permute-start | bytes 393224 | tf_op jit(solution)/shard_map/ppermute | solution.py:231
  49.2 5.9 %all-to-all-start.1 = ((bf16[16,64,128]{2,1,0:T(8,128)(2,1)}), bf16[16,64,128]{2,1,0:T(8,128)(2,1)S(1)}, u32[]{:S(2)}, u32[]{:S(2)}) async-start(bf16[16,64,128]{2,1,0:T(8,128)(2,1)} %bitcast.8), calls=%async_computation.1 | async-start | bytes 524288 | tf_op jit(solution)/shard_map/all_to_all | solution.py:186
  57.6 11.5 %all-to-all-done.1 = bf16[16,64,128]{2,1,0:T(8,128)(2,1)S(1)} async-done(((bf16[16,64,128]{2,1,0:T(8,128)(2,1)}), bf16[16,64,128]{2,1,0:T(8,128)(2,1)S(1)}, u32[]{:S(2)}, u32[]{:S(2)}) %all-to-all-start.1) | async-done | bytes 262176 | tf_op jit(solution)/shard_map/all_to_all | solution.py:186
  69.1 8.2 %all-gather.3.cloned.1.call-done.early_ref = bf16[3072,256]{1,0:T(8,128)(2,1)} async-done(((bf16[192,256]{1,0:T(8,128)(2,1)}), bf16[3072,256]{1,0:T(8,128)(2,1)}) %all-gather.3.cloned.1.call-update) | async-done | bytes 1572880 | tf_op jit(solution)/shard_map/all_gather | solution.py:284
  78.7 13.5 %edge_sums.2 = (bf16[2048,128]{1,0:T(8,128)(2,1)}, bf16[2048,128]{1,0:T(8,128)(2,1)}) custom-call(s32[3,16]{1,0:T(4,128)S(1)} %add_add_fusion.bounds_ref, s32[65536]{0:T(1024)S(1)} %bitcast.100, bf16[3072,256]{1,0:T(8,128)(2,1)S(1)} %copy-done.1, bf16[1024,128]{1,0:T(8,128)(2,1)S(1)} %bitcast.102), custom_call_target="tpu_custom_call" | custom-call | flops 2097152 | bytes 2097152 | tf_op jit(solution)/shard_map/edge_sums/pallas_call | solution.py:118
  92.2 4.5 %all-to-all-start.2 = ((bf16[16,128,128]{2,1,0:T(8,128)(2,1)}), bf16[16,128,128]{2,1,0:T(8,128)(2,1)S(1)}, u32[]{:S(2)}, u32[]{:S(2)}) async-start(bf16[16,128,128]{2,1,0:T(8,128)(2,1)} %bitcast.10), calls=%async_computation.2 | async-start | bytes 1048576 | tf_op jit(solution)/shard_map/all_to_all | solution.py:186
  97.5 16.6 %all-to-all-done.2 = bf16[16,128,128]{2,1,0:T(8,128)(2,1)S(1)} async-done(((bf16[16,128,128]{2,1,0:T(8,128)(2,1)}), bf16[16,128,128]{2,1,0:T(8,128)(2,1)S(1)}, u32[]{:S(2)}, u32[]{:S(2)}) %all-to-all-start.2) | async-done | bytes 524320 | tf_op jit(solution)/shard_map/all_to_all | solution.py:186
  115.1 11.0 %all-to-all-start.3 = ((bf16[32,4,256]{2,1,0:T(4,128)(2,1)}), bf16[32,4,256]{2,1,0:T(4,128)(2,1)S(1)}, u32[]{:S(2)}, u32[]{:S(2)}) async-start(bf16[32,4,256]{2,1,0:T(4,128)(2,1)} %reshape.455), calls=%async_computation.3 | async-start | bytes 131072 | tf_op jit(solution)/shard_map/all_to_all | solution.py:173
  126.2 9.1 %all-to-all-done.3 = bf16[32,4,256]{2,1,0:T(4,128)(2,1)S(1)} async-done(((bf16[32,4,256]{2,1,0:T(4,128)(2,1)}), bf16[32,4,256]{2,1,0:T(4,128)(2,1)S(1)}, u32[]{:S(2)}, u32[]{:S(2)}) %all-to-all-start.3) | async-done | bytes 65568 | tf_op jit(solution)/shard_map/all_to_all | solution.py:173
  135.6 1.7 reduce-scatter.3.cloned.1.call-done
  138.1 7.5 %collective-permute-start.4 = (bf16[128,128]{1,0:T(8,128)(2,1)S(1)}, bf16[128,128]{1,0:T(8,128)(2,1)S(1)}, u32[]{:S(2)}, u32[]{:S(2)}) collective-permute-start(bf16[128,128]{1,0:T(8,128)(2,1)S(1)} %get-tuple-element.41), channel_id=1, source_target_pairs={{0,1},{1,0},{2,3},{3,2},{4,5},{5,4},{6,7},{7,6},{8,9},{9,8},{10,11... | collective-permute-start | bytes 98312 | tf_op jit(solution)/shard_map/ppermute | solution.py:194
  148.8 23.8 %all_to_all.40 = bf16[32,12,512]{2,1,0:T(8,128)(2,1)S(1)} all-to-all(bf16[32,12,512]{2,1,0:T(8,128)(2,1)S(1)} %maximum_maximum_fusion), channel_id=1, replica_groups=mesh['dom'=32,'y'=8,'core'=2] {'dom'}, dimensions={0} | all-to-all | bytes 786432 | tf_op jit(solution)/shard_map/all_to_all | solution.py:173
  173.6 8.2 %all-to-all-start.5 = ((bf16[16,64,128]{2,1,0:T(8,128)(2,1)}), bf16[16,64,128]{2,1,0:T(8,128)(2,1)S(1)}, u32[]{:S(2)}, u32[]{:S(2)}) async-start(bf16[16,64,128]{2,1,0:T(8,128)(2,1)} %bitcast.19), calls=%async_computation.6 | async-start | bytes 524288 | tf_op jit(solution)/shard_map/all_to_all | solution.py:186
  181.9 11.3 %all-to-all-done.5 = bf16[16,64,128]{2,1,0:T(8,128)(2,1)S(1)} async-done(((bf16[16,64,128]{2,1,0:T(8,128)(2,1)}), bf16[16,64,128]{2,1,0:T(8,128)(2,1)S(1)}, u32[]{:S(2)}, u32[]{:S(2)}) %all-to-all-start.5) | async-done | bytes 262176 | tf_op jit(solution)/shard_map/all_to_all | solution.py:186
  194.7 13.3 %edge_sums.3 = (bf16[2048,128]{1,0:T(8,128)(2,1)}, bf16[2048,128]{1,0:T(8,128)(2,1)S(1)}) custom-call(s32[3,16]{1,0:T(4,128)S(1)} %add_add_fusion.bounds_ref, s32[65536]{0:T(1024)S(1)} %bitcast.101, bf16[3072,256]{1,0:T(8,128)(2,1)S(1)} %copy-done.2, bf16[1024,128]{1,0:T(8,128)(2,1)S(1)} %bitcast.103), custom_call_target="tpu_custom_call" | custom-call | flops 2097152 | bytes 2097152 | tf_op jit(solution)/shard_map/edge_sums/pallas_call | solution.py:118
  208.1 23.4 %all_to_all.41 = bf16[16,160,128]{2,1,0:T(8,128)(2,1)S(1)} all-to-all(bf16[16,160,128]{2,1,0:T(8,128)(2,1)S(1)} %pad_maximum_fusion), channel_id=1, replica_groups=mesh['dom'=32,'y'=8,'core'=2] {'y','core'}, dimensions={0} | all-to-all | bytes 1310720 | tf_op jit(solution)/shard_map/all_to_all | solution.py:186
  232.9 8.9 %all-to-all-start.7 = ((bf16[32,20,256]{2,1,0:T(8,128)(2,1)}), bf16[32,20,256]{2,1,0:T(8,128)(2,1)S(1)}, u32[]{:S(2)}, u32[]{:S(2)}) async-start(bf16[32,20,256]{2,1,0:T(8,128)(2,1)} %pad_maximum_fusion.1), calls=%async_computation.8 | async-start | bytes 786432 | tf_op jit(solution)/shard_map/all_to_all | solution.py:173
  243.4 11.5 %all-to-all-done.7 = bf16[32,20,256]{2,1,0:T(8,128)(2,1)S(1)} async-done(((bf16[32,20,256]{2,1,0:T(8,128)(2,1)}), bf16[32,20,256]{2,1,0:T(8,128)(2,1)S(1)}, u32[]{:S(2)}, u32[]{:S(2)}) %all-to-all-start.7) | async-done | bytes 327712 | tf_op jit(solution)/shard_map/all_to_all | solution.py:173
  255.5 21.1 %reduce-scatter.5.cloned.1.call-done = bf16[256,128]{1,0:T(8,128)(2,1)} async-done(((bf16[2048,128]{1,0:T(8,128)(2,1)}), bf16[256,128]{1,0:T(8,128)(2,1)}) %reduce-scatter.5.cloned.1.call-update) | async-done | bytes 65552 | tf_op jit(solution)/shard_map/reduce_scatter | solution.py:254
  277.4 7.5 %collective-permute-start.5 = (bf16[128,128]{1,0:T(8,128)(2,1)S(1)}, bf16[128,128]{1,0:T(8,128)(2,1)S(1)}, u32[]{:S(2)}, u32[]{:S(2)}) collective-permute-start(bf16[128,128]{1,0:T(8,128)(2,1)S(1)} %get-tuple-element.39), channel_id=1, source_target_pairs={{0,1},{1,0},{2,3},{3,2},{4,5},{5,4},{6,7},{7,6},{8,9},{9,8},{10,11... | collective-permute-start | bytes 98312 | tf_op jit(solution)/shard_map/ppermute | solution.py:194
  (110 shorter events, 27.0 us)
Async XLA Ops:
  7.2 139.5 %copy-start = (bf16[256,256]{1,0:T(8,128)(2,1)S(1)}, bf16[256,256]{1,0:T(8,128)(2,1)}, u32[]{:S(2)}) copy-start(bf16[256,256]{1,0:T(8,128)(2,1)} %param.17) | copy-start | bytes 393220
  7.2 41.0 %copy-start.3 = (bf16[256,256]{1,0:T(8,128)(2,1)S(1)}, bf16[256,256]{1,0:T(8,128)(2,1)}, u32[]{:S(2)}) copy-start(bf16[256,256]{1,0:T(8,128)(2,1)} %param.9) | copy-start | bytes 393220
  8.3 20.6 %collective-permute-start = (s32[1,4096]{1,0:T(1,128)S(1)}, s32[1,4096]{1,0:T(1,128)S(1)}, u32[]{:S(2)}, u32[]{:S(2)}) collective-permute-start(s32[1,4096]{1,0:T(1,128)S(1)} %compare_select_fusion.2), channel_id=1, source_target_pairs={{0,1},{1,0},{2,3},{3,2},{4,5},{5,4},{6,7},{7,6},{8,9},{9,8},{10,11... | collective-permute-start | bytes 49160 | tf_op jit(solution)/shard_map/ppermute | solution.py:194
  19.7 28.4 %all-to-all-start = ((bf16[32,4,256]{2,1,0:T(4,128)(2,1)}), bf16[32,4,256]{2,1,0:T(4,128)(2,1)S(1)}, u32[]{:S(2)}, u32[]{:S(2)}) async-start(bf16[32,4,256]{2,1,0:T(4,128)(2,1)} %reshape.450), calls=%async_computation | async-start | bytes 131072 | tf_op jit(solution)/shard_map/all_to_all | solution.py:173
  27.2 50.1 %all-gather.3.cloned.1.call-start = ((), (), s32[]{:S(2)}) async-start(), calls=%async_computation.10 | async-start | bytes 1671168 | tf_op jit(solution)/shard_map/all_gather | solution.py:284
  28.9 5.0 %collective-permute-start.1 = (s32[2,4096]{1,0:T(2,128)S(1)}, s32[2,4096]{1,0:T(2,128)S(1)}, u32[]{:S(2)}, u32[]{:S(2)}) collective-permute-start(s32[2,4096]{1,0:T(2,128)S(1)} %pad_add_fusion.3), channel_id=1, source_target_pairs={{0,2},{2,0},{4,6},{6,4},{8,10},{10,8},{12,14},{14,12},{1,3},{3,1},... | collective-permute-start | bytes 98312 | tf_op jit(solution)/shard_map/ppermute | solution.py:231
  34.0 5.9 %collective-permute-start.2 = (s32[4,4096]{1,0:T(4,128)S(1)}, s32[4,4096]{1,0:T(4,128)S(1)}, u32[]{:S(2)}, u32[]{:S(2)}) collective-permute-start(s32[4,4096]{1,0:T(4,128)S(1)} %pad_add_fusion.2), channel_id=1, source_target_pairs={{0,4},{2,6},{4,0},{6,2},{8,12},{10,14},{12,8},{14,10},{1,5},{3,7},... | collective-permute-start | bytes 196616 | tf_op jit(solution)/shard_map/ppermute | solution.py:231
  40.0 15.2 %collective-permute-start.3 = (s32[8,4096]{1,0:T(8,128)S(1)}, s32[8,4096]{1,0:T(8,128)S(1)}, u32[]{:S(2)}, u32[]{:S(2)}) collective-permute-start(s32[8,4096]{1,0:T(8,128)S(1)} %pad_add_fusion.1), channel_id=1, source_target_pairs={{0,8},{2,10},{4,12},{6,14},{8,0},{10,2},{12,4},{14,6},{1,9},{3,11}... | collective-permute-start | bytes 393224 | tf_op jit(solution)/shard_map/ppermute | solution.py:231
  49.2 19.8 %all-to-all-start.1 = ((bf16[16,64,128]{2,1,0:T(8,128)(2,1)}), bf16[16,64,128]{2,1,0:T(8,128)(2,1)S(1)}, u32[]{:S(2)}, u32[]{:S(2)}) async-start(bf16[16,64,128]{2,1,0:T(8,128)(2,1)} %bitcast.8), calls=%async_computation.1 | async-start | bytes 524288 | tf_op jit(solution)/shard_map/all_to_all | solution.py:186
  77.3 1.4 copy-start.1
  78.7 18.1 %copy-start.4 = (bf16[256,256]{1,0:T(8,128)(2,1)S(1)}, bf16[256,256]{1,0:T(8,128)(2,1)}, u32[]{:S(2)}) copy-start(bf16[256,256]{1,0:T(8,128)(2,1)} %param.16) | copy-start | bytes 393220
  92.2 21.8 %all-to-all-start.2 = ((bf16[16,128,128]{2,1,0:T(8,128)(2,1)}), bf16[16,128,128]{2,1,0:T(8,128)(2,1)S(1)}, u32[]{:S(2)}, u32[]{:S(2)}) async-start(bf16[16,128,128]{2,1,0:T(8,128)(2,1)} %bitcast.10), calls=%async_computation.2 | async-start | bytes 1048576 | tf_op jit(solution)/shard_map/all_to_all | solution.py:186
  96.8 40.6 %reduce-scatter.3.cloned.1.call-start = ((), (), s32[]{:S(2)}) async-start(), calls=%async_computation.11 | async-start | bytes 589824 | tf_op jit(solution)/shard_map/reduce_scatter | solution.py:254
  97.5 28.7 %copy-start.5 = (s32[1,1,256]{2,1,0:T(1,128)S(1)}, s32[1,1,256]{2,1,0:T(1,128)}, u32[]{:S(2)}) copy-start(s32[1,1,256]{2,1,0:T(1,128)} %param.15) | copy-start | bytes 3076
  114.2 32.4 %copy-start.6 = (bf16[256,256]{1,0:T(8,128)(2,1)S(1)}, bf16[256,256]{1,0:T(8,128)(2,1)}, u32[]{:S(2)}) copy-start(bf16[256,256]{1,0:T(8,128)(2,1)} %param.10) | copy-start | bytes 393220
  115.1 20.2 %all-to-all-start.3 = ((bf16[32,4,256]{2,1,0:T(4,128)(2,1)}), bf16[32,4,256]{2,1,0:T(4,128)(2,1)S(1)}, u32[]{:S(2)}, u32[]{:S(2)}) async-start(bf16[32,4,256]{2,1,0:T(4,128)(2,1)} %reshape.455), calls=%async_computation.3 | async-start | bytes 131072 | tf_op jit(solution)/shard_map/all_to_all | solution.py:173
  126.2 67.1 %all-gather.5.cloned.1.call-start = ((), (), s32[]{:S(2)}) async-start(), calls=%async_computation.12 | async-start | bytes 1671168 | tf_op jit(solution)/shard_map/all_gather | solution.py:299
  138.1 8.3 %collective-permute-start.4 = (bf16[128,128]{1,0:T(8,128)(2,1)S(1)}, bf16[128,128]{1,0:T(8,128)(2,1)S(1)}, u32[]{:S(2)}, u32[]{:S(2)}) collective-permute-start(bf16[128,128]{1,0:T(8,128)(2,1)S(1)} %get-tuple-element.41), channel_id=1, source_target_pairs={{0,1},{1,0},{2,3},{3,2},{4,5},{5,4},{6,7},{7,6},{8,9},{9,8},{10,11... | collective-permute-start | bytes 98312 | tf_op jit(solution)/shard_map/ppermute | solution.py:194
  173.6 19.6 %all-to-all-start.5 = ((bf16[16,64,128]{2,1,0:T(8,128)(2,1)}), bf16[16,64,128]{2,1,0:T(8,128)(2,1)S(1)}, u32[]{:S(2)}, u32[]{:S(2)}) async-start(bf16[16,64,128]{2,1,0:T(8,128)(2,1)} %bitcast.19), calls=%async_computation.6 | async-start | bytes 524288 | tf_op jit(solution)/shard_map/all_to_all | solution.py:186
  193.2 1.4 copy-start.2
  232.9 22.0 %all-to-all-start.7 = ((bf16[32,20,256]{2,1,0:T(8,128)(2,1)}), bf16[32,20,256]{2,1,0:T(8,128)(2,1)S(1)}, u32[]{:S(2)}, u32[]{:S(2)}) async-start(bf16[32,20,256]{2,1,0:T(8,128)(2,1)} %pad_maximum_fusion.1), calls=%async_computation.8 | async-start | bytes 786432 | tf_op jit(solution)/shard_map/all_to_all | solution.py:173
  241.9 34.8 %reduce-scatter.5.cloned.1.call-start = ((), (), s32[]{:S(2)}) async-start(), calls=%async_computation.13 | async-start | bytes 589824 | tf_op jit(solution)/shard_map/reduce_scatter | solution.py:254
  277.4 8.3 %collective-permute-start.5 = (bf16[128,128]{1,0:T(8,128)(2,1)S(1)}, bf16[128,128]{1,0:T(8,128)(2,1)S(1)}, u32[]{:S(2)}, u32[]{:S(2)}) collective-permute-start(bf16[128,128]{1,0:T(8,128)(2,1)S(1)} %get-tuple-element.39), channel_id=1, source_target_pairs={{0,1},{1,0},{2,3},{3,2},{4,5},{5,4},{6,7},{7,6},{8,9},{9,8},{10,11... | collective-permute-start | bytes 98312 | tf_op jit(solution)/shard_map/ppermute | solution.py:194
Sparse Core Ops, SparseCore 0:
  30.8 46.4 all-gather.2
  100.4 36.9 reduce-scatter.2
  148.0 41.5 all-gather.4
  245.4 31.1 reduce-scatter.4

commit v5 on v3

v5 whole, which is shorter than its diff:
```python
import jax
import jax.numpy as jnp
from jax import lax
from jax.experimental import pallas as pl
from jax.experimental.pallas import tpu as pltpu
from jax.sharding import Mesh, PartitionSpec as P

MIRR = 62
LATE = 64
UNROLL = 16
ACCS = 8
CHUNK = 128
WINDOW = 1024


def edge_kernel(bounds_ref, words_ref, table_ref, out_ref, words, table, *rest):
    accs, sems = rest[:-1], rest[-1]
    rows, width = table_ref.shape
    own = out_ref.shape[0]
    lists = sems.shape[0]
    length = words.shape[0] // lists

    def windows(m, act):
        def step(at, _):
            span = pl.ds(pl.multiple_of(m * length + at * WINDOW, WINDOW), WINDOW)
            act(pltpu.make_async_copy(words_ref.at[span], words.at[span], sems.at[m]))
            return 0

        last = (bounds_ref[1, m] + (WINDOW - 1)) // WINDOW
        lax.fori_loop(bounds_ref[0, m] // WINDOW, last, step, 0)

    for m in range(lists):
        windows(m, lambda copy: copy.start())

    def load(i, _):
        span = pl.ds(pl.multiple_of(i * CHUNK, CHUNK), CHUNK)
        table[span, :] = table_ref[span, :].astype(jnp.float32)
        return 0

    lax.fori_loop(0, rows // CHUNK, load, 0)

    def clear(i, _):
        span = pl.ds(pl.multiple_of(i * CHUNK, CHUNK), CHUNK)
        for acc in accs:
            acc[span, :] = jnp.zeros((CHUNK, width), jnp.float32)
        return 0

    lax.fori_loop(0, own // CHUNK, clear, 0)

    table_rows = table.reshape((rows, 1, width))
    acc_rows = [acc.reshape((own, 1, width)) for acc in accs]

    def add(base, count):
        takes, places = [], []
        for k in range(count):
            word = words[base + k]
            takes.append(word & 0xFFFF)
            places.append((word >> 16) & (own - 1))
        sums = [acc_rows[k][places[k]] + table_rows[takes[k]] for k in range(count)]
        for k in range(count):
            acc_rows[k][places[k]] = sums[k]

    for m in range(lists):
        windows(m, lambda copy: copy.wait())
        low, high = bounds_ref[0, m], bounds_ref[1, m]
        blocks = (high - low) // UNROLL

        def block(i, _):
            for group in range(UNROLL // ACCS):
                add(m * length + low + i * UNROLL + group * ACCS, ACCS)
            return 0

        def single(i, _):
            add(m * length + i, 1)
            return 0

        lax.fori_loop(0, blocks, block, 0)
        lax.fori_loop(low + blocks * UNROLL, high, single, 0)

    def store(i, _):
        span = pl.ds(pl.multiple_of(i * CHUNK, CHUNK), CHUNK)
        total = accs[0][span, :]
        for acc in accs[1:]:
            total = total + acc[span, :]
        out_ref[span, :] = total
        return 0

    lax.fori_loop(0, own // CHUNK, store, 0)


def edge_sums(bounds, words, table):
    rows, width = table.shape
    lists = bounds.shape[1]
    own = 2 * (rows // lists)
    vmem = pl.BlockSpec(memory_space=pltpu.VMEM)
    return pl.pallas_call(
        edge_kernel,
        out_shape=jax.ShapeDtypeStruct((own, width), jnp.float32),
        in_specs=[
            pl.BlockSpec(memory_space=pltpu.SMEM),
            pl.BlockSpec(memory_space=pl.ANY),
            vmem,
        ],
        out_specs=vmem,
        scratch_shapes=[
            pltpu.SMEM(words.shape, jnp.int32),
            pltpu.VMEM((rows, width), jnp.float32),
        ]
        + [pltpu.VMEM((own, width), jnp.float32)] * ACCS
        + [pltpu.SemaphoreType.DMA((lists,))],
        compiler_params=pltpu.CompilerParams(vmem_limit_bytes=40 * 1024 * 1024),
        cost_estimate=pl.CostEstimate(
            flops=16384 * width, bytes_accessed=4 * rows * width, transcendentals=0
        ),
        name="edge_sums",
    )(bounds, words, table)


def body(
    features,
    cotangent,
    edge_src,
    edge_dst,
    send_rows,
    recv_rows,
    in_degree,
    weight_self,
    weight_neigh,
):
    rows, width = features.shape
    half = width // 2
    early = rows - LATE
    dom_count = lax.axis_size("dom")
    member = ("y", "core")
    chips = lax.axis_size("y")
    members = 2 * chips
    core = lax.axis_index("core")
    chip = lax.axis_index("y")
    part_rows = rows * members
    contract_first = (((0,), (0,)), ((), ()))
    f32, bf16 = jnp.float32, jnp.bfloat16

    send_list = send_rows.reshape(-1)
    recv_list = recv_rows.reshape(-1)
    slot_count = send_list.shape[0]
    cap = slot_count // dom_count
    columns = lax.broadcasted_iota(jnp.int32, (slot_count, rows), 1)
    late_columns = lax.broadcasted_iota(jnp.int32, (slot_count, LATE), 1) + early
    pick_send = (send_list[:, None] == late_columns).astype(bf16)
    pick_recv = (recv_list[:, None] == columns).astype(bf16)
    is_mirror = lax.broadcasted_iota(jnp.int32, (rows, 1), 0) >= rows - MIRR
    late_mirror = is_mirror[early:]
    denominator = in_degree.reshape(-1).astype(f32)[:, None] + 1.0

    def over_dom(slots):
        return lax.all_to_all(slots, "dom", split_axis=0, concat_axis=0, tiled=True)

    def from_masters(values):
        slots = jnp.dot(pick_recv, values, preferred_element_type=f32).astype(bf16)
        return slots.reshape(dom_count, -1, values.shape[1])

    def at_mirrors(slots, values):
        arrived = lax.dot_general(
            pick_send, slots.reshape(slot_count, -1), contract_first, preferred_element_type=f32
        )
        return jnp.where(late_mirror, arrived.astype(bf16), values[early:])

    def over_member(blocks):
        return lax.all_to_all(blocks, member, split_axis=0, concat_axis=0, tiled=True)

    def gather(values):
        halves = jnp.stack([values[:, :half], values[:, half:]])
        every = jnp.broadcast_to(halves[None], (members // 2,) + halves.shape)
        return over_member(every.reshape(members, rows, half)).reshape(-1, half)

    def twin(values):
        return lax.ppermute(values, "core", [(0, 1), (1, 0)])

    def spread(values, combine):
        values = combine(values, twin(values), core == 0)
        bit = 1
        while bit < chips:
            theirs = lax.ppermute(values, "y", [(y, y ^ bit) for y in range(chips)])
            values = combine(values, theirs, (chip & bit) == 0)
            bit *= 2
        return values

    def edge_lists(place, take):
        words = jnp.where(place >= 0, (place << 16) | take, part_rows << 16)
        words = lax.sort(words.reshape(1, -1), dimension=1)
        words = spread(
            words,
            lambda mine, theirs, low: jnp.concatenate(
                [jnp.where(low, mine, theirs), jnp.where(low, theirs, mine)]
            ),
        )
        bounds = jnp.stack(
            [
                jnp.sum((words < (at * (2 * rows) << 16)).astype(jnp.int32), axis=1)
                for at in (chip, chip + 1)
            ]
        )
        return bounds, words.reshape(-1)

    def row_sums(lists, table):
        block = edge_sums(*lists, table)
        mine = lax.dynamic_slice_in_dim(block, core * rows, rows, 0)
        other = lax.dynamic_slice_in_dim(block, (1 - core) * rows, rows, 0)
        other = twin(other.astype(bf16)).astype(f32)
        return jnp.where(
            core == 0,
            jnp.concatenate([mine, other], axis=1),
            jnp.concatenate([other, mine], axis=1),
        )

    def mirror_slots(totals):
        slots = jnp.dot(pick_send, totals[early:].astype(bf16), preferred_element_type=f32)
        return slots.astype(bf16).reshape(dom_count, -1, width)

    def add_at_masters(slots):
        return lax.dot_general(
            pick_recv, slots.reshape(slot_count, width), contract_first, preferred_element_type=f32
        )

    src, dst = edge_src.reshape(-1), edge_dst.reshape(-1)
    slots, src, dst = lax.optimization_barrier((from_masters(features), src, dst))
    lists = edge_lists(dst, src)
    late_rows = at_mirrors(over_dom(slots), features)
    table = gather(jnp.concatenate([features[:early], late_rows], axis=0))
    totals = row_sums(lists, table)
    totals, src, dst = lax.optimization_barrier((totals, src, dst))
    lists = edge_lists(src, dst)
    totals = totals + add_at_masters(over_dom(mirror_slots(totals)))
    averaged = (totals / denominator).astype(bf16)

    pre = jnp.dot(features, weight_self, preferred_element_type=f32) + jnp.dot(
        averaged, weight_neigh, preferred_element_type=f32
    )
    gate_sig = jax.nn.sigmoid(pre)
    activated = (pre * gate_sig).astype(bf16)
    slope = gate_sig * (1.0 + pre * (1.0 - gate_sig))
    grad_pre = jnp.where(is_mirror, 0.0, cotangent.astype(f32) * slope).astype(bf16)
    grad_mean = (
        jnp.dot(grad_pre, weight_neigh.T, preferred_element_type=f32) / denominator
    ).astype(bf16)
    local_self = lax.dot_general(features, grad_pre, contract_first, preferred_element_type=f32)
    local_neigh = lax.dot_general(averaged, grad_pre, contract_first, preferred_element_type=f32)
    self_term = jnp.dot(grad_pre, weight_self.T, preferred_element_type=f32)

    local_weights = jnp.concatenate([local_self, local_neigh], axis=1).astype(bf16)
    share = local_weights.reshape(dom_count, -1, 2 * width)
    slots = from_masters(jnp.concatenate([grad_mean, activated], axis=1))
    moved = over_dom(jnp.concatenate([slots, share], axis=1))
    arrived = moved[:, :cap]
    late_rows = at_mirrors(arrived[:, :, :width], grad_mean)
    table = gather(jnp.concatenate([grad_mean[:early], late_rows], axis=0))
    activated_late = at_mirrors(arrived[:, :, width:], activated)
    activated = jnp.concatenate([activated[:early], activated_late], axis=0)

    weight_sum = spread(
        jnp.sum(moved[:, cap:].astype(f32), axis=0), lambda mine, theirs, low: mine + theirs
    )
    share = weight_sum.astype(bf16).reshape(-1, width)
    share = jnp.broadcast_to(share[None], (dom_count,) + share.shape)
    totals = row_sums(lists, table)
    moved = over_dom(jnp.concatenate([mirror_slots(totals), share], axis=1))
    weight_sums = moved[:, cap:].reshape(-1, 2 * width).astype(f32)
    back_sum = totals + add_at_masters(moved[:, :cap])
    grad_features = jnp.where(is_mirror, 0.0, back_sum + self_term).astype(bf16)
    return activated, grad_features, weight_sums[:, :width], weight_sums[:, width:]


def solution(mesh):
    devices = mesh.devices
    split = Mesh(
        devices.reshape(devices.shape[0], devices.shape[1] // 2, 2), ("dom", "y", "core")
    )
    every = ("dom", "y", "core")
    member = ("y", "core")
    placed = (
        P(every, None),
        P(every, None),
        P("dom", member, None),
        P("dom", member, None),
        P("dom", member, None, None),
        P("dom", member, None, None),
        P("dom", member, None),
        P(),
        P(),
    )
    return jax.shard_map(
        body,
        mesh=split,
        in_specs=placed,
        out_specs=(P(every, None), P(every, None), P(), P()),
        check_vma=False,
    )
```

time: 275 us -> 268 us (0.975)
  waiting for transfers between devices: 119 us -> 79.3 us
  starting transfers between devices: 70.5 us -> 107 us
  blocking collectives: 34.9 us -> 0 us
  local copies, waits for them, and re-layouts: 7.69 us -> 20 us
  between operations: 2.5 us -> 14.8 us
  Pallas kernels: 26.6 us -> 32.9 us
    all_to_all x3 -> x2, waiting for transfers between devices: 55.5 us -> 0.01 us  [over_member(): lax.all_to_all(blocks, member, split_axis=0, concat_axis=0, tiled=True)]
    all_to_all x1 -> x0, blocking collectives: 34.9 us -> none  [over_member(): lax.all_to_all(blocks, 'member', split_axis=0, concat_axis=0, tiled=True)]
    ppermute x4 -> x14, starting transfers between devices: 23.4 us -> 54.9 us  [the longest x9 35.1 us: spread(): theirs = lax.ppermute(values, 'y', [(y, y ^ bit) for y in range(chips)])]
    ppermute x4 -> x14, waiting for transfers between devices: 26.2 us -> 53.1 us  [the longest x9 49.5 us: spread(): theirs = lax.ppermute(values, 'y', [(y, y ^ bit) for y in range(chips)])]
    sort x0 -> x4, local copies, waits for them, and re-layouts: none -> 11.8 us  [edge_lists(): words = lax.sort(words.reshape(1, -1), dimension=1)]
    all_to_all x4, waiting for transfers between devices: 37.7 us -> 26.2 us  [over_dom(): return lax.all_to_all(slots, 'dom', split_axis=0, concat_axis=0, tiled=True)]
    all_to_all x4, starting transfers between devices: 26.9 us -> 35.6 us  [over_dom(): return lax.all_to_all(slots, 'dom', split_axis=0, concat_axis=0, tiled=True)]
    pallas_call x2, Pallas kernels: 26.6 us -> 32.9 us  [edge_sums(): pl.pallas_call(edge_kernel, out_shape=jax.ShapeDtypeStruct((own, width),...]
  transfers between devices with their start and end apart: 11 -> 20, of which waited for: 7 -> 12; matrix products, arithmetic and copies ran while one was open for 3% -> 4% of each run, Pallas kernels for 0% -> 0%
where the time goes in v5:
time: 268 us; the launch traced here: 265 us
  starting transfers between devices  107 us (40%)
  waiting for transfers between devices  79.3 us (30%)
  Pallas kernels  32.9 us (12%)
  local copies, waits for them, and re-layouts  20 us (7%)
  between operations  14.8 us (6%)
  other arithmetic  5.66 us (2%)
  matrix products  5.16 us (2%)
    ppermute x9, waiting for transfers between devices, spread(): theirs = lax.ppermute(values, 'y', [(y, y ^ bit) for y in range(chips)])  49.5 us
    all_to_all x4, starting transfers between devices, over_dom(): return lax.all_to_all(slots, 'dom', split_axis=0, concat_axis=0, tiled=True)  35.6 us
    ppermute x9, starting transfers between devices, spread(): theirs = lax.ppermute(values, 'y', [(y, y ^ bit) for y in range(chips)])  35.1 us
    pallas_call x2, Pallas kernels, edge_sums(): pl.pallas_call(edge_kernel, out_shape=jax.ShapeDtypeStruct((own, width),...  32.9 us
    all_to_all x4, waiting for transfers between devices, over_dom(): return lax.all_to_all(slots, 'dom', split_axis=0, concat_axis=0, tiled=True)  26.2 us
    ppermute x5, starting transfers between devices, twin(): return lax.ppermute(values, 'core', [(0, 1), (1, 0)])  19.8 us
    all_to_all x2, starting transfers between devices, over_member(): lax.all_to_all(blocks, member, split_axis=0, concat_axis=0, tiled=True)  16.7 us
    sort x4, local copies, waits for them, and re-layouts, edge_lists(): words = lax.sort(words.reshape(1, -1), dimension=1)  11.8 us
  transfers between devices with their start and end apart: 20, of which 12 were waited for; matrix products, arithmetic and copies ran while one was open for 4% of the time, Pallas kernels for 0%

profile of v5, /device:TPU:1, one launch (start us, length us, event | category | flops | bytes accessed | tf_op | source)
XLA Modules:
  0.0 265.0 jit_solution(13155108316324964005)
XLA Ops:
  10.6 13.7 %all-to-all-start = ((bf16[32,4,256]{2,1,0:T(4,128)(2,1)}), bf16[32,4,256]{2,1,0:T(4,128)(2,1)S(1)}, u32[]{:S(2)}, u32[]{:S(2)}) async-start(bf16[32,4,256]{2,1,0:T(4,128)(2,1)} %reshape.98), calls=%async_computation | async-start | bytes 131072 | tf_op jit(solution)/shard_map/all_to_all | solution.py:156
  24.5 6.9 %collective-permute-start = (s32[1,4096]{1,0:T(1,128)}, s32[1,4096]{1,0:T(1,128)S(1)}, u32[]{:S(2)}, u32[]{:S(2)}) collective-permute-start(s32[1,4096]{1,0:T(1,128)} %sort.17.cloned.1.call-done), channel_id=1, source_target_pairs={{0,1},{1,0},{2,3},{3,2},{4,5},{5,4},{6,7},{7,6},{8,9},{9,8},{10,11... | collective-permute-start | bytes 49160 | tf_op jit(solution)/shard_map/ppermute | solution.py:177
  42.0 5.7 %all-to-all-start.1 = ((bf16[16,256,128]{2,1,0:T(8,128)(2,1)}), bf16[16,256,128]{2,1,0:T(8,128)(2,1)S(1)}, u32[]{:S(2)}, u32[]{:S(2)}) async-start(bf16[16,256,128]{2,1,0:T(8,128)(2,1)} %bitcast.8), calls=%async_computation.1 | async-start | bytes 2097152 | tf_op jit(solution)/shard_map/all_to_all | solution.py:169
  47.9 7.2 %collective-permute-start.3 = (s32[8,4096]{1,0:T(8,128)S(1)}, s32[8,4096]{1,0:T(8,128)S(1)}, u32[]{:S(2)}, u32[]{:S(2)}) collective-permute-start(s32[8,4096]{1,0:T(8,128)S(1)} %pad_add_fusion.2), channel_id=1, source_target_pairs={{0,8},{2,10},{4,12},{6,14},{8,0},{10,2},{12,4},{14,6},{1,9},{3,11}... | collective-permute-start | bytes 393224 | tf_op jit(solution)/shard_map/ppermute | solution.py:183
  55.1 24.4 %collective-permute-done.3 = s32[8,4096]{1,0:T(8,128)S(1)} collective-permute-done((s32[8,4096]{1,0:T(8,128)S(1)}, s32[8,4096]{1,0:T(8,128)S(1)}, u32[]{:S(2)}, u32[]{:S(2)}) %collective-permute-start.3) | collective-permute-done | bytes 131104 | tf_op jit(solution)/shard_map/ppermute | solution.py:183
  79.8 17.8 %edge_sums.2 = f32[512,128]{1,0:T(8,128)S(1)} custom-call(s32[2,16]{1,0:T(2,128)S(1)} %pad_add_fusion.8.bounds_ref, s32[65536]{0:T(1024)S(1)} %bitcast.60, bf16[4096,128]{1,0:T(8,128)(2,1)S(1)} %bitcast.58), custom_call_target="tpu_custom_call" | custom-call | flops 2097152 | bytes 2097152 | tf_op jit(solution)/shard_map/edge_sums/pallas_call | solution.py:96
  97.7 3.0 %collective-permute-start.4 = (bf16[256,128]{1,0:T(8,128)(2,1)S(1)}, bf16[256,128]{1,0:T(8,128)(2,1)S(1)}, u32[]{:S(2)}, u32[]{:S(2)}) collective-permute-start(bf16[256,128]{1,0:T(8,128)(2,1)S(1)} %dynamic-slice_convert_fusion.1), channel_id=1, source_target_pairs={{0,1},{1,0},{2,3},{3,2},{4,5},{5,4},{6,7},{7,6},{8,9},{9,8},{10,11... | collective-permute-start | bytes 196616 | tf_op jit(solution)/shard_map/ppermute | solution.py:177
  102.3 11.8 %sort.19.cloned.1.call-done = s32[1,4096]{1,0:T(1,128)} async-done(((s32[1,4096]{1,0:T(1,128)}), s32[1,4096]{1,0:T(1,128)}) %sort.19.cloned.1.call-update) | async-done | bytes 16400 | tf_op jit(solution)/shard_map/sort | solution.py:190
  117.2 12.4 %all-to-all-start.2 = ((bf16[32,4,256]{2,1,0:T(4,128)(2,1)}), bf16[32,4,256]{2,1,0:T(4,128)(2,1)S(1)}, u32[]{:S(2)}, u32[]{:S(2)}) async-start(bf16[32,4,256]{2,1,0:T(4,128)(2,1)} %reshape.106), calls=%async_computation.2 | async-start | bytes 131072 | tf_op jit(solution)/shard_map/all_to_all | solution.py:156
  129.7 2.7 %collective-permute-start.6 = (s32[2,4096]{1,0:T(2,128)S(1)}, s32[2,4096]{1,0:T(2,128)S(1)}, u32[]{:S(2)}, u32[]{:S(2)}) collective-permute-start(s32[2,4096]{1,0:T(2,128)S(1)} %pad_add_fusion.7), channel_id=1, source_target_pairs={{0,2},{2,0},{4,6},{6,4},{8,10},{10,8},{12,14},{14,12},{1,3},{3,1},... | collective-permute-start | bytes 98312 | tf_op jit(solution)/shard_map/ppermute | solution.py:183
  132.4 6.1 %all-to-all-done.2 = bf16[32,4,256]{2,1,0:T(4,128)(2,1)S(1)} async-done(((bf16[32,4,256]{2,1,0:T(4,128)(2,1)}), bf16[32,4,256]{2,1,0:T(4,128)(2,1)S(1)}, u32[]{:S(2)}, u32[]{:S(2)}) %all-to-all-start.2) | async-done | bytes 65568 | tf_op jit(solution)/shard_map/all_to_all | solution.py:156
  141.6 3.9 %all-to-all-start.3 = ((bf16[32,12,512]{2,1,0:T(8,128)(2,1)}), bf16[32,12,512]{2,1,0:T(8,128)(2,1)S(1)}, u32[]{:S(2)}, u32[]{:S(2)}) async-start(bf16[32,12,512]{2,1,0:T(8,128)(2,1)} %maximum_maximum_fusion), calls=%async_computation.3 | async-start | bytes 1048576 | tf_op jit(solution)/shard_map/all_to_all | solution.py:156
  145.6 4.1 %collective-permute-start.7 = (s32[4,4096]{1,0:T(4,128)S(1)}, s32[4,4096]{1,0:T(4,128)S(1)}, u32[]{:S(2)}, u32[]{:S(2)}) collective-permute-start(s32[4,4096]{1,0:T(4,128)S(1)} %pad_add_fusion.5), channel_id=1, source_target_pairs={{0,4},{2,6},{4,0},{6,2},{8,12},{10,14},{12,8},{14,10},{1,5},{3,7},... | collective-permute-start | bytes 196616 | tf_op jit(solution)/shard_map/ppermute | solution.py:183
  149.7 9.5 %all-to-all-done.3 = bf16[32,12,512]{2,1,0:T(8,128)(2,1)S(1)} async-done(((bf16[32,12,512]{2,1,0:T(8,128)(2,1)}), bf16[32,12,512]{2,1,0:T(8,128)(2,1)S(1)}, u32[]{:S(2)}, u32[]{:S(2)}) %all-to-all-start.3) | async-done | bytes 393248 | tf_op jit(solution)/shard_map/all_to_all | solution.py:156
  160.8 11.0 %all-to-all-start.4 = ((bf16[16,256,128]{2,1,0:T(8,128)(2,1)}), bf16[16,256,128]{2,1,0:T(8,128)(2,1)S(1)}, u32[]{:S(2)}, u32[]{:S(2)}) async-start(bf16[16,256,128]{2,1,0:T(8,128)(2,1)} %bitcast.19), calls=%async_computation.4 | async-start | bytes 2097152 | tf_op jit(solution)/shard_map/all_to_all | solution.py:169
  171.9 7.2 %collective-permute-start.8 = (s32[8,4096]{1,0:T(8,128)S(1)}, s32[8,4096]{1,0:T(8,128)S(1)}, u32[]{:S(2)}, u32[]{:S(2)}) collective-permute-start(s32[8,4096]{1,0:T(8,128)S(1)} %pad_add_fusion.3), channel_id=1, source_target_pairs={{0,8},{2,10},{4,12},{6,14},{8,0},{10,2},{12,4},{14,6},{1,9},{3,11}... | collective-permute-start | bytes 393224 | tf_op jit(solution)/shard_map/ppermute | solution.py:183
  179.2 2.5 collective-permute-start.10
  184.8 17.9 %collective-permute-done.11 = f32[8,512]{1,0:T(8,128)S(1)} collective-permute-done((f32[8,512]{1,0:T(8,128)S(1)}, f32[8,512]{1,0:T(8,128)S(1)}, u32[]{:S(2)}, u32[]{:S(2)}) %collective-permute-start.11) | collective-permute-done | bytes 16416 | tf_op jit(solution)/shard_map/ppermute | solution.py:183
  205.0 3.1 %collective-permute-done.12 = f32[8,512]{1,0:T(8,128)S(1)} collective-permute-done((f32[8,512]{1,0:T(8,128)S(1)}, f32[8,512]{1,0:T(8,128)S(1)}, u32[]{:S(2)}, u32[]{:S(2)}) %collective-permute-start.12) | collective-permute-done | bytes 16416 | tf_op jit(solution)/shard_map/ppermute | solution.py:183
  208.0 5.9 %collective-permute-start.13 = (f32[8,512]{1,0:T(8,128)S(1)}, f32[8,512]{1,0:T(8,128)S(1)}, u32[]{:S(2)}, u32[]{:S(2)}) collective-permute-start(f32[8,512]{1,0:T(8,128)S(1)} %add.77), channel_id=1, source_target_pairs={{0,8},{2,10},{4,12},{6,14},{8,0},{10,2},{12,4},{14,6},{1,9},{3,11}... | collective-permute-start | bytes 49160 | tf_op jit(solution)/shard_map/ppermute | solution.py:183
  216.4 15.1 %edge_sums.3 = f32[512,128]{1,0:T(8,128)S(1)} custom-call(s32[2,16]{1,0:T(2,128)S(1)} %pad_add_fusion.9.bounds_ref, s32[65536]{0:T(1024)S(1)} %bitcast.59, bf16[4096,128]{1,0:T(8,128)(2,1)S(1)} %bitcast.57), custom_call_target="tpu_custom_call" | custom-call | flops 2097152 | bytes 2097152 | tf_op jit(solution)/shard_map/edge_sums/pallas_call | solution.py:96
  231.5 5.1 %collective-permute-start.9 = (bf16[256,128]{1,0:T(8,128)(2,1)S(1)}, bf16[256,128]{1,0:T(8,128)(2,1)S(1)}, u32[]{:S(2)}, u32[]{:S(2)}) collective-permute-start(bf16[256,128]{1,0:T(8,128)(2,1)S(1)} %dynamic-slice_convert_fusion), channel_id=1, source_target_pairs={{0,1},{1,0},{2,3},{3,2},{4,5},{5,4},{6,7},{7,6},{8,9},{9,8},{10,11... | collective-permute-start | bytes 196616 | tf_op jit(solution)/shard_map/ppermute | solution.py:177
  238.7 5.6 %all-to-all-start.5 = ((bf16[32,20,256]{2,1,0:T(8,128)(2,1)}), bf16[32,20,256]{2,1,0:T(8,128)(2,1)S(1)}, u32[]{:S(2)}, u32[]{:S(2)}) async-start(bf16[32,20,256]{2,1,0:T(8,128)(2,1)} %pad_maximum_fusion), calls=%async_computation.5 | async-start | bytes 786432 | tf_op jit(solution)/shard_map/all_to_all | solution.py:156
  245.5 10.6 %all-to-all-done.5 = bf16[32,20,256]{2,1,0:T(8,128)(2,1)S(1)} async-done(((bf16[32,20,256]{2,1,0:T(8,128)(2,1)}), bf16[32,20,256]{2,1,0:T(8,128)(2,1)S(1)}, u32[]{:S(2)}, u32[]{:S(2)}) %all-to-all-start.5) | async-done | bytes 327712 | tf_op jit(solution)/shard_map/all_to_all | solution.py:156
  (129 shorter events, 37.2 us)
Async XLA Ops:
  7.2 131.6 %copy-start = (bf16[256,256]{1,0:T(8,128)(2,1)S(1)}, bf16[256,256]{1,0:T(8,128)(2,1)}, u32[]{:S(2)}) copy-start(bf16[256,256]{1,0:T(8,128)(2,1)} %param.17) | copy-start | bytes 393220
  7.2 17.4 %sort.17.cloned.1.call-start = ((), (), s32[]{:S(2)}) async-start(), calls=%async_computation.6 | async-start | bytes 49184 | tf_op jit(solution)/shard_map/sort | solution.py:190
  9.3 15.0 %copy-start.2 = (bf16[256,256]{1,0:T(8,128)(2,1)S(1)}, bf16[256,256]{1,0:T(8,128)(2,1)}, u32[]{:S(2)}) copy-start(bf16[256,256]{1,0:T(8,128)(2,1)} %param.16) | copy-start | bytes 393220
  10.6 29.3 %all-to-all-start = ((bf16[32,4,256]{2,1,0:T(4,128)(2,1)}), bf16[32,4,256]{2,1,0:T(4,128)(2,1)S(1)}, u32[]{:S(2)}, u32[]{:S(2)}) async-start(bf16[32,4,256]{2,1,0:T(4,128)(2,1)} %reshape.98), calls=%async_computation | async-start | bytes 131072 | tf_op jit(solution)/shard_map/all_to_all | solution.py:156
  24.5 7.9 %collective-permute-start = (s32[1,4096]{1,0:T(1,128)}, s32[1,4096]{1,0:T(1,128)S(1)}, u32[]{:S(2)}, u32[]{:S(2)}) collective-permute-start(s32[1,4096]{1,0:T(1,128)} %sort.17.cloned.1.call-done), channel_id=1, source_target_pairs={{0,1},{1,0},{2,3},{3,2},{4,5},{5,4},{6,7},{7,6},{8,9},{9,8},{10,11... | collective-permute-start | bytes 49160 | tf_op jit(solution)/shard_map/ppermute | solution.py:177
  33.2 4.7 %collective-permute-start.1 = (s32[2,4096]{1,0:T(2,128)S(1)}, s32[2,4096]{1,0:T(2,128)S(1)}, u32[]{:S(2)}, u32[]{:S(2)}) collective-permute-start(s32[2,4096]{1,0:T(2,128)S(1)} %pad_add_fusion.6), channel_id=1, source_target_pairs={{0,2},{2,0},{4,6},{6,4},{8,10},{10,8},{12,14},{14,12},{1,3},{3,1},... | collective-permute-start | bytes 98312 | tf_op jit(solution)/shard_map/ppermute | solution.py:183
  38.0 9.8 %collective-permute-start.2 = (s32[4,4096]{1,0:T(4,128)S(1)}, s32[4,4096]{1,0:T(4,128)S(1)}, u32[]{:S(2)}, u32[]{:S(2)}) collective-permute-start(s32[4,4096]{1,0:T(4,128)S(1)} %pad_add_fusion.4), channel_id=1, source_target_pairs={{0,4},{2,6},{4,0},{6,2},{8,12},{10,14},{12,8},{14,10},{1,5},{3,7},... | collective-permute-start | bytes 196616 | tf_op jit(solution)/shard_map/ppermute | solution.py:183
  42.0 37.8 %all-to-all-start.1 = ((bf16[16,256,128]{2,1,0:T(8,128)(2,1)}), bf16[16,256,128]{2,1,0:T(8,128)(2,1)S(1)}, u32[]{:S(2)}, u32[]{:S(2)}) async-start(bf16[16,256,128]{2,1,0:T(8,128)(2,1)} %bitcast.8), calls=%async_computation.1 | async-start | bytes 2097152 | tf_op jit(solution)/shard_map/all_to_all | solution.py:169
  47.7 66.3 %sort.19.cloned.1.call-start = ((), (), s32[]{:S(2)}) async-start(), calls=%async_computation.7 | async-start | bytes 49184 | tf_op jit(solution)/shard_map/sort | solution.py:190
  47.9 31.6 %collective-permute-start.3 = (s32[8,4096]{1,0:T(8,128)S(1)}, s32[8,4096]{1,0:T(8,128)S(1)}, u32[]{:S(2)}, u32[]{:S(2)}) collective-permute-start(s32[8,4096]{1,0:T(8,128)S(1)} %pad_add_fusion.2), channel_id=1, source_target_pairs={{0,8},{2,10},{4,12},{6,14},{8,0},{10,2},{12,4},{14,6},{1,9},{3,11}... | collective-permute-start | bytes 393224 | tf_op jit(solution)/shard_map/ppermute | solution.py:183
  97.7 3.9 %collective-permute-start.4 = (bf16[256,128]{1,0:T(8,128)(2,1)S(1)}, bf16[256,128]{1,0:T(8,128)(2,1)S(1)}, u32[]{:S(2)}, u32[]{:S(2)}) collective-permute-start(bf16[256,128]{1,0:T(8,128)(2,1)S(1)} %dynamic-slice_convert_fusion.1), channel_id=1, source_target_pairs={{0,1},{1,0},{2,3},{3,2},{4,5},{5,4},{6,7},{7,6},{8,9},{9,8},{10,11... | collective-permute-start | bytes 196616 | tf_op jit(solution)/shard_map/ppermute | solution.py:177
  114.0 15.6 %collective-permute-start.5 = (s32[1,4096]{1,0:T(1,128)}, s32[1,4096]{1,0:T(1,128)S(1)}, u32[]{:S(2)}, u32[]{:S(2)}) collective-permute-start(s32[1,4096]{1,0:T(1,128)} %sort.19.cloned.1.call-done), channel_id=1, source_target_pairs={{0,1},{1,0},{2,3},{3,2},{4,5},{5,4},{6,7},{7,6},{8,9},{9,8},{10,11... | collective-permute-start | bytes 49160 | tf_op jit(solution)/shard_map/ppermute | solution.py:177
  117.2 21.3 %all-to-all-start.2 = ((bf16[32,4,256]{2,1,0:T(4,128)(2,1)}), bf16[32,4,256]{2,1,0:T(4,128)(2,1)S(1)}, u32[]{:S(2)}, u32[]{:S(2)}) async-start(bf16[32,4,256]{2,1,0:T(4,128)(2,1)} %reshape.106), calls=%async_computation.2 | async-start | bytes 131072 | tf_op jit(solution)/shard_map/all_to_all | solution.py:156
  129.7 15.8 %collective-permute-start.6 = (s32[2,4096]{1,0:T(2,128)S(1)}, s32[2,4096]{1,0:T(2,128)S(1)}, u32[]{:S(2)}, u32[]{:S(2)}) collective-permute-start(s32[2,4096]{1,0:T(2,128)S(1)} %pad_add_fusion.7), channel_id=1, source_target_pairs={{0,2},{2,0},{4,6},{6,4},{8,10},{10,8},{12,14},{14,12},{1,3},{3,1},... | collective-permute-start | bytes 98312 | tf_op jit(solution)/shard_map/ppermute | solution.py:183
  141.6 17.6 %all-to-all-start.3 = ((bf16[32,12,512]{2,1,0:T(8,128)(2,1)}), bf16[32,12,512]{2,1,0:T(8,128)(2,1)S(1)}, u32[]{:S(2)}, u32[]{:S(2)}) async-start(bf16[32,12,512]{2,1,0:T(8,128)(2,1)} %maximum_maximum_fusion), calls=%async_computation.3 | async-start | bytes 1048576 | tf_op jit(solution)/shard_map/all_to_all | solution.py:156
  145.6 26.2 %collective-permute-start.7 = (s32[4,4096]{1,0:T(4,128)S(1)}, s32[4,4096]{1,0:T(4,128)S(1)}, u32[]{:S(2)}, u32[]{:S(2)}) collective-permute-start(s32[4,4096]{1,0:T(4,128)S(1)} %pad_add_fusion.5), channel_id=1, source_target_pairs={{0,4},{2,6},{4,0},{6,2},{8,12},{10,14},{12,8},{14,10},{1,5},{3,7},... | collective-permute-start | bytes 196616 | tf_op jit(solution)/shard_map/ppermute | solution.py:183
  160.8 55.7 %all-to-all-start.4 = ((bf16[16,256,128]{2,1,0:T(8,128)(2,1)}), bf16[16,256,128]{2,1,0:T(8,128)(2,1)S(1)}, u32[]{:S(2)}, u32[]{:S(2)}) async-start(bf16[16,256,128]{2,1,0:T(8,128)(2,1)} %bitcast.19), calls=%async_computation.4 | async-start | bytes 2097152 | tf_op jit(solution)/shard_map/all_to_all | solution.py:169
  171.9 32.8 %collective-permute-start.8 = (s32[8,4096]{1,0:T(8,128)S(1)}, s32[8,4096]{1,0:T(8,128)S(1)}, u32[]{:S(2)}, u32[]{:S(2)}) collective-permute-start(s32[8,4096]{1,0:T(8,128)S(1)} %pad_add_fusion.3), channel_id=1, source_target_pairs={{0,8},{2,10},{4,12},{6,14},{8,0},{10,2},{12,4},{14,6},{1,9},{3,11}... | collective-permute-start | bytes 393224 | tf_op jit(solution)/shard_map/ppermute | solution.py:183
  179.2 3.4 %collective-permute-start.10 = (f32[8,512]{1,0:T(8,128)S(1)}, f32[8,512]{1,0:T(8,128)S(1)}, u32[]{:S(2)}, u32[]{:S(2)}) collective-permute-start(f32[8,512]{1,0:T(8,128)S(1)} %convert_reduce_fusion), channel_id=1, source_target_pairs={{0,1},{1,0},{2,3},{3,2},{4,5},{5,4},{6,7},{7,6},{8,9},{9,8},{10,11... | collective-permute-start | bytes 49160 | tf_op jit(solution)/shard_map/ppermute | solution.py:177
  182.6 20.1 %collective-permute-start.11 = (f32[8,512]{1,0:T(8,128)S(1)}, f32[8,512]{1,0:T(8,128)S(1)}, u32[]{:S(2)}, u32[]{:S(2)}) collective-permute-start(f32[8,512]{1,0:T(8,128)S(1)} %add.75), channel_id=1, source_target_pairs={{0,2},{2,0},{4,6},{6,4},{8,10},{10,8},{12,14},{14,12},{1,3},{3,1},... | collective-permute-start | bytes 49160 | tf_op jit(solution)/shard_map/ppermute | solution.py:183
  202.7 5.4 %collective-permute-start.12 = (f32[8,512]{1,0:T(8,128)S(1)}, f32[8,512]{1,0:T(8,128)S(1)}, u32[]{:S(2)}, u32[]{:S(2)}) collective-permute-start(f32[8,512]{1,0:T(8,128)S(1)} %add.76), channel_id=1, source_target_pairs={{0,4},{2,6},{4,0},{6,2},{8,12},{10,14},{12,8},{14,10},{1,5},{3,7},... | collective-permute-start | bytes 49160 | tf_op jit(solution)/shard_map/ppermute | solution.py:183
  208.0 8.4 %collective-permute-start.13 = (f32[8,512]{1,0:T(8,128)S(1)}, f32[8,512]{1,0:T(8,128)S(1)}, u32[]{:S(2)}, u32[]{:S(2)}) collective-permute-start(f32[8,512]{1,0:T(8,128)S(1)} %add.77), channel_id=1, source_target_pairs={{0,8},{2,10},{4,12},{6,14},{8,0},{10,2},{12,4},{14,6},{1,9},{3,11}... | collective-permute-start | bytes 49160 | tf_op jit(solution)/shard_map/ppermute | solution.py:183
  231.5 6.0 %collective-permute-start.9 = (bf16[256,128]{1,0:T(8,128)(2,1)S(1)}, bf16[256,128]{1,0:T(8,128)(2,1)S(1)}, u32[]{:S(2)}, u32[]{:S(2)}) collective-permute-start(bf16[256,128]{1,0:T(8,128)(2,1)S(1)} %dynamic-slice_convert_fusion), channel_id=1, source_target_pairs={{0,1},{1,0},{2,3},{3,2},{4,5},{5,4},{6,7},{7,6},{8,9},{9,8},{10,11... | collective-permute-start | bytes 196616 | tf_op jit(solution)/shard_map/ppermute | solution.py:177
  238.7 17.4 %all-to-all-start.5 = ((bf16[32,20,256]{2,1,0:T(8,128)(2,1)}), bf16[32,20,256]{2,1,0:T(8,128)(2,1)S(1)}, u32[]{:S(2)}, u32[]{:S(2)}) async-start(bf16[32,20,256]{2,1,0:T(8,128)(2,1)} %pad_maximum_fusion), calls=%async_computation.5 | async-start | bytes 786432 | tf_op jit(solution)/shard_map/all_to_all | solution.py:156
  (8 other events, 40.2 us)
Sparse Core Ops, SparseCore 0:
  11.0 11.3 sort.21.cloned.1.call-done
  102.4 11.3 sort.23.cloned.1.call-done
  (2 shorter events, 0.0 us)

commit v6 on v5

--- a/solution.py
+++ b/solution.py
@@ -7,10 +7,54 @@
 
 MIRR = 62
 LATE = 64
-UNROLL = 16
+UNROLL = 8
 ACCS = 8
 CHUNK = 128
 WINDOW = 1024
+
+
+def sort_kernel(words_ref, out_ref):
+    lists, rows, lanes = words_ref.shape
+    row = lax.broadcasted_iota(jnp.int32, (rows, lanes), 0)
+    lane = lax.broadcasted_iota(jnp.int32, (rows, lanes), 1)
+    values = [words_ref[n] for n in range(lists)]
+
+    def bit(distance):
+        if distance < lanes:
+            return (lane & distance) != 0
+        return (row & (distance // lanes)) != 0
+
+    size = 2
+    while size <= rows * lanes:
+        distance = size // 2
+        while distance:
+            high = bit(distance)
+            keep_larger = high if size == rows * lanes else jnp.logical_xor(high, bit(size))
+            axis, step = (1, distance) if distance < lanes else (0, distance // lanes)
+            extent = (rows, lanes)[axis]
+            for n, x in enumerate(values):
+                other = jnp.where(
+                    high, pltpu.roll(x, step, axis), pltpu.roll(x, extent - step, axis)
+                )
+                values[n] = jnp.where(keep_larger, jnp.maximum(x, other), jnp.minimum(x, other))
+            distance //= 2
+        size *= 2
+    for n in range(lists):
+        out_ref[n] = values[n]
+
+
+def sort_lists(words):
+    vmem = pl.BlockSpec(memory_space=pltpu.VMEM)
+    return pl.pallas_call(
+        sort_kernel,
+        out_shape=jax.ShapeDtypeStruct(words.shape, words.dtype),
+        in_specs=[vmem],
+        out_specs=vmem,
+        cost_estimate=pl.CostEstimate(
+            flops=1000 * words.size, bytes_accessed=8 * words.size, transcendentals=0
+        ),
+        name="sort_lists",
+    )(words)
 
 
 def edge_kernel(bounds_ref, words_ref, table_ref, out_ref, words, table, *rest):
@@ -177,30 +221,26 @@
         return lax.ppermute(values, "core", [(0, 1), (1, 0)])
 
     def spread(values, combine):
-        values = combine(values, twin(values), core == 0)
-        bit = 1
-        while bit < chips:
+        bit = chips // 2
+        while bit:
             theirs = lax.ppermute(values, "y", [(y, y ^ bit) for y in range(chips)])
-            values = combine(values, theirs, (chip & bit) == 0)
-            bit *= 2
-        return values
-
-    def edge_lists(place, take):
-        words = jnp.where(place >= 0, (place << 16) | take, part_rows << 16)
-        words = lax.sort(words.reshape(1, -1), dimension=1)
-        words = spread(
-            words,
-            lambda mine, theirs, low: jnp.concatenate(
-                [jnp.where(low, mine, theirs), jnp.where(low, theirs, mine)]
-            ),
-        )
+            values = combine(values, theirs)
+            bit //= 2
+        return combine(values, twin(values))
+
+    def edge_lists(places, takes):
+        words = jnp.where(places >= 0, (places << 16) | takes, part_rows << 16)
+        words = sort_lists(words.reshape(2, -1, 128))
+        words = spread(words, lambda mine, theirs: jnp.concatenate([mine, theirs], axis=1))
+        lists = words.reshape(2, members, -1)
         bounds = jnp.stack(
             [
-                jnp.sum((words < (at * (2 * rows) << 16)).astype(jnp.int32), axis=1)
+                jnp.sum((lists < (at * (2 * rows) << 16)).astype(jnp.int32), axis=2)
                 for at in (chip, chip + 1)
-            ]
+            ],
+            axis=1,
         )
-        return bounds, words.reshape(-1)
+        return [(bounds[n], words[n].reshape(-1)) for n in range(2)]
 
     def row_sums(lists, table):
         block = edge_sums(*lists, table)
@@ -222,14 +262,12 @@
             pick_recv, slots.reshape(slot_count, width), contract_first, preferred_element_type=f32
         )
 
-    src, dst = edge_src.reshape(-1), edge_dst.reshape(-1)
-    slots, src, dst = lax.optimization_barrier((from_masters(features), src, dst))
-    lists = edge_lists(dst, src)
+    slots, src, dst = lax.optimization_barrier((from_masters(features), edge_src, edge_dst))
+    src, dst = src.reshape(1, -1), dst.reshape(1, -1)
+    by_dst, by_src = edge_lists(jnp.concatenate([dst, src]), jnp.concatenate([src, dst]))
     late_rows = at_mirrors(over_dom(slots), features)
     table = gather(jnp.concatenate([features[:early], late_rows], axis=0))
-    totals = row_sums(lists, table)
-    totals, src, dst = lax.optimization_barrier((totals, src, dst))
-    lists = edge_lists(src, dst)
+    totals = row_sums(by_dst, table)
     totals = totals + add_at_masters(over_dom(mirror_slots(totals)))
     averaged = (totals / denominator).astype(bf16)
 
@@ -258,11 +296,12 @@
     activated = jnp.concatenate([activated[:early], activated_late], axis=0)
 
     weight_sum = spread(
-        jnp.sum(moved[:, cap:].astype(f32), axis=0), lambda mine, theirs, low: mine + theirs
+        jnp.sum(moved[:, cap:].astype(f32), axis=0), lambda mine, theirs: mine + theirs
     )
     share = weight_sum.astype(bf16).reshape(-1, width)
     share = jnp.broadcast_to(share[None], (dom_count,) + share.shape)
-    totals = row_sums(lists, table)
+    table, share = lax.optimization_barrier((table, share))
+    totals = row_sums(by_src, table)
     moved = over_dom(jnp.concatenate([mirror_slots(totals), share], axis=1))
     weight_sums = moved[:, cap:].reshape(-1, 2 * width).astype(f32)
     back_sum = totals + add_at_masters(moved[:, :cap])

time: 268 us -> 250 us (0.933)
  waiting for transfers between devices: 79.3 us -> 97.7 us
  starting transfers between devices: 107 us -> 92.2 us
  between operations: 14.8 us -> 1.29 us
  local copies, waits for them, and re-layouts: 20 us -> 8.38 us
  Pallas kernels: 32.9 us -> 38.5 us
    all_to_all x2, waiting for transfers between devices: 0.01 us -> 27 us  [over_member(): lax.all_to_all(blocks, member, split_axis=0, concat_axis=0, tiled=True)]
    ppermute x9 -> x6, waiting for transfers between devices: 49.5 us -> 34.7 us  [spread(): theirs = lax.ppermute(values, 'y', [(y, y ^ bit) for y in range(chips)])]
    sort x4 -> x0, local copies, waits for them, and re-layouts: 11.8 us -> none  [edge_lists(): words = lax.sort(words.reshape(1, -1), dimension=1)]
    ppermute x9 -> x6, starting transfers between devices: 35.1 us -> 24.6 us  [spread(): theirs = lax.ppermute(values, 'y', [(y, y ^ bit) for y in range(chips)])]
    all_to_all x4, waiting for transfers between devices: 26.2 us -> 33.1 us  [over_dom(): return lax.all_to_all(slots, 'dom', split_axis=0, concat_axis=0, tiled=True)]
    pallas_call x0 -> x1, Pallas kernels: none -> 6.17 us  [sort_lists(): pl.pallas_call(sort_kernel, out_shape=jax.ShapeDtypeStruct(words.shape, w...]
    ppermute x5 -> x4, starting transfers between devices: 19.8 us -> 14.8 us  [twin(): return lax.ppermute(values, 'core', [(0, 1), (1, 0)])]
    all_to_all x4, starting transfers between devices: 35.6 us -> 39.5 us  [over_dom(): return lax.all_to_all(slots, 'dom', split_axis=0, concat_axis=0, tiled=True)]
  transfers between devices with their start and end apart: 20 -> 16, of which waited for: 12 -> 12; matrix products, arithmetic and copies ran while one was open for 4% -> 2% of each run, Pallas kernels for 0% -> 0%
where the time goes in v6:
time: 250 us; the launch traced here: 247 us
  waiting for transfers between devices  97.7 us (39%)
  starting transfers between devices  92.2 us (37%)
  Pallas kernels  38.5 us (15%)
  local copies, waits for them, and re-layouts  8.38 us (3%)
  matrix products  5.17 us (2%)
  other arithmetic  4.12 us (2%)
    all_to_all x4, starting transfers between devices, over_dom(): return lax.all_to_all(slots, 'dom', split_axis=0, concat_axis=0, tiled=True)  39.5 us
    ppermute x6, waiting for transfers between devices, spread(): theirs = lax.ppermute(values, 'y', [(y, y ^ bit) for y in range(chips)])  34.7 us
    all_to_all x4, waiting for transfers between devices, over_dom(): return lax.all_to_all(slots, 'dom', split_axis=0, concat_axis=0, tiled=True)  33.1 us
    pallas_call x2, Pallas kernels, edge_sums(): pl.pallas_call(edge_kernel, out_shape=jax.ShapeDtypeStruct((own, width),...  32.3 us
    all_to_all x2, waiting for transfers between devices, over_member(): lax.all_to_all(blocks, member, split_axis=0, concat_axis=0, tiled=True)  27 us
    ppermute x6, starting transfers between devices, spread(): theirs = lax.ppermute(values, 'y', [(y, y ^ bit) for y in range(chips)])  24.6 us
    ppermute x4, starting transfers between devices, twin(): return lax.ppermute(values, 'core', [(0, 1), (1, 0)])  14.8 us
    all_to_all x2, starting transfers between devices, over_member(): lax.all_to_all(blocks, member, split_axis=0, concat_axis=0, tiled=True)  13.4 us
  transfers between devices with their start and end apart: 16, of which 12 were waited for; matrix products, arithmetic and copies ran while one was open for 2% of the time, Pallas kernels for 0%

profile of v6, /device:TPU:1, one launch (start us, length us, event | category | flops | bytes accessed | tf_op | source)
XLA Modules:
  0.0 247.3 jit_solution(14889760307928069307)
XLA Ops:
  4.0 6.2 %sort_lists.1 = s32[2,32,128]{2,1,0:T(8,128)} custom-call(s32[2,32,128]{2,1,0:T(8,128)} %fusion.29.words_ref), custom_call_target="tpu_custom_call" | custom-call | flops 8192000 | bytes 65536 | tf_op jit(solution)/shard_map/sort_lists/pallas_call | solution.py:48
  10.2 8.4 %collective-permute-start = (s32[2,32,128]{2,1,0:T(8,128)}, s32[2,32,128]{2,1,0:T(8,128)S(1)}, u32[]{:S(2)}, u32[]{:S(2)}) collective-permute-start(s32[2,32,128]{2,1,0:T(8,128)} %sort_lists.1), channel_id=1, source_target_pairs={{0,8},{2,10},{4,12},{6,14},{8,0},{10,2},{12,4},{14,6},{1,9},{3,11}... | collective-permute-start | bytes 98312 | tf_op jit(solution)/shard_map/ppermute | solution.py:226
  18.6 12.9 %all-to-all-start = ((bf16[32,4,256]{2,1,0:T(4,128)(2,1)}), bf16[32,4,256]{2,1,0:T(4,128)(2,1)S(1)}, u32[]{:S(2)}, u32[]{:S(2)}) async-start(bf16[32,4,256]{2,1,0:T(4,128)(2,1)} %reshape.94), calls=%async_computation | async-start | bytes 131072 | tf_op jit(solution)/shard_map/all_to_all | solution.py:200
  32.6 2.4 collective-permute-start.1
  35.1 4.5 %collective-permute-done.1 = s32[2,64,128]{2,1,0:T(8,128)S(1)} collective-permute-done((s32[2,64,128]{2,1,0:T(8,128)S(1)}, s32[2,64,128]{2,1,0:T(8,128)S(1)}, u32[]{:S(2)}, u32[]{:S(2)}) %collective-permute-start.1) | collective-permute-done | bytes 65568 | tf_op jit(solution)/shard_map/ppermute | solution.py:226
  41.8 3.4 %collective-permute-done.2 = s32[2,128,128]{2,1,0:T(8,128)S(1)} collective-permute-done((s32[2,128,128]{2,1,0:T(8,128)S(1)}, s32[2,128,128]{2,1,0:T(8,128)S(1)}, u32[]{:S(2)}, u32[]{:S(2)}) %collective-permute-start.2) | collective-permute-done | bytes 131104 | tf_op jit(solution)/shard_map/ppermute | solution.py:226
  45.3 5.2 %collective-permute-start.3 = (s32[2,256,128]{2,1,0:T(8,128)S(1)}, s32[2,256,128]{2,1,0:T(8,128)S(1)}, u32[]{:S(2)}, u32[]{:S(2)}) collective-permute-start(s32[2,256,128]{2,1,0:T(8,128)S(1)} %pad_add_fusion), channel_id=1, source_target_pairs={{0,1},{1,0},{2,3},{3,2},{4,5},{5,4},{6,7},{7,6},{8,9},{9,8},{10,11... | collective-permute-start | bytes 786440 | tf_op jit(solution)/shard_map/ppermute | solution.py:221
  51.7 3.5 %all-to-all-start.1 = ((bf16[16,256,128]{2,1,0:T(8,128)(2,1)}), bf16[16,256,128]{2,1,0:T(8,128)(2,1)S(1)}, u32[]{:S(2)}, u32[]{:S(2)}) async-start(bf16[16,256,128]{2,1,0:T(8,128)(2,1)} %bitcast.9), calls=%async_computation.1 | async-start | bytes 2097152 | tf_op jit(solution)/shard_map/all_to_all | solution.py:213
  56.1 27.0 %all-to-all-done.1 = bf16[16,256,128]{2,1,0:T(8,128)(2,1)S(1)} async-done(((bf16[16,256,128]{2,1,0:T(8,128)(2,1)}), bf16[16,256,128]{2,1,0:T(8,128)(2,1)S(1)}, u32[]{:S(2)}, u32[]{:S(2)}) %all-to-all-start.1) | async-done | bytes 1048608 | tf_op jit(solution)/shard_map/all_to_all | solution.py:213
  83.1 16.1 %edge_sums.2 = f32[512,128]{1,0:T(8,128)S(1)} custom-call(s32[2,16]{1,0:T(2,128)S(1)} %bitcast.56, s32[65536]{0:T(1024)S(1)} %get-tuple-element.21.words_ref, bf16[4096,128]{1,0:T(8,128)(2,1)S(1)} %bitcast.54), custom_call_target="tpu_custom_call" | custom-call | flops 2097152 | bytes 2097152 | tf_op jit(solution)/shard_map/edge_sums/pallas_call | solution.py:140
  103.3 15.8 %all-to-all-start.2 = ((bf16[32,4,256]{2,1,0:T(4,128)(2,1)}), bf16[32,4,256]{2,1,0:T(4,128)(2,1)S(1)}, u32[]{:S(2)}, u32[]{:S(2)}) async-start(bf16[32,4,256]{2,1,0:T(4,128)(2,1)} %reshape.98), calls=%async_computation.2 | async-start | bytes 131072 | tf_op jit(solution)/shard_map/all_to_all | solution.py:200
  119.2 8.8 %all-to-all-done.2 = bf16[32,4,256]{2,1,0:T(4,128)(2,1)S(1)} async-done(((bf16[32,4,256]{2,1,0:T(4,128)(2,1)}), bf16[32,4,256]{2,1,0:T(4,128)(2,1)S(1)}, u32[]{:S(2)}, u32[]{:S(2)}) %all-to-all-start.2) | async-done | bytes 65568 | tf_op jit(solution)/shard_map/all_to_all | solution.py:200
  131.9 3.9 %all-to-all-start.3 = ((bf16[32,12,512]{2,1,0:T(8,128)(2,1)}), bf16[32,12,512]{2,1,0:T(8,128)(2,1)S(1)}, u32[]{:S(2)}, u32[]{:S(2)}) async-start(bf16[32,12,512]{2,1,0:T(8,128)(2,1)} %maximum_maximum_fusion), calls=%async_computation.3 | async-start | bytes 1048576 | tf_op jit(solution)/shard_map/all_to_all | solution.py:200
  135.8 13.7 %all-to-all-done.3 = bf16[32,12,512]{2,1,0:T(8,128)(2,1)S(1)} async-done(((bf16[32,12,512]{2,1,0:T(8,128)(2,1)}), bf16[32,12,512]{2,1,0:T(8,128)(2,1)S(1)}, u32[]{:S(2)}, u32[]{:S(2)}) %all-to-all-start.3) | async-done | bytes 393248 | tf_op jit(solution)/shard_map/all_to_all | solution.py:200
  151.1 9.8 %all-to-all-start.4 = ((bf16[16,256,128]{2,1,0:T(8,128)(2,1)}), bf16[16,256,128]{2,1,0:T(8,128)(2,1)S(1)}, u32[]{:S(2)}, u32[]{:S(2)}) async-start(bf16[16,256,128]{2,1,0:T(8,128)(2,1)} %bitcast.19), calls=%async_computation.4 | async-start | bytes 2097152 | tf_op jit(solution)/shard_map/all_to_all | solution.py:213
  161.0 7.2 %collective-permute-start.5 = (f32[8,512]{1,0:T(8,128)S(1)}, f32[8,512]{1,0:T(8,128)S(1)}, u32[]{:S(2)}, u32[]{:S(2)}) collective-permute-start(f32[8,512]{1,0:T(8,128)S(1)} %convert_reduce_fusion), channel_id=1, source_target_pairs={{0,8},{2,10},{4,12},{6,14},{8,0},{10,2},{12,4},{14,6},{1,9},{3,11}... | collective-permute-start | bytes 49160 | tf_op jit(solution)/shard_map/ppermute | solution.py:226
  168.2 21.5 %collective-permute-done.5 = f32[8,512]{1,0:T(8,128)S(1)} collective-permute-done((f32[8,512]{1,0:T(8,128)S(1)}, f32[8,512]{1,0:T(8,128)S(1)}, u32[]{:S(2)}, u32[]{:S(2)}) %collective-permute-start.5) | collective-permute-done | bytes 16416 | tf_op jit(solution)/shard_map/ppermute | solution.py:226
  191.8 3.4 %collective-permute-done.6 = f32[8,512]{1,0:T(8,128)S(1)} collective-permute-done((f32[8,512]{1,0:T(8,128)S(1)}, f32[8,512]{1,0:T(8,128)S(1)}, u32[]{:S(2)}, u32[]{:S(2)}) %collective-permute-start.6) | collective-permute-done | bytes 16416 | tf_op jit(solution)/shard_map/ppermute | solution.py:226
  195.1 2.6 %collective-permute-start.7 = (f32[8,512]{1,0:T(8,128)S(1)}, f32[8,512]{1,0:T(8,128)S(1)}, u32[]{:S(2)}, u32[]{:S(2)}) collective-permute-start(f32[8,512]{1,0:T(8,128)S(1)} %add.75), channel_id=1, source_target_pairs={{0,2},{2,0},{4,6},{6,4},{8,10},{10,8},{12,14},{14,12},{1,3},{3,1},... | collective-permute-start | bytes 49160 | tf_op jit(solution)/shard_map/ppermute | solution.py:226
  199.6 5.5 %collective-permute-start.8 = (f32[8,512]{1,0:T(8,128)S(1)}, f32[8,512]{1,0:T(8,128)S(1)}, u32[]{:S(2)}, u32[]{:S(2)}) collective-permute-start(f32[8,512]{1,0:T(8,128)S(1)} %add.76), channel_id=1, source_target_pairs={{0,1},{1,0},{2,3},{3,2},{4,5},{5,4},{6,7},{7,6},{8,9},{9,8},{10,11... | collective-permute-start | bytes 49160 | tf_op jit(solution)/shard_map/ppermute | solution.py:221
  206.0 16.3 %edge_sums.3 = f32[512,128]{1,0:T(8,128)S(1)} custom-call(s32[2,16]{1,0:T(2,128)S(1)} %bitcast.55, s32[65536]{0:T(1024)S(1)} %get-tuple-element.20.words_ref, bf16[4096,128]{1,0:T(8,128)(2,1)S(1)} %bitcast.53), custom_call_target="tpu_custom_call" | custom-call | flops 2097152 | bytes 2097152 | tf_op jit(solution)/shard_map/edge_sums/pallas_call | solution.py:140
  222.3 2.3 collective-permute-start.9
  226.6 6.8 %all-to-all-start.5 = ((bf16[32,20,256]{2,1,0:T(8,128)(2,1)}), bf16[32,20,256]{2,1,0:T(8,128)(2,1)S(1)}, u32[]{:S(2)}, u32[]{:S(2)}) async-start(bf16[32,20,256]{2,1,0:T(8,128)(2,1)} %pad_maximum_fusion), calls=%async_computation.5 | async-start | bytes 786432 | tf_op jit(solution)/shard_map/all_to_all | solution.py:200
  234.7 10.6 %all-to-all-done.5 = bf16[32,20,256]{2,1,0:T(8,128)(2,1)S(1)} async-done(((bf16[32,20,256]{2,1,0:T(8,128)(2,1)}), bf16[32,20,256]{2,1,0:T(8,128)(2,1)S(1)}, u32[]{:S(2)}, u32[]{:S(2)}) %all-to-all-start.5) | async-done | bytes 327712 | tf_op jit(solution)/shard_map/all_to_all | solution.py:200
  (112 shorter events, 28.2 us)
Async XLA Ops:
  0.6 127.7 %copy-start = (bf16[256,256]{1,0:T(8,128)(2,1)S(1)}, bf16[256,256]{1,0:T(8,128)(2,1)}, u32[]{:S(2)}) copy-start(bf16[256,256]{1,0:T(8,128)(2,1)} %param.17) | copy-start | bytes 393220
  1.5 1.8 copy-start.5
  1.6 1.8 copy-start.6
  2.7 28.8 %copy-start.4 = (bf16[256,256]{1,0:T(8,128)(2,1)S(1)}, bf16[256,256]{1,0:T(8,128)(2,1)}, u32[]{:S(2)}) copy-start(bf16[256,256]{1,0:T(8,128)(2,1)} %param.16) | copy-start | bytes 393220
  4.0 27.5 %copy-start.1 = (bf16[256,256]{1,0:T(8,128)(2,1)S(1)}, bf16[256,256]{1,0:T(8,128)(2,1)}, u32[]{:S(2)}) copy-start(bf16[256,256]{1,0:T(8,128)(2,1)} %param.9) | copy-start | bytes 393220
  10.2 21.3 %copy-start.3 = (s32[2,32,128]{2,1,0:T(8,128)S(1)}, s32[2,32,128]{2,1,0:T(8,128)}, u32[]{:S(2)}) copy-start(s32[2,32,128]{2,1,0:T(8,128)} %sort_lists.1) | copy-start | bytes 98308
  10.2 22.5 %collective-permute-start = (s32[2,32,128]{2,1,0:T(8,128)}, s32[2,32,128]{2,1,0:T(8,128)S(1)}, u32[]{:S(2)}, u32[]{:S(2)}) collective-permute-start(s32[2,32,128]{2,1,0:T(8,128)} %sort_lists.1), channel_id=1, source_target_pairs={{0,8},{2,10},{4,12},{6,14},{8,0},{10,2},{12,4},{14,6},{1,9},{3,11}... | collective-permute-start | bytes 98312 | tf_op jit(solution)/shard_map/ppermute | solution.py:226
  18.6 22.9 %all-to-all-start = ((bf16[32,4,256]{2,1,0:T(4,128)(2,1)}), bf16[32,4,256]{2,1,0:T(4,128)(2,1)S(1)}, u32[]{:S(2)}, u32[]{:S(2)}) async-start(bf16[32,4,256]{2,1,0:T(4,128)(2,1)} %reshape.94), calls=%async_computation | async-start | bytes 131072 | tf_op jit(solution)/shard_map/all_to_all | solution.py:200
  32.6 6.9 %collective-permute-start.1 = (s32[2,64,128]{2,1,0:T(8,128)S(1)}, s32[2,64,128]{2,1,0:T(8,128)S(1)}, u32[]{:S(2)}, u32[]{:S(2)}) collective-permute-start(s32[2,64,128]{2,1,0:T(8,128)S(1)} %pad_add_fusion.2), channel_id=1, source_target_pairs={{0,4},{2,6},{4,0},{6,2},{8,12},{10,14},{12,8},{14,10},{1,5},{3,7},... | collective-permute-start | bytes 196616 | tf_op jit(solution)/shard_map/ppermute | solution.py:226
  39.6 5.7 %collective-permute-start.2 = (s32[2,128,128]{2,1,0:T(8,128)S(1)}, s32[2,128,128]{2,1,0:T(8,128)S(1)}, u32[]{:S(2)}, u32[]{:S(2)}) collective-permute-start(s32[2,128,128]{2,1,0:T(8,128)S(1)} %pad_add_fusion.1), channel_id=1, source_target_pairs={{0,2},{2,0},{4,6},{6,4},{8,10},{10,8},{12,14},{14,12},{1,3},{3,1},... | collective-permute-start | bytes 393224 | tf_op jit(solution)/shard_map/ppermute | solution.py:226
  41.8 8.6 %slice-start = ((bf16[256,256]{1,0:T(8,128)(2,1)}), bf16[192,256]{1,0:T(8,128)(2,1)S(1)}, s32[]{:S(2)}) async-start(bf16[256,256]{1,0:T(8,128)(2,1)} %param.9), calls=%async_computation.6 | async-start | bytes 196608 | tf_op jit(solution)/shard_map/slice | solution.py:269
  45.3 10.0 %collective-permute-start.3 = (s32[2,256,128]{2,1,0:T(8,128)S(1)}, s32[2,256,128]{2,1,0:T(8,128)S(1)}, u32[]{:S(2)}, u32[]{:S(2)}) collective-permute-start(s32[2,256,128]{2,1,0:T(8,128)S(1)} %pad_add_fusion), channel_id=1, source_target_pairs={{0,1},{1,0},{2,3},{3,2},{4,5},{5,4},{6,7},{7,6},{8,9},{9,8},{10,11... | collective-permute-start | bytes 786440 | tf_op jit(solution)/shard_map/ppermute | solution.py:221
  51.7 31.4 %all-to-all-start.1 = ((bf16[16,256,128]{2,1,0:T(8,128)(2,1)}), bf16[16,256,128]{2,1,0:T(8,128)(2,1)S(1)}, u32[]{:S(2)}, u32[]{:S(2)}) async-start(bf16[16,256,128]{2,1,0:T(8,128)(2,1)} %bitcast.9), calls=%async_computation.1 | async-start | bytes 2097152 | tf_op jit(solution)/shard_map/all_to_all | solution.py:213
  99.2 3.1 %collective-permute-start.4 = (bf16[256,128]{1,0:T(8,128)(2,1)S(1)}, bf16[256,128]{1,0:T(8,128)(2,1)S(1)}, u32[]{:S(2)}, u32[]{:S(2)}) collective-permute-start(bf16[256,128]{1,0:T(8,128)(2,1)S(1)} %dynamic-slice_convert_fusion.1), channel_id=1, source_target_pairs={{0,1},{1,0},{2,3},{3,2},{4,5},{5,4},{6,7},{7,6},{8,9},{9,8},{10,11... | collective-permute-start | bytes 196616 | tf_op jit(solution)/shard_map/ppermute | solution.py:221
  103.3 15.9 %copy-start.8 = (s32[1,1,256]{2,1,0:T(1,128)S(1)}, s32[1,1,256]{2,1,0:T(1,128)}, u32[]{:S(2)}) copy-start(s32[1,1,256]{2,1,0:T(1,128)} %param.15) | copy-start | bytes 3076
  103.3 24.7 %all-to-all-start.2 = ((bf16[32,4,256]{2,1,0:T(4,128)(2,1)}), bf16[32,4,256]{2,1,0:T(4,128)(2,1)S(1)}, u32[]{:S(2)}, u32[]{:S(2)}) async-start(bf16[32,4,256]{2,1,0:T(4,128)(2,1)} %reshape.98), calls=%async_computation.2 | async-start | bytes 131072 | tf_op jit(solution)/shard_map/all_to_all | solution.py:200
  131.9 17.6 %all-to-all-start.3 = ((bf16[32,12,512]{2,1,0:T(8,128)(2,1)}), bf16[32,12,512]{2,1,0:T(8,128)(2,1)S(1)}, u32[]{:S(2)}, u32[]{:S(2)}) async-start(bf16[32,12,512]{2,1,0:T(8,128)(2,1)} %maximum_maximum_fusion), calls=%async_computation.3 | async-start | bytes 1048576 | tf_op jit(solution)/shard_map/all_to_all | solution.py:200
  151.1 54.9 %all-to-all-start.4 = ((bf16[16,256,128]{2,1,0:T(8,128)(2,1)}), bf16[16,256,128]{2,1,0:T(8,128)(2,1)S(1)}, u32[]{:S(2)}, u32[]{:S(2)}) async-start(bf16[16,256,128]{2,1,0:T(8,128)(2,1)} %bitcast.19), calls=%async_computation.4 | async-start | bytes 2097152 | tf_op jit(solution)/shard_map/all_to_all | solution.py:213
  161.0 28.7 %collective-permute-start.5 = (f32[8,512]{1,0:T(8,128)S(1)}, f32[8,512]{1,0:T(8,128)S(1)}, u32[]{:S(2)}, u32[]{:S(2)}) collective-permute-start(f32[8,512]{1,0:T(8,128)S(1)} %convert_reduce_fusion), channel_id=1, source_target_pairs={{0,8},{2,10},{4,12},{6,14},{8,0},{10,2},{12,4},{14,6},{1,9},{3,11}... | collective-permute-start | bytes 49160 | tf_op jit(solution)/shard_map/ppermute | solution.py:226
  189.8 5.4 %collective-permute-start.6 = (f32[8,512]{1,0:T(8,128)S(1)}, f32[8,512]{1,0:T(8,128)S(1)}, u32[]{:S(2)}, u32[]{:S(2)}) collective-permute-start(f32[8,512]{1,0:T(8,128)S(1)} %add.74), channel_id=1, source_target_pairs={{0,4},{2,6},{4,0},{6,2},{8,12},{10,14},{12,8},{14,10},{1,5},{3,7},... | collective-permute-start | bytes 49160 | tf_op jit(solution)/shard_map/ppermute | solution.py:226
  195.1 4.5 %collective-permute-start.7 = (f32[8,512]{1,0:T(8,128)S(1)}, f32[8,512]{1,0:T(8,128)S(1)}, u32[]{:S(2)}, u32[]{:S(2)}) collective-permute-start(f32[8,512]{1,0:T(8,128)S(1)} %add.75), channel_id=1, source_target_pairs={{0,2},{2,0},{4,6},{6,4},{8,10},{10,8},{12,14},{14,12},{1,3},{3,1},... | collective-permute-start | bytes 49160 | tf_op jit(solution)/shard_map/ppermute | solution.py:226
  199.6 6.3 %collective-permute-start.8 = (f32[8,512]{1,0:T(8,128)S(1)}, f32[8,512]{1,0:T(8,128)S(1)}, u32[]{:S(2)}, u32[]{:S(2)}) collective-permute-start(f32[8,512]{1,0:T(8,128)S(1)} %add.76), channel_id=1, source_target_pairs={{0,1},{1,0},{2,3},{3,2},{4,5},{5,4},{6,7},{7,6},{8,9},{9,8},{10,11... | collective-permute-start | bytes 49160 | tf_op jit(solution)/shard_map/ppermute | solution.py:221
  222.3 3.1 %collective-permute-start.9 = (bf16[256,128]{1,0:T(8,128)(2,1)S(1)}, bf16[256,128]{1,0:T(8,128)(2,1)S(1)}, u32[]{:S(2)}, u32[]{:S(2)}) collective-permute-start(bf16[256,128]{1,0:T(8,128)(2,1)S(1)} %dynamic-slice_convert_fusion), channel_id=1, source_target_pairs={{0,1},{1,0},{2,3},{3,2},{4,5},{5,4},{6,7},{7,6},{8,9},{9,8},{10,11... | collective-permute-start | bytes 196616 | tf_op jit(solution)/shard_map/ppermute | solution.py:221
  226.6 18.7 %all-to-all-start.5 = ((bf16[32,20,256]{2,1,0:T(8,128)(2,1)}), bf16[32,20,256]{2,1,0:T(8,128)(2,1)S(1)}, u32[]{:S(2)}, u32[]{:S(2)}) async-start(bf16[32,20,256]{2,1,0:T(8,128)(2,1)} %pad_maximum_fusion), calls=%async_computation.5 | async-start | bytes 786432 | tf_op jit(solution)/shard_map/all_to_all | solution.py:200
  (3 other events, 2.5 us)

commit v7 on v6

--- a/solution.py
+++ b/solution.py
@@ -7,7 +7,7 @@
 
 MIRR = 62
 LATE = 64
-UNROLL = 8
+UNROLL = 32
 ACCS = 8
 CHUNK = 128
 WINDOW = 1024
@@ -59,7 +59,7 @@
 
 def edge_kernel(bounds_ref, words_ref, table_ref, out_ref, words, table, *rest):
     accs, sems = rest[:-1], rest[-1]
-    rows, width = table_ref.shape
+    rows, width = table.shape
     own = out_ref.shape[0]
     lists = sems.shape[0]
     length = words.shape[0] // lists
@@ -76,12 +76,13 @@
     for m in range(lists):
         windows(m, lambda copy: copy.start())
 
-    def load(i, _):
-        span = pl.ds(pl.multiple_of(i * CHUNK, CHUNK), CHUNK)
-        table[span, :] = table_ref[span, :].astype(jnp.float32)
+    def load(m, _):
+        for at in range(0, rows // lists, CHUNK):
+            span = pl.ds(pl.multiple_of(m * (rows // lists) + at, CHUNK), CHUNK)
+            table[span, :] = table_ref[m, pl.ds(at, CHUNK), :].astype(jnp.float32)
         return 0
 
-    lax.fori_loop(0, rows // CHUNK, load, 0)
+    lax.fori_loop(0, lists, load, 0)
 
     def clear(i, _):
         span = pl.ds(pl.multiple_of(i * CHUNK, CHUNK), CHUNK)
@@ -107,19 +108,17 @@
     for m in range(lists):
         windows(m, lambda copy: copy.wait())
         low, high = bounds_ref[0, m], bounds_ref[1, m]
-        blocks = (high - low) // UNROLL
-
-        def block(i, _):
-            for group in range(UNROLL // ACCS):
-                add(m * length + low + i * UNROLL + group * ACCS, ACCS)
-            return 0
-
-        def single(i, _):
-            add(m * length + i, 1)
-            return 0
-
-        lax.fori_loop(0, blocks, block, 0)
-        lax.fori_loop(low + blocks * UNROLL, high, single, 0)
+        done = low
+        for count in (UNROLL, ACCS, 1):
+
+            def block(i, _):
+                for group in range(0, count, ACCS):
+                    add(m * length + done + i * count + group, min(count, ACCS))
+                return 0
+
+            blocks = (high - done) // count
+            lax.fori_loop(0, blocks, block, 0)
+            done = done + blocks * count
 
     def store(i, _):
         span = pl.ds(pl.multiple_of(i * CHUNK, CHUNK), CHUNK)
@@ -132,10 +131,9 @@
     lax.fori_loop(0, own // CHUNK, store, 0)
 
 
-def edge_sums(bounds, words, table):
-    rows, width = table.shape
-    lists = bounds.shape[1]
-    own = 2 * (rows // lists)
+def edge_sums(bounds, words, table, own):
+    lists, _, width = table.shape
+    rows = lists * (own // 2)
     vmem = pl.BlockSpec(memory_space=pltpu.VMEM)
     return pl.pallas_call(
         edge_kernel,
@@ -212,26 +210,29 @@
     def over_member(blocks):
         return lax.all_to_all(blocks, member, split_axis=0, concat_axis=0, tiled=True)
 
-    def gather(values):
+    def gather(values, share=None):
         halves = jnp.stack([values[:, :half], values[:, half:]])
         every = jnp.broadcast_to(halves[None], (members // 2,) + halves.shape)
-        return over_member(every.reshape(members, rows, half)).reshape(-1, half)
+        every = every.reshape(members, rows, half)
+        if share is not None:
+            share = jnp.broadcast_to(share[None], (members,) + share.shape)
+            every = jnp.concatenate([every, share], axis=1)
+        return over_member(every)
 
     def twin(values):
         return lax.ppermute(values, "core", [(0, 1), (1, 0)])
 
-    def spread(values, combine):
+    def spread(values):
         bit = chips // 2
         while bit:
             theirs = lax.ppermute(values, "y", [(y, y ^ bit) for y in range(chips)])
-            values = combine(values, theirs)
+            values = jnp.concatenate([values, theirs], axis=1)
             bit //= 2
-        return combine(values, twin(values))
+        return jnp.concatenate([values, twin(values)], axis=1)
 
     def edge_lists(places, takes):
         words = jnp.where(places >= 0, (places << 16) | takes, part_rows << 16)
-        words = sort_lists(words.reshape(2, -1, 128))
-        words = spread(words, lambda mine, theirs: jnp.concatenate([mine, theirs], axis=1))
+        words = spread(sort_lists(words.reshape(2, -1, 128)))
         lists = words.reshape(2, members, -1)
         bounds = jnp.stack(
             [
@@ -243,7 +244,7 @@
         return [(bounds[n], words[n].reshape(-1)) for n in range(2)]
 
     def row_sums(lists, table):
-        block = edge_sums(*lists, table)
+        block = edge_sums(*lists, table, 2 * rows)
         mine = lax.dynamic_slice_in_dim(block, core * rows, rows, 0)
         other = lax.dynamic_slice_in_dim(block, (1 - core) * rows, rows, 0)
         other = twin(other.astype(bf16)).astype(f32)
@@ -291,16 +292,13 @@
     moved = over_dom(jnp.concatenate([slots, share], axis=1))
     arrived = moved[:, :cap]
     late_rows = at_mirrors(arrived[:, :, :width], grad_mean)
-    table = gather(jnp.concatenate([grad_mean[:early], late_rows], axis=0))
+    share = jnp.sum(moved[:, cap:].astype(f32), axis=0).astype(bf16).reshape(-1, half)
+    table = gather(jnp.concatenate([grad_mean[:early], late_rows], axis=0), share)
     activated_late = at_mirrors(arrived[:, :, width:], activated)
     activated = jnp.concatenate([activated[:early], activated_late], axis=0)
 
-    weight_sum = spread(
-        jnp.sum(moved[:, cap:].astype(f32), axis=0), lambda mine, theirs: mine + theirs
-    )
-    share = weight_sum.astype(bf16).reshape(-1, width)
+    share = jnp.sum(table[:, rows:].astype(f32), axis=0).astype(bf16).reshape(-1, width)
     share = jnp.broadcast_to(share[None], (dom_count,) + share.shape)
-    table, share = lax.optimization_barrier((table, share))
     totals = row_sums(by_src, table)
     moved = over_dom(jnp.concatenate([mirror_slots(totals), share], axis=1))
     weight_sums = moved[:, cap:].reshape(-1, 2 * width).astype(f32)

time: 250 us -> 227 us (0.908)
  blocking collectives: 0 us -> 38.5 us
  starting transfers between devices: 92.2 us -> 64 us
  waiting for transfers between devices: 97.7 us -> 70.7 us
  Pallas kernels: 38.5 us -> 31.7 us
    all_to_all x0 -> x1, blocking collectives: none -> 38.5 us  [over_member(): lax.all_to_all(blocks, member, split_axis=0, concat_axis=0, tiled=True)]
    ppermute x6 -> x3, waiting for transfers between devices: 34.7 us -> 7.92 us  [spread(): theirs = lax.ppermute(values, 'y', [(y, y ^ bit) for y in range(chips)])]
    ppermute x6 -> x3, starting transfers between devices: 24.6 us -> 12.7 us  [spread(): theirs = lax.ppermute(values, 'y', [(y, y ^ bit) for y in range(chips)])]
    all_to_all x2 -> x1, starting transfers between devices: 13.4 us -> 3.55 us  [over_member(): lax.all_to_all(blocks, member, split_axis=0, concat_axis=0, tiled=True)]
    pallas_call x2, Pallas kernels: 32.3 us -> 25.6 us  [edge_sums(): pl.pallas_call(edge_kernel, out_shape=jax.ShapeDtypeStruct((own, width),...]
    ppermute x4 -> x3, starting transfers between devices: 14.8 us -> 8.99 us  [twin(): return lax.ppermute(values, 'core', [(0, 1), (1, 0)])]
    all_to_all x2 -> x1, waiting for transfers between devices: 27 us -> 27 us  [over_member(): lax.all_to_all(blocks, member, split_axis=0, concat_axis=0, tiled=True)]
  transfers between devices with their start and end apart: 16 -> 11, of which waited for: 12 -> 8; matrix products, arithmetic and copies ran while one was open for 2% -> 3% of each run, Pallas kernels for 0% -> 0%
where the time goes in v7:
time: 227 us; the launch traced here: 224 us
  waiting for transfers between devices  70.7 us (31%)
  starting transfers between devices  64 us (28%)
  blocking collectives  38.5 us (17%)
  Pallas kernels  31.7 us (14%)
  local copies, waits for them, and re-layouts  6.22 us (3%)
  matrix products  6.14 us (3%)
  other arithmetic  5.73 us (3%)
    all_to_all x4, starting transfers between devices, over_dom(): return lax.all_to_all(slots, 'dom', split_axis=0, concat_axis=0, tiled=True)  38.8 us
    all_to_all x1, blocking collectives, over_member(): lax.all_to_all(blocks, member, split_axis=0, concat_axis=0, tiled=True)  38.5 us
    all_to_all x4, waiting for transfers between devices, over_dom(): return lax.all_to_all(slots, 'dom', split_axis=0, concat_axis=0, tiled=True)  33.5 us
    all_to_all x1, waiting for transfers between devices, over_member(): lax.all_to_all(blocks, member, split_axis=0, concat_axis=0, tiled=True)  27 us
    pallas_call x2, Pallas kernels, edge_sums(): pl.pallas_call(edge_kernel, out_shape=jax.ShapeDtypeStruct((own, width),...  25.6 us
    ppermute x3, starting transfers between devices, spread(): theirs = lax.ppermute(values, 'y', [(y, y ^ bit) for y in range(chips)])  12.7 us
    ppermute x3, starting transfers between devices, twin(): return lax.ppermute(values, 'core', [(0, 1), (1, 0)])  8.99 us
    ppermute x3, waiting for transfers between devices, spread(): theirs = lax.ppermute(values, 'y', [(y, y ^ bit) for y in range(chips)])  7.92 us
  transfers between devices with their start and end apart: 11, of which 8 were waited for; matrix products, arithmetic and copies ran while one was open for 3% of the time, Pallas kernels for 0%

profile of v7, /device:TPU:1, one launch (start us, length us, event | category | flops | bytes accessed | tf_op | source)
XLA Modules:
  0.0 224.4 jit_solution(14901923371489420285)
XLA Ops:
  3.4 1.4 fusion.29.words_ref
  4.8 6.1 %sort_lists.1 = s32[2,32,128]{2,1,0:T(8,128)} custom-call(s32[2,32,128]{2,1,0:T(8,128)} %fusion.29.words_ref), custom_call_target="tpu_custom_call" | custom-call | flops 8192000 | bytes 65536 | tf_op jit(solution)/shard_map/sort_lists/pallas_call | solution.py:48
  10.9 8.4 %collective-permute-start = (s32[2,32,128]{2,1,0:T(8,128)}, s32[2,32,128]{2,1,0:T(8,128)S(1)}, u32[]{:S(2)}, u32[]{:S(2)}) collective-permute-start(s32[2,32,128]{2,1,0:T(8,128)} %sort_lists.1), channel_id=1, source_target_pairs={{0,8},{2,10},{4,12},{6,14},{8,0},{10,2},{12,4},{14,6},{1,9},{3,11}... | collective-permute-start | bytes 98312 | tf_op jit(solution)/shard_map/ppermute | solution.py:228
  19.3 12.9 %all-to-all-start = ((bf16[32,4,256]{2,1,0:T(4,128)(2,1)}), bf16[32,4,256]{2,1,0:T(4,128)(2,1)S(1)}, u32[]{:S(2)}, u32[]{:S(2)}) async-start(bf16[32,4,256]{2,1,0:T(4,128)(2,1)} %reshape.89), calls=%async_computation | async-start | bytes 131072 | tf_op jit(solution)/shard_map/all_to_all | solution.py:198
  35.2 2.4 %collective-permute-start.1 = (s32[2,64,128]{2,1,0:T(8,128)S(1)}, s32[2,64,128]{2,1,0:T(8,128)S(1)}, u32[]{:S(2)}, u32[]{:S(2)}) collective-permute-start(s32[2,64,128]{2,1,0:T(8,128)S(1)} %pad_add_fusion.2), channel_id=1, source_target_pairs={{0,4},{2,6},{4,0},{6,2},{8,12},{10,14},{12,8},{14,10},{1,5},{3,7},... | collective-permute-start | bytes 196616 | tf_op jit(solution)/shard_map/ppermute | solution.py:228
  37.6 4.5 %collective-permute-done.1 = s32[2,64,128]{2,1,0:T(8,128)S(1)} collective-permute-done((s32[2,64,128]{2,1,0:T(8,128)S(1)}, s32[2,64,128]{2,1,0:T(8,128)S(1)}, u32[]{:S(2)}, u32[]{:S(2)}) %collective-permute-start.1) | collective-permute-done | bytes 65568 | tf_op jit(solution)/shard_map/ppermute | solution.py:228
  42.1 1.9 collective-permute-start.2
  44.3 3.5 %collective-permute-done.2 = s32[2,128,128]{2,1,0:T(8,128)S(1)} collective-permute-done((s32[2,128,128]{2,1,0:T(8,128)S(1)}, s32[2,128,128]{2,1,0:T(8,128)S(1)}, u32[]{:S(2)}, u32[]{:S(2)}) %collective-permute-start.2) | collective-permute-done | bytes 131104 | tf_op jit(solution)/shard_map/ppermute | solution.py:228
  47.8 5.1 %collective-permute-start.3 = (s32[2,256,128]{2,1,0:T(8,128)S(1)}, s32[2,256,128]{2,1,0:T(8,128)S(1)}, u32[]{:S(2)}, u32[]{:S(2)}) collective-permute-start(s32[2,256,128]{2,1,0:T(8,128)S(1)} %pad_add_fusion), channel_id=1, source_target_pairs={{0,1},{1,0},{2,3},{3,2},{4,5},{5,4},{6,7},{7,6},{8,9},{9,8},{10,11... | collective-permute-start | bytes 786440 | tf_op jit(solution)/shard_map/ppermute | solution.py:223
  53.0 1.2 broadcast_in_dim.76
  54.2 3.5 %all-to-all-start.1 = ((bf16[16,256,128]{2,1,0:T(8,128)(2,1)}), bf16[16,256,128]{2,1,0:T(8,128)(2,1)S(1)}, u32[]{:S(2)}, u32[]{:S(2)}) async-start(bf16[16,256,128]{2,1,0:T(8,128)(2,1)} %bitcast.9), calls=%async_computation.1 | async-start | bytes 2097152 | tf_op jit(solution)/shard_map/all_to_all | solution.py:211
  58.6 27.0 %all-to-all-done.1.table_ref = bf16[16,256,128]{2,1,0:T(8,128)(2,1)S(1)} async-done(((bf16[16,256,128]{2,1,0:T(8,128)(2,1)}), bf16[16,256,128]{2,1,0:T(8,128)(2,1)S(1)}, u32[]{:S(2)}, u32[]{:S(2)}) %all-to-all-start.1) | async-done | bytes 1048608 | tf_op jit(solution)/shard_map/all_to_all | solution.py:211
  85.6 12.7 %edge_sums.2 = f32[512,128]{1,0:T(8,128)S(1)} custom-call(s32[2,16]{1,0:T(2,128)S(1)} %bitcast.52, s32[65536]{0:T(1024)S(1)} %get-tuple-element.17.words_ref, bf16[16,256,128]{2,1,0:T(8,128)(2,1)S(1)} %all-to-all-done.1.table_ref), custom_call_target="tpu_custom_call" | custom-call | flops 2097152 | bytes 2097152 | tf_op jit(solution)/shard_map/edge_sums/pallas_call | solution.py:138
  98.3 1.9 collective-permute-start.4
  100.3 1.2 collective-permute-done.4
  102.4 16.0 %all-to-all-start.2 = ((bf16[32,4,256]{2,1,0:T(4,128)(2,1)}), bf16[32,4,256]{2,1,0:T(4,128)(2,1)S(1)}, u32[]{:S(2)}, u32[]{:S(2)}) async-start(bf16[32,4,256]{2,1,0:T(4,128)(2,1)} %reshape.92), calls=%async_computation.2 | async-start | bytes 131072 | tf_op jit(solution)/shard_map/all_to_all | solution.py:198
  118.5 8.8 %all-to-all-done.2 = bf16[32,4,256]{2,1,0:T(4,128)(2,1)S(1)} async-done(((bf16[32,4,256]{2,1,0:T(4,128)(2,1)}), bf16[32,4,256]{2,1,0:T(4,128)(2,1)S(1)}, u32[]{:S(2)}, u32[]{:S(2)}) %all-to-all-start.2) | async-done | bytes 65568 | tf_op jit(solution)/shard_map/all_to_all | solution.py:198
  129.9 3.9 %all-to-all-start.3 = ((bf16[32,12,512]{2,1,0:T(8,128)(2,1)}), bf16[32,12,512]{2,1,0:T(8,128)(2,1)S(1)}, u32[]{:S(2)}, u32[]{:S(2)}) async-start(bf16[32,12,512]{2,1,0:T(8,128)(2,1)} %maximum_maximum_fusion), calls=%async_computation.3 | async-start | bytes 1048576 | tf_op jit(solution)/shard_map/all_to_all | solution.py:198
  133.8 13.7 %all-to-all-done.3 = bf16[32,12,512]{2,1,0:T(8,128)(2,1)S(1)} async-done(((bf16[32,12,512]{2,1,0:T(8,128)(2,1)}), bf16[32,12,512]{2,1,0:T(8,128)(2,1)S(1)}, u32[]{:S(2)}, u32[]{:S(2)}) %all-to-all-start.3) | async-done | bytes 393248 | tf_op jit(solution)/shard_map/all_to_all | solution.py:198
  148.3 38.5 %all_to_all.30.table_ref = bf16[16,288,128]{2,1,0:T(8,128)(2,1)S(1)} all-to-all(bf16[16,288,128]{2,1,0:T(8,128)(2,1)S(1)} %pad_maximum_fusion), channel_id=1, replica_groups=mesh['dom'=32,'y'=8,'core'=2] {'y','core'}, dimensions={0} | all-to-all | bytes 2359296 | tf_op jit(solution)/shard_map/all_to_all | solution.py:211
  186.9 12.9 %edge_sums.3 = f32[512,128]{1,0:T(8,128)S(1)} custom-call(s32[2,16]{1,0:T(2,128)S(1)} %bitcast.51, s32[65536]{0:T(1024)S(1)} %get-tuple-element.16.words_ref, bf16[16,288,128]{2,1,0:T(8,128)(2,1)S(1)} %all_to_all.30.table_ref), custom_call_target="tpu_custom_call" | custom-call | flops 2097152 | bytes 2097152 | tf_op jit(solution)/shard_map/edge_sums/pallas_call | solution.py:138
  199.8 1.9 collective-permute-start.5
  204.2 5.9 %all-to-all-start.5 = ((bf16[32,20,256]{2,1,0:T(8,128)(2,1)}), bf16[32,20,256]{2,1,0:T(8,128)(2,1)S(1)}, u32[]{:S(2)}, u32[]{:S(2)}) async-start(bf16[32,20,256]{2,1,0:T(8,128)(2,1)} %pad_maximum_fusion.1), calls=%async_computation.5 | async-start | bytes 786432 | tf_op jit(solution)/shard_map/all_to_all | solution.py:198
  211.4 10.9 %all-to-all-done.5 = bf16[32,20,256]{2,1,0:T(8,128)(2,1)S(1)} async-done(((bf16[32,20,256]{2,1,0:T(8,128)(2,1)}), bf16[32,20,256]{2,1,0:T(8,128)(2,1)S(1)}, u32[]{:S(2)}, u32[]{:S(2)}) %all-to-all-start.5) | async-done | bytes 327712 | tf_op jit(solution)/shard_map/all_to_all | solution.py:198
  (97 shorter events, 16.6 us)
Async XLA Ops:
  0.6 127.0 %copy-start = (bf16[256,256]{1,0:T(8,128)(2,1)S(1)}, bf16[256,256]{1,0:T(8,128)(2,1)}, u32[]{:S(2)}) copy-start(bf16[256,256]{1,0:T(8,128)(2,1)} %param.17) | copy-start | bytes 393220
  0.6 43.4 %copy-start.1 = (bf16[256,256]{1,0:T(8,128)(2,1)S(1)}, bf16[256,256]{1,0:T(8,128)(2,1)}, u32[]{:S(2)}) copy-start(bf16[256,256]{1,0:T(8,128)(2,1)} %param.9) | copy-start | bytes 393220
  0.7 33.5 %copy-start.4 = (s32[1,1,32,4]{2,3,1,0:T(4,128)S(1)}, s32[1,1,32,4]{2,3,1,0:T(4,128)}, u32[]{:S(2)}) copy-start(s32[1,1,32,4]{2,3,1,0:T(4,128)} %param.13) | copy-start | bytes 1540
  10.9 31.1 %copy-start.2 = (s32[2,32,128]{2,1,0:T(8,128)S(1)}, s32[2,32,128]{2,1,0:T(8,128)}, u32[]{:S(2)}) copy-start(s32[2,32,128]{2,1,0:T(8,128)} %sort_lists.1) | copy-start | bytes 98308
  10.9 42.0 %slice-start = ((bf16[256,256]{1,0:T(8,128)(2,1)}), bf16[192,256]{1,0:T(8,128)(2,1)S(1)}, s32[]{:S(2)}) async-start(bf16[256,256]{1,0:T(8,128)(2,1)} %param.9), calls=%async_computation.6 | async-start | bytes 196608 | tf_op jit(solution)/shard_map/slice | solution.py:270
  10.9 23.5 %collective-permute-start = (s32[2,32,128]{2,1,0:T(8,128)}, s32[2,32,128]{2,1,0:T(8,128)S(1)}, u32[]{:S(2)}, u32[]{:S(2)}) collective-permute-start(s32[2,32,128]{2,1,0:T(8,128)} %sort_lists.1), channel_id=1, source_target_pairs={{0,8},{2,10},{4,12},{6,14},{8,0},{10,2},{12,4},{14,6},{1,9},{3,11}... | collective-permute-start | bytes 98312 | tf_op jit(solution)/shard_map/ppermute | solution.py:228
  19.3 24.7 %all-to-all-start = ((bf16[32,4,256]{2,1,0:T(4,128)(2,1)}), bf16[32,4,256]{2,1,0:T(4,128)(2,1)S(1)}, u32[]{:S(2)}, u32[]{:S(2)}) async-start(bf16[32,4,256]{2,1,0:T(4,128)(2,1)} %reshape.89), calls=%async_computation | async-start | bytes 131072 | tf_op jit(solution)/shard_map/all_to_all | solution.py:198
  35.2 6.9 %collective-permute-start.1 = (s32[2,64,128]{2,1,0:T(8,128)S(1)}, s32[2,64,128]{2,1,0:T(8,128)S(1)}, u32[]{:S(2)}, u32[]{:S(2)}) collective-permute-start(s32[2,64,128]{2,1,0:T(8,128)S(1)} %pad_add_fusion.2), channel_id=1, source_target_pairs={{0,4},{2,6},{4,0},{6,2},{8,12},{10,14},{12,8},{14,10},{1,5},{3,7},... | collective-permute-start | bytes 196616 | tf_op jit(solution)/shard_map/ppermute | solution.py:228
  42.1 5.7 %collective-permute-start.2 = (s32[2,128,128]{2,1,0:T(8,128)S(1)}, s32[2,128,128]{2,1,0:T(8,128)S(1)}, u32[]{:S(2)}, u32[]{:S(2)}) collective-permute-start(s32[2,128,128]{2,1,0:T(8,128)S(1)} %pad_add_fusion.1), channel_id=1, source_target_pairs={{0,2},{2,0},{4,6},{6,4},{8,10},{10,8},{12,14},{14,12},{1,3},{3,1},... | collective-permute-start | bytes 393224 | tf_op jit(solution)/shard_map/ppermute | solution.py:228
  47.8 10.0 %collective-permute-start.3 = (s32[2,256,128]{2,1,0:T(8,128)S(1)}, s32[2,256,128]{2,1,0:T(8,128)S(1)}, u32[]{:S(2)}, u32[]{:S(2)}) collective-permute-start(s32[2,256,128]{2,1,0:T(8,128)S(1)} %pad_add_fusion), channel_id=1, source_target_pairs={{0,1},{1,0},{2,3},{3,2},{4,5},{5,4},{6,7},{7,6},{8,9},{9,8},{10,11... | collective-permute-start | bytes 786440 | tf_op jit(solution)/shard_map/ppermute | solution.py:223
  54.2 31.4 %all-to-all-start.1 = ((bf16[16,256,128]{2,1,0:T(8,128)(2,1)}), bf16[16,256,128]{2,1,0:T(8,128)(2,1)S(1)}, u32[]{:S(2)}, u32[]{:S(2)}) async-start(bf16[16,256,128]{2,1,0:T(8,128)(2,1)} %bitcast.9), calls=%async_computation.1 | async-start | bytes 2097152 | tf_op jit(solution)/shard_map/all_to_all | solution.py:211
  85.6 32.8 %copy-start.5 = (s32[1,1,256]{2,1,0:T(1,128)S(1)}, s32[1,1,256]{2,1,0:T(1,128)}, u32[]{:S(2)}) copy-start(s32[1,1,256]{2,1,0:T(1,128)} %param.15) | copy-start | bytes 3076
  98.3 3.1 %collective-permute-start.4 = (bf16[256,128]{1,0:T(8,128)(2,1)S(1)}, bf16[256,128]{1,0:T(8,128)(2,1)S(1)}, u32[]{:S(2)}, u32[]{:S(2)}) collective-permute-start(bf16[256,128]{1,0:T(8,128)(2,1)S(1)} %dynamic-slice_convert_fusion.1), channel_id=1, source_target_pairs={{0,1},{1,0},{2,3},{3,2},{4,5},{5,4},{6,7},{7,6},{8,9},{9,8},{10,11... | collective-permute-start | bytes 196616 | tf_op jit(solution)/shard_map/ppermute | solution.py:223
  100.3 27.4 %copy-start.6 = (bf16[256,256]{1,0:T(8,128)(2,1)S(1)}, bf16[256,256]{1,0:T(8,128)(2,1)}, u32[]{:S(2)}) copy-start(bf16[256,256]{1,0:T(8,128)(2,1)} %param.10) | copy-start | bytes 393220
  102.4 24.9 %all-to-all-start.2 = ((bf16[32,4,256]{2,1,0:T(4,128)(2,1)}), bf16[32,4,256]{2,1,0:T(4,128)(2,1)S(1)}, u32[]{:S(2)}, u32[]{:S(2)}) async-start(bf16[32,4,256]{2,1,0:T(4,128)(2,1)} %reshape.92), calls=%async_computation.2 | async-start | bytes 131072 | tf_op jit(solution)/shard_map/all_to_all | solution.py:198
  129.9 17.6 %all-to-all-start.3 = ((bf16[32,12,512]{2,1,0:T(8,128)(2,1)}), bf16[32,12,512]{2,1,0:T(8,128)(2,1)S(1)}, u32[]{:S(2)}, u32[]{:S(2)}) async-start(bf16[32,12,512]{2,1,0:T(8,128)(2,1)} %maximum_maximum_fusion), calls=%async_computation.3 | async-start | bytes 1048576 | tf_op jit(solution)/shard_map/all_to_all | solution.py:198
  199.8 3.1 %collective-permute-start.5 = (bf16[256,128]{1,0:T(8,128)(2,1)S(1)}, bf16[256,128]{1,0:T(8,128)(2,1)S(1)}, u32[]{:S(2)}, u32[]{:S(2)}) collective-permute-start(bf16[256,128]{1,0:T(8,128)(2,1)S(1)} %dynamic-slice_convert_fusion), channel_id=1, source_target_pairs={{0,1},{1,0},{2,3},{3,2},{4,5},{5,4},{6,7},{7,6},{8,9},{9,8},{10,11... | collective-permute-start | bytes 196616 | tf_op jit(solution)/shard_map/ppermute | solution.py:223
  203.0 7.1 %copy-start.3 = (bf16[256,256]{1,0:T(8,128)(2,1)S(1)}, bf16[256,256]{1,0:T(8,128)(2,1)}, u32[]{:S(2)}) copy-start(bf16[256,256]{1,0:T(8,128)(2,1)} %param.16) | copy-start | bytes 393220
  204.2 18.1 %all-to-all-start.5 = ((bf16[32,20,256]{2,1,0:T(8,128)(2,1)}), bf16[32,20,256]{2,1,0:T(8,128)(2,1)S(1)}, u32[]{:S(2)}, u32[]{:S(2)}) async-start(bf16[32,20,256]{2,1,0:T(8,128)(2,1)} %pad_maximum_fusion.1), calls=%async_computation.5 | async-start | bytes 786432 | tf_op jit(solution)/shard_map/all_to_all | solution.py:198

commit v8 on v7

--- a/solution.py
+++ b/solution.py
@@ -100,7 +100,7 @@
         for k in range(count):
             word = words[base + k]
             takes.append(word & 0xFFFF)
-            places.append((word >> 16) & (own - 1))
+            places.append(word >> 16)
         sums = [acc_rows[k][places[k]] + table_rows[takes[k]] for k in range(count)]
         for k in range(count):
             acc_rows[k][places[k]] = sums[k]
@@ -210,29 +210,27 @@
     def over_member(blocks):
         return lax.all_to_all(blocks, member, split_axis=0, concat_axis=0, tiled=True)
 
-    def gather(values, share=None):
+    def copies(values, share=None):
         halves = jnp.stack([values[:, :half], values[:, half:]])
         every = jnp.broadcast_to(halves[None], (members // 2,) + halves.shape)
         every = every.reshape(members, rows, half)
         if share is not None:
             share = jnp.broadcast_to(share[None], (members,) + share.shape)
             every = jnp.concatenate([every, share], axis=1)
-        return over_member(every)
+        return every
 
     def twin(values):
         return lax.ppermute(values, "core", [(0, 1), (1, 0)])
 
-    def spread(values):
-        bit = chips // 2
-        while bit:
-            theirs = lax.ppermute(values, "y", [(y, y ^ bit) for y in range(chips)])
-            values = jnp.concatenate([values, theirs], axis=1)
-            bit //= 2
-        return jnp.concatenate([values, twin(values)], axis=1)
-
-    def edge_lists(places, takes):
+    def with_theirs(words, bit):
+        theirs = lax.ppermute(words, "y", [(y, y ^ bit) for y in range(chips)])
+        return jnp.concatenate([words, theirs], axis=1)
+
+    def own_lists(places, takes):
         words = jnp.where(places >= 0, (places << 16) | takes, part_rows << 16)
-        words = spread(sort_lists(words.reshape(2, -1, 128)))
+        return sort_lists(words.reshape(2, -1, 128))
+
+    def runs(words):
         lists = words.reshape(2, members, -1)
         bounds = jnp.stack(
             [
@@ -241,6 +239,7 @@
             ],
             axis=1,
         )
+        words = words & ((2 * rows - 1) << 16 | 0xFFFF)
         return [(bounds[n], words[n].reshape(-1)) for n in range(2)]
 
     def row_sums(lists, table):
@@ -265,9 +264,17 @@
 
     slots, src, dst = lax.optimization_barrier((from_masters(features), edge_src, edge_dst))
     src, dst = src.reshape(1, -1), dst.reshape(1, -1)
-    by_dst, by_src = edge_lists(jnp.concatenate([dst, src]), jnp.concatenate([src, dst]))
+    words = own_lists(jnp.concatenate([dst, src]), jnp.concatenate([src, dst]))
+    bit = chips // 2
+    while bit > 1:
+        words = with_theirs(words, bit)
+        bit //= 2
     late_rows = at_mirrors(over_dom(slots), features)
-    table = gather(jnp.concatenate([features[:early], late_rows], axis=0))
+    every = copies(jnp.concatenate([features[:early], late_rows], axis=0))
+    every, words = lax.optimization_barrier((every, words))
+    table = over_member(every)
+    words = with_theirs(words, 1)
+    by_dst, by_src = runs(jnp.concatenate([words, twin(words)], axis=1))
     totals = row_sums(by_dst, table)
     totals = totals + add_at_masters(over_dom(mirror_slots(totals)))
     averaged = (totals / denominator).astype(bf16)
@@ -293,7 +300,7 @@
     arrived = moved[:, :cap]
     late_rows = at_mirrors(arrived[:, :, :width], grad_mean)
     share = jnp.sum(moved[:, cap:].astype(f32), axis=0).astype(bf16).reshape(-1, half)
-    table = gather(jnp.concatenate([grad_mean[:early], late_rows], axis=0), share)
+    table = over_member(copies(jnp.concatenate([grad_mean[:early], late_rows], axis=0), share))
     activated_late = at_mirrors(arrived[:, :, width:], activated)
     activated = jnp.concatenate([activated[:early], activated_late], axis=0)
 

time: 227 us -> 226 us (level)
  blocking collectives: 38.5 us -> 43.4 us
  starting transfers between devices: 64 us -> 59.7 us
    all_to_all x4, starting transfers between devices: 38.8 us -> 33.8 us  [over_dom(): return lax.all_to_all(slots, 'dom', split_axis=0, concat_axis=0, tiled=True)]
    all_to_all x1, blocking collectives: 38.5 us -> 43.4 us  [over_member(): lax.all_to_all(blocks, member, split_axis=0, concat_axis=0, tiled=True)]
  transfers between devices with their start and end apart: 11 -> 11, of which waited for: 8 -> 9; matrix products, arithmetic and copies ran while one was open for 3% -> 2% of each run, Pallas kernels for 0% -> 0%
where the time goes in v8:
time: 226 us; the launch traced here: 223 us
  waiting for transfers between devices  70.2 us (31%)
  starting transfers between devices  59.7 us (26%)
  blocking collectives  43.4 us (19%)
  Pallas kernels  30.6 us (14%)
  other arithmetic  6.5 us (3%)
  local copies, waits for them, and re-layouts  6.13 us (3%)
  matrix products  5.17 us (2%)
    all_to_all x1, blocking collectives, over_member(): lax.all_to_all(blocks, member, split_axis=0, concat_axis=0, tiled=True)  43.4 us
    all_to_all x4, waiting for transfers between devices, over_dom(): return lax.all_to_all(slots, 'dom', split_axis=0, concat_axis=0, tiled=True)  33.9 us
    all_to_all x4, starting transfers between devices, over_dom(): return lax.all_to_all(slots, 'dom', split_axis=0, concat_axis=0, tiled=True)  33.8 us
    all_to_all x1, waiting for transfers between devices, over_member(): lax.all_to_all(blocks, member, split_axis=0, concat_axis=0, tiled=True)  27 us
    pallas_call x2, Pallas kernels, edge_sums(): pl.pallas_call(edge_kernel, out_shape=jax.ShapeDtypeStruct((own, width),...  24.5 us
    ppermute x3, starting transfers between devices, with_theirs(): theirs = lax.ppermute(words, 'y', [(y, y ^ bit) for y in range(chips)])  13 us
    ppermute x3, starting transfers between devices, twin(): return lax.ppermute(values, 'core', [(0, 1), (1, 0)])  9.29 us
    ppermute x3, waiting for transfers between devices, with_theirs(): theirs = lax.ppermute(words, 'y', [(y, y ^ bit) for y in range(chips)])  7 us
  transfers between devices with their start and end apart: 11, of which 9 were waited for; matrix products, arithmetic and copies ran while one was open for 2% of the time, Pallas kernels for 0%

profile of v8, /device:TPU:1, one launch (start us, length us, event | category | flops | bytes accessed | tf_op | source)
XLA Modules:
  0.0 223.0 jit_solution(6192768543997841145)
XLA Ops:
  3.4 1.4 fusion.29.words_ref
  4.8 6.1 %sort_lists.1 = s32[2,32,128]{2,1,0:T(8,128)} custom-call(s32[2,32,128]{2,1,0:T(8,128)} %fusion.29.words_ref), custom_call_target="tpu_custom_call" | custom-call | flops 8192000 | bytes 65536 | tf_op jit(solution)/shard_map/sort_lists/pallas_call | solution.py:48
  10.9 8.3 %collective-permute-start = (s32[2,32,128]{2,1,0:T(8,128)}, s32[2,32,128]{2,1,0:T(8,128)S(1)}, u32[]{:S(2)}, u32[]{:S(2)}) collective-permute-start(s32[2,32,128]{2,1,0:T(8,128)} %sort_lists.1), channel_id=1, source_target_pairs={{0,8},{2,10},{4,12},{6,14},{8,0},{10,2},{12,4},{14,6},{1,9},{3,11}... | collective-permute-start | bytes 98312 | tf_op jit(solution)/shard_map/ppermute | solution.py:226
  19.2 12.9 %all-to-all-start = ((bf16[32,4,256]{2,1,0:T(4,128)(2,1)}), bf16[32,4,256]{2,1,0:T(4,128)(2,1)S(1)}, u32[]{:S(2)}, u32[]{:S(2)}) async-start(bf16[32,4,256]{2,1,0:T(4,128)(2,1)} %reshape.89), calls=%async_computation | async-start | bytes 131072 | tf_op jit(solution)/shard_map/all_to_all | solution.py:198
  32.9 2.4 %collective-permute-start.1 = (s32[2,64,128]{2,1,0:T(8,128)S(1)}, s32[2,64,128]{2,1,0:T(8,128)S(1)}, u32[]{:S(2)}, u32[]{:S(2)}) collective-permute-start(s32[2,64,128]{2,1,0:T(8,128)S(1)} %pad_add_fusion.2), channel_id=1, source_target_pairs={{0,4},{2,6},{4,0},{6,2},{8,12},{10,14},{12,8},{14,10},{1,5},{3,7},... | collective-permute-start | bytes 196616 | tf_op jit(solution)/shard_map/ppermute | solution.py:226
  36.2 3.6 %collective-permute-done.1 = s32[2,64,128]{2,1,0:T(8,128)S(1)} collective-permute-done((s32[2,64,128]{2,1,0:T(8,128)S(1)}, s32[2,64,128]{2,1,0:T(8,128)S(1)}, u32[]{:S(2)}, u32[]{:S(2)}) %collective-permute-start.1) | collective-permute-done | bytes 65568 | tf_op jit(solution)/shard_map/ppermute | solution.py:226
  41.3 1.2 broadcast_in_dim.75
  42.5 2.3 %collective-permute-start.2 = (s32[2,128,128]{2,1,0:T(8,128)S(1)}, s32[2,128,128]{2,1,0:T(8,128)S(1)}, u32[]{:S(2)}, u32[]{:S(2)}) collective-permute-start(s32[2,128,128]{2,1,0:T(8,128)S(1)} %pad_add_fusion.1), channel_id=1, source_target_pairs={{0,2},{2,0},{4,6},{6,4},{8,10},{10,8},{12,14},{14,12},{1,3},{3,1},... | collective-permute-start | bytes 393224 | tf_op jit(solution)/shard_map/ppermute | solution.py:226
  44.8 3.4 %collective-permute-done.2 = s32[2,128,128]{2,1,0:T(8,128)S(1)} collective-permute-done((s32[2,128,128]{2,1,0:T(8,128)S(1)}, s32[2,128,128]{2,1,0:T(8,128)S(1)}, u32[]{:S(2)}, u32[]{:S(2)}) %collective-permute-start.2) | collective-permute-done | bytes 131104 | tf_op jit(solution)/shard_map/ppermute | solution.py:226
  48.2 5.4 %collective-permute-start.3 = (s32[2,256,128]{2,1,0:T(8,128)S(1)}, s32[2,256,128]{2,1,0:T(8,128)S(1)}, u32[]{:S(2)}, u32[]{:S(2)}) collective-permute-start(s32[2,256,128]{2,1,0:T(8,128)S(1)} %pad_add_fusion), channel_id=1, source_target_pairs={{0,1},{1,0},{2,3},{3,2},{4,5},{5,4},{6,7},{7,6},{8,9},{9,8},{10,11... | collective-permute-start | bytes 786440 | tf_op jit(solution)/shard_map/ppermute | solution.py:223
  53.9 3.6 %all-to-all-start.1 = ((bf16[16,256,128]{2,1,0:T(8,128)(2,1)}), bf16[16,256,128]{2,1,0:T(8,128)(2,1)S(1)}, u32[]{:S(2)}, u32[]{:S(2)}) async-start(bf16[16,256,128]{2,1,0:T(8,128)(2,1)} %bitcast.3), calls=%async_computation.1 | async-start | bytes 2097152 | tf_op jit(solution)/shard_map/all_to_all | solution.py:211
  58.4 27.0 %all-to-all-done.1.table_ref = bf16[16,256,128]{2,1,0:T(8,128)(2,1)S(1)} async-done(((bf16[16,256,128]{2,1,0:T(8,128)(2,1)}), bf16[16,256,128]{2,1,0:T(8,128)(2,1)S(1)}, u32[]{:S(2)}, u32[]{:S(2)}) %all-to-all-start.1) | async-done | bytes 1048608 | tf_op jit(solution)/shard_map/all_to_all | solution.py:211
  85.4 12.4 %edge_sums.2 = f32[512,128]{1,0:T(8,128)S(1)} custom-call(s32[2,16]{1,0:T(2,128)S(1)} %bitcast.52, s32[65536]{0:T(1024)S(1)} %get-tuple-element.21.words_ref, bf16[16,256,128]{2,1,0:T(8,128)(2,1)S(1)} %all-to-all-done.1.table_ref), custom_call_target="tpu_custom_call" | custom-call | flops 2097152 | bytes 2097152 | tf_op jit(solution)/shard_map/edge_sums/pallas_call | solution.py:138
  97.8 1.9 collective-permute-start.4
  99.7 1.2 collective-permute-done.4
  101.8 10.9 %all-to-all-start.2 = ((bf16[32,4,256]{2,1,0:T(4,128)(2,1)}), bf16[32,4,256]{2,1,0:T(4,128)(2,1)S(1)}, u32[]{:S(2)}, u32[]{:S(2)}) async-start(bf16[32,4,256]{2,1,0:T(4,128)(2,1)} %reshape.92), calls=%async_computation.2 | async-start | bytes 131072 | tf_op jit(solution)/shard_map/all_to_all | solution.py:198
  112.8 8.8 %all-to-all-done.2 = bf16[32,4,256]{2,1,0:T(4,128)(2,1)S(1)} async-done(((bf16[32,4,256]{2,1,0:T(4,128)(2,1)}), bf16[32,4,256]{2,1,0:T(4,128)(2,1)S(1)}, u32[]{:S(2)}, u32[]{:S(2)}) %all-to-all-start.2) | async-done | bytes 65568 | tf_op jit(solution)/shard_map/all_to_all | solution.py:198
  124.2 3.9 %all-to-all-start.3 = ((bf16[32,12,512]{2,1,0:T(8,128)(2,1)}), bf16[32,12,512]{2,1,0:T(8,128)(2,1)S(1)}, u32[]{:S(2)}, u32[]{:S(2)}) async-start(bf16[32,12,512]{2,1,0:T(8,128)(2,1)} %maximum_maximum_fusion), calls=%async_computation.3 | async-start | bytes 1048576 | tf_op jit(solution)/shard_map/all_to_all | solution.py:198
  128.1 13.7 %all-to-all-done.3 = bf16[32,12,512]{2,1,0:T(8,128)(2,1)S(1)} async-done(((bf16[32,12,512]{2,1,0:T(8,128)(2,1)}), bf16[32,12,512]{2,1,0:T(8,128)(2,1)S(1)}, u32[]{:S(2)}, u32[]{:S(2)}) %all-to-all-start.3) | async-done | bytes 393248 | tf_op jit(solution)/shard_map/all_to_all | solution.py:198
  142.6 43.4 %all_to_all.30.table_ref = bf16[16,288,128]{2,1,0:T(8,128)(2,1)S(1)} all-to-all(bf16[16,288,128]{2,1,0:T(8,128)(2,1)S(1)} %pad_maximum_fusion), channel_id=1, replica_groups=mesh['dom'=32,'y'=8,'core'=2] {'y','core'}, dimensions={0} | all-to-all | bytes 2359296 | tf_op jit(solution)/shard_map/all_to_all | solution.py:211
  186.0 12.1 %edge_sums.3 = f32[512,128]{1,0:T(8,128)S(1)} custom-call(s32[2,16]{1,0:T(2,128)S(1)} %bitcast.51, s32[65536]{0:T(1024)S(1)} %get-tuple-element.20.words_ref, bf16[16,288,128]{2,1,0:T(8,128)(2,1)S(1)} %all_to_all.30.table_ref), custom_call_target="tpu_custom_call" | custom-call | flops 2097152 | bytes 2097152 | tf_op jit(solution)/shard_map/edge_sums/pallas_call | solution.py:138
  198.2 1.9 collective-permute-start.5
  202.6 6.2 %all-to-all-start.5 = ((bf16[32,20,256]{2,1,0:T(8,128)(2,1)}), bf16[32,20,256]{2,1,0:T(8,128)(2,1)S(1)}, u32[]{:S(2)}, u32[]{:S(2)}) async-start(bf16[32,20,256]{2,1,0:T(8,128)(2,1)} %pad_maximum_fusion.1), calls=%async_computation.5 | async-start | bytes 786432 | tf_op jit(solution)/shard_map/all_to_all | solution.py:198
  209.9 11.0 %all-to-all-done.5 = bf16[32,20,256]{2,1,0:T(8,128)(2,1)S(1)} async-done(((bf16[32,20,256]{2,1,0:T(8,128)(2,1)}), bf16[32,20,256]{2,1,0:T(8,128)(2,1)S(1)}, u32[]{:S(2)}, u32[]{:S(2)}) %all-to-all-start.5) | async-done | bytes 327712 | tf_op jit(solution)/shard_map/all_to_all | solution.py:198
  (91 shorter events, 16.8 us)
Async XLA Ops:
  0.6 121.3 %copy-start = (bf16[256,256]{1,0:T(8,128)(2,1)S(1)}, bf16[256,256]{1,0:T(8,128)(2,1)}, u32[]{:S(2)}) copy-start(bf16[256,256]{1,0:T(8,128)(2,1)} %param.17) | copy-start | bytes 393220
  0.6 40.4 %copy-start.1 = (bf16[256,256]{1,0:T(8,128)(2,1)S(1)}, bf16[256,256]{1,0:T(8,128)(2,1)}, u32[]{:S(2)}) copy-start(bf16[256,256]{1,0:T(8,128)(2,1)} %param.9) | copy-start | bytes 393220
  0.7 40.6 %slice-start = ((bf16[256,256]{1,0:T(8,128)(2,1)}), bf16[192,256]{1,0:T(8,128)(2,1)S(1)}, s32[]{:S(2)}) async-start(bf16[256,256]{1,0:T(8,128)(2,1)} %param.9), calls=%async_computation.6 | async-start | bytes 196608 | tf_op jit(solution)/shard_map/slice | solution.py:273
  10.9 21.2 %collective-permute-start = (s32[2,32,128]{2,1,0:T(8,128)}, s32[2,32,128]{2,1,0:T(8,128)S(1)}, u32[]{:S(2)}, u32[]{:S(2)}) collective-permute-start(s32[2,32,128]{2,1,0:T(8,128)} %sort_lists.1), channel_id=1, source_target_pairs={{0,8},{2,10},{4,12},{6,14},{8,0},{10,2},{12,4},{14,6},{1,9},{3,11}... | collective-permute-start | bytes 98312 | tf_op jit(solution)/shard_map/ppermute | solution.py:226
  19.2 21.8 %all-to-all-start = ((bf16[32,4,256]{2,1,0:T(4,128)(2,1)}), bf16[32,4,256]{2,1,0:T(4,128)(2,1)S(1)}, u32[]{:S(2)}, u32[]{:S(2)}) async-start(bf16[32,4,256]{2,1,0:T(4,128)(2,1)} %reshape.89), calls=%async_computation | async-start | bytes 131072 | tf_op jit(solution)/shard_map/all_to_all | solution.py:198
  32.9 6.9 %collective-permute-start.1 = (s32[2,64,128]{2,1,0:T(8,128)S(1)}, s32[2,64,128]{2,1,0:T(8,128)S(1)}, u32[]{:S(2)}, u32[]{:S(2)}) collective-permute-start(s32[2,64,128]{2,1,0:T(8,128)S(1)} %pad_add_fusion.2), channel_id=1, source_target_pairs={{0,4},{2,6},{4,0},{6,2},{8,12},{10,14},{12,8},{14,10},{1,5},{3,7},... | collective-permute-start | bytes 196616 | tf_op jit(solution)/shard_map/ppermute | solution.py:226
  41.0 12.7 %copy-start.2 = (bf16[256,256]{1,0:T(8,128)(2,1)S(1)}, bf16[256,256]{1,0:T(8,128)(2,1)}, u32[]{:S(2)}) copy-start(bf16[256,256]{1,0:T(8,128)(2,1)} %param.16) | copy-start | bytes 393220
  42.5 5.7 %collective-permute-start.2 = (s32[2,128,128]{2,1,0:T(8,128)S(1)}, s32[2,128,128]{2,1,0:T(8,128)S(1)}, u32[]{:S(2)}, u32[]{:S(2)}) collective-permute-start(s32[2,128,128]{2,1,0:T(8,128)S(1)} %pad_add_fusion.1), channel_id=1, source_target_pairs={{0,2},{2,0},{4,6},{6,4},{8,10},{10,8},{12,14},{14,12},{1,3},{3,1},... | collective-permute-start | bytes 393224 | tf_op jit(solution)/shard_map/ppermute | solution.py:226
  48.2 9.3 %collective-permute-start.3 = (s32[2,256,128]{2,1,0:T(8,128)S(1)}, s32[2,256,128]{2,1,0:T(8,128)S(1)}, u32[]{:S(2)}, u32[]{:S(2)}) collective-permute-start(s32[2,256,128]{2,1,0:T(8,128)S(1)} %pad_add_fusion), channel_id=1, source_target_pairs={{0,1},{1,0},{2,3},{3,2},{4,5},{5,4},{6,7},{7,6},{8,9},{9,8},{10,11... | collective-permute-start | bytes 786440 | tf_op jit(solution)/shard_map/ppermute | solution.py:223
  53.9 31.4 %all-to-all-start.1 = ((bf16[16,256,128]{2,1,0:T(8,128)(2,1)}), bf16[16,256,128]{2,1,0:T(8,128)(2,1)S(1)}, u32[]{:S(2)}, u32[]{:S(2)}) async-start(bf16[16,256,128]{2,1,0:T(8,128)(2,1)} %bitcast.3), calls=%async_computation.1 | async-start | bytes 2097152 | tf_op jit(solution)/shard_map/all_to_all | solution.py:211
  85.3 27.4 %copy-start.3 = (s32[1,1,256]{2,1,0:T(1,128)S(1)}, s32[1,1,256]{2,1,0:T(1,128)}, u32[]{:S(2)}) copy-start(s32[1,1,256]{2,1,0:T(1,128)} %param.15) | copy-start | bytes 3076
  97.8 3.1 %collective-permute-start.4 = (bf16[256,128]{1,0:T(8,128)(2,1)S(1)}, bf16[256,128]{1,0:T(8,128)(2,1)S(1)}, u32[]{:S(2)}, u32[]{:S(2)}) collective-permute-start(bf16[256,128]{1,0:T(8,128)(2,1)S(1)} %dynamic-slice_convert_fusion.1), channel_id=1, source_target_pairs={{0,1},{1,0},{2,3},{3,2},{4,5},{5,4},{6,7},{7,6},{8,9},{9,8},{10,11... | collective-permute-start | bytes 196616 | tf_op jit(solution)/shard_map/ppermute | solution.py:223
  99.7 22.2 %copy-start.4 = (bf16[256,256]{1,0:T(8,128)(2,1)S(1)}, bf16[256,256]{1,0:T(8,128)(2,1)}, u32[]{:S(2)}) copy-start(bf16[256,256]{1,0:T(8,128)(2,1)} %param.10) | copy-start | bytes 393220
  101.8 19.7 %all-to-all-start.2 = ((bf16[32,4,256]{2,1,0:T(4,128)(2,1)}), bf16[32,4,256]{2,1,0:T(4,128)(2,1)S(1)}, u32[]{:S(2)}, u32[]{:S(2)}) async-start(bf16[32,4,256]{2,1,0:T(4,128)(2,1)} %reshape.92), calls=%async_computation.2 | async-start | bytes 131072 | tf_op jit(solution)/shard_map/all_to_all | solution.py:198
  124.2 17.6 %all-to-all-start.3 = ((bf16[32,12,512]{2,1,0:T(8,128)(2,1)}), bf16[32,12,512]{2,1,0:T(8,128)(2,1)S(1)}, u32[]{:S(2)}, u32[]{:S(2)}) async-start(bf16[32,12,512]{2,1,0:T(8,128)(2,1)} %maximum_maximum_fusion), calls=%async_computation.3 | async-start | bytes 1048576 | tf_op jit(solution)/shard_map/all_to_all | solution.py:198
  198.2 3.1 %collective-permute-start.5 = (bf16[256,128]{1,0:T(8,128)(2,1)S(1)}, bf16[256,128]{1,0:T(8,128)(2,1)S(1)}, u32[]{:S(2)}, u32[]{:S(2)}) collective-permute-start(bf16[256,128]{1,0:T(8,128)(2,1)S(1)} %dynamic-slice_convert_fusion), channel_id=1, source_target_pairs={{0,1},{1,0},{2,3},{3,2},{4,5},{5,4},{6,7},{7,6},{8,9},{9,8},{10,11... | collective-permute-start | bytes 196616 | tf_op jit(solution)/shard_map/ppermute | solution.py:223
  202.6 18.3 %all-to-all-start.5 = ((bf16[32,20,256]{2,1,0:T(8,128)(2,1)}), bf16[32,20,256]{2,1,0:T(8,128)(2,1)S(1)}, u32[]{:S(2)}, u32[]{:S(2)}) async-start(bf16[32,20,256]{2,1,0:T(8,128)(2,1)} %pad_maximum_fusion.1), calls=%async_computation.5 | async-start | bytes 786432 | tf_op jit(solution)/shard_map/all_to_all | solution.py:198

commit v9 on v8

--- a/solution.py
+++ b/solution.py
@@ -273,7 +273,7 @@
     every = copies(jnp.concatenate([features[:early], late_rows], axis=0))
     every, words = lax.optimization_barrier((every, words))
     table = over_member(every)
-    words = with_theirs(words, 1)
+    words, table = lax.optimization_barrier((with_theirs(words, 1), table))
     by_dst, by_src = runs(jnp.concatenate([words, twin(words)], axis=1))
     totals = row_sums(by_dst, table)
     totals = totals + add_at_masters(over_dom(mirror_slots(totals)))

time: 226 us -> 222 us (0.982)
  waiting for transfers between devices: 70.2 us -> 64.8 us
  starting transfers between devices: 59.7 us -> 63.3 us
  Pallas kernels: 30.6 us -> 27.8 us
    all_to_all x1, waiting for transfers between devices: 27 us -> 0.27 us  [over_member(): lax.all_to_all(blocks, member, split_axis=0, concat_axis=0, tiled=True)]
    ppermute x3, waiting for transfers between devices: 7 us -> 28 us  [with_theirs(): theirs = lax.ppermute(words, 'y', [(y, y ^ bit) for y in range(chips)])]
    all_to_all x4, starting transfers between devices: 33.8 us -> 36.7 us  [over_dom(): return lax.all_to_all(slots, 'dom', split_axis=0, concat_axis=0, tiled=True)]
    pallas_call x2, Pallas kernels: 24.5 us -> 21.7 us  [edge_sums(): pl.pallas_call(edge_kernel, out_shape=jax.ShapeDtypeStruct((own, width),...]
    ppermute x3, starting transfers between devices: 9.29 us -> 6.72 us  [twin(): return lax.ppermute(values, 'core', [(0, 1), (1, 0)])]
    all_to_all x1, starting transfers between devices: 3.56 us -> 5.96 us  [over_member(): lax.all_to_all(blocks, member, split_axis=0, concat_axis=0, tiled=True)]
  transfers between devices with their start and end apart: 11 -> 11, of which waited for: 9 -> 10; matrix products, arithmetic and copies ran while one was open for 2% -> 2% of each run, Pallas kernels for 0% -> 0%
where the time goes in v9:
time: 222 us; the launch traced here: 220 us
  waiting for transfers between devices  64.8 us (29%)
  starting transfers between devices  63.3 us (29%)
  blocking collectives  45.5 us (20%)
  Pallas kernels  27.8 us (13%)
  other arithmetic  6.5 us (3%)
  local copies, waits for them, and re-layouts  6.13 us (3%)
  matrix products  5.17 us (2%)
    all_to_all x1, blocking collectives, over_member(): lax.all_to_all(blocks, member, split_axis=0, concat_axis=0, tiled=True)  45.5 us
    all_to_all x4, starting transfers between devices, over_dom(): return lax.all_to_all(slots, 'dom', split_axis=0, concat_axis=0, tiled=True)  36.7 us
    all_to_all x4, waiting for transfers between devices, over_dom(): return lax.all_to_all(slots, 'dom', split_axis=0, concat_axis=0, tiled=True)  33.7 us
    ppermute x3, waiting for transfers between devices, with_theirs(): theirs = lax.ppermute(words, 'y', [(y, y ^ bit) for y in range(chips)])  28 us
    pallas_call x2, Pallas kernels, edge_sums(): pl.pallas_call(edge_kernel, out_shape=jax.ShapeDtypeStruct((own, width),...  21.7 us
    ppermute x3, starting transfers between devices, with_theirs(): theirs = lax.ppermute(words, 'y', [(y, y ^ bit) for y in range(chips)])  14 us
    ppermute x3, starting transfers between devices, twin(): return lax.ppermute(values, 'core', [(0, 1), (1, 0)])  6.72 us
    pallas_call x1, Pallas kernels, sort_lists(): pl.pallas_call(sort_kernel, out_shape=jax.ShapeDtypeStruct(words.shape, w...  6.13 us
  transfers between devices with their start and end apart: 11, of which 10 were waited for; matrix products, arithmetic and copies ran while one was open for 2% of the time, Pallas kernels for 0%

profile of v9, /device:TPU:1, one launch (start us, length us, event | category | flops | bytes accessed | tf_op | source)
XLA Modules:
  0.0 220.5 jit_solution(15379824257003193116)
XLA Ops:
  1.6 1.1 convolution_convert_fusion.5
  3.4 1.4 fusion.29.words_ref
  4.8 6.1 %sort_lists.1 = s32[2,32,128]{2,1,0:T(8,128)} custom-call(s32[2,32,128]{2,1,0:T(8,128)} %fusion.29.words_ref), custom_call_target="tpu_custom_call" | custom-call | flops 8192000 | bytes 65536 | tf_op jit(solution)/shard_map/sort_lists/pallas_call | solution.py:48
  10.9 8.3 %collective-permute-start = (s32[2,32,128]{2,1,0:T(8,128)}, s32[2,32,128]{2,1,0:T(8,128)S(1)}, u32[]{:S(2)}, u32[]{:S(2)}) collective-permute-start(s32[2,32,128]{2,1,0:T(8,128)} %sort_lists.1), channel_id=1, source_target_pairs={{0,8},{2,10},{4,12},{6,14},{8,0},{10,2},{12,4},{14,6},{1,9},{3,11}... | collective-permute-start | bytes 98312 | tf_op jit(solution)/shard_map/ppermute | solution.py:226
  19.2 12.9 %all-to-all-start = ((bf16[32,4,256]{2,1,0:T(4,128)(2,1)}), bf16[32,4,256]{2,1,0:T(4,128)(2,1)S(1)}, u32[]{:S(2)}, u32[]{:S(2)}) async-start(bf16[32,4,256]{2,1,0:T(4,128)(2,1)} %reshape.89), calls=%async_computation | async-start | bytes 131072 | tf_op jit(solution)/shard_map/all_to_all | solution.py:198
  32.9 2.4 %collective-permute-start.1 = (s32[2,64,128]{2,1,0:T(8,128)S(1)}, s32[2,64,128]{2,1,0:T(8,128)S(1)}, u32[]{:S(2)}, u32[]{:S(2)}) collective-permute-start(s32[2,64,128]{2,1,0:T(8,128)S(1)} %pad_add_fusion.2), channel_id=1, source_target_pairs={{0,4},{2,6},{4,0},{6,2},{8,12},{10,14},{12,8},{14,10},{1,5},{3,7},... | collective-permute-start | bytes 196616 | tf_op jit(solution)/shard_map/ppermute | solution.py:226
  36.2 3.6 %collective-permute-done.1 = s32[2,64,128]{2,1,0:T(8,128)S(1)} collective-permute-done((s32[2,64,128]{2,1,0:T(8,128)S(1)}, s32[2,64,128]{2,1,0:T(8,128)S(1)}, u32[]{:S(2)}, u32[]{:S(2)}) %collective-permute-start.1) | collective-permute-done | bytes 65568 | tf_op jit(solution)/shard_map/ppermute | solution.py:226
  41.3 1.2 broadcast_in_dim.75
  42.5 6.0 %all-to-all-start.1 = ((bf16[16,256,128]{2,1,0:T(8,128)(2,1)}), bf16[16,256,128]{2,1,0:T(8,128)(2,1)S(1)}, u32[]{:S(2)}, u32[]{:S(2)}) async-start(bf16[16,256,128]{2,1,0:T(8,128)(2,1)} %bitcast.3), calls=%async_computation.1 | async-start | bytes 2097152 | tf_op jit(solution)/shard_map/all_to_all | solution.py:211
  48.5 3.3 %collective-permute-start.2 = (s32[2,128,128]{2,1,0:T(8,128)S(1)}, s32[2,128,128]{2,1,0:T(8,128)S(1)}, u32[]{:S(2)}, u32[]{:S(2)}) collective-permute-start(s32[2,128,128]{2,1,0:T(8,128)S(1)} %pad_add_fusion.1), channel_id=1, source_target_pairs={{0,2},{2,0},{4,6},{6,4},{8,10},{10,8},{12,14},{14,12},{1,3},{3,1},... | collective-permute-start | bytes 393224 | tf_op jit(solution)/shard_map/ppermute | solution.py:226
  51.8 24.4 %collective-permute-done.2 = s32[2,128,128]{2,1,0:T(8,128)S(1)} collective-permute-done((s32[2,128,128]{2,1,0:T(8,128)S(1)}, s32[2,128,128]{2,1,0:T(8,128)S(1)}, u32[]{:S(2)}, u32[]{:S(2)}) %collective-permute-start.2) | collective-permute-done | bytes 131104 | tf_op jit(solution)/shard_map/ppermute | solution.py:226
  76.5 2.5 %collective-permute-start.3 = (s32[2,256,128]{2,1,0:T(8,128)S(1)}, s32[2,256,128]{2,1,0:T(8,128)S(1)}, u32[]{:S(2)}, u32[]{:S(2)}) collective-permute-start(s32[2,256,128]{2,1,0:T(8,128)S(1)} %pad_add_fusion), channel_id=1, source_target_pairs={{0,1},{1,0},{2,3},{3,2},{4,5},{5,4},{6,7},{7,6},{8,9},{9,8},{10,11... | collective-permute-start | bytes 786440 | tf_op jit(solution)/shard_map/ppermute | solution.py:223
  81.0 10.7 %edge_sums.2 = f32[512,128]{1,0:T(8,128)S(1)} custom-call(s32[2,16]{1,0:T(2,128)S(1)} %bitcast.52, s32[65536]{0:T(1024)S(1)} %get-tuple-element.25.words_ref, bf16[16,256,128]{2,1,0:T(8,128)(2,1)S(1)} %all-to-all-done.1.table_ref), custom_call_target="tpu_custom_call" | custom-call | flops 2097152 | bytes 2097152 | tf_op jit(solution)/shard_map/edge_sums/pallas_call | solution.py:138
  91.7 2.3 %collective-permute-start.4 = (bf16[256,128]{1,0:T(8,128)(2,1)S(1)}, bf16[256,128]{1,0:T(8,128)(2,1)S(1)}, u32[]{:S(2)}, u32[]{:S(2)}) collective-permute-start(bf16[256,128]{1,0:T(8,128)(2,1)S(1)} %dynamic-slice_convert_fusion.1), channel_id=1, source_target_pairs={{0,1},{1,0},{2,3},{3,2},{4,5},{5,4},{6,7},{7,6},{8,9},{9,8},{10,11... | collective-permute-start | bytes 196616 | tf_op jit(solution)/shard_map/ppermute | solution.py:223
  95.8 12.7 %all-to-all-start.2 = ((bf16[32,4,256]{2,1,0:T(4,128)(2,1)}), bf16[32,4,256]{2,1,0:T(4,128)(2,1)S(1)}, u32[]{:S(2)}, u32[]{:S(2)}) async-start(bf16[32,4,256]{2,1,0:T(4,128)(2,1)} %reshape.92), calls=%async_computation.2 | async-start | bytes 131072 | tf_op jit(solution)/shard_map/all_to_all | solution.py:198
  108.5 8.9 %all-to-all-done.2 = bf16[32,4,256]{2,1,0:T(4,128)(2,1)S(1)} async-done(((bf16[32,4,256]{2,1,0:T(4,128)(2,1)}), bf16[32,4,256]{2,1,0:T(4,128)(2,1)S(1)}, u32[]{:S(2)}, u32[]{:S(2)}) %all-to-all-start.2) | async-done | bytes 65568 | tf_op jit(solution)/shard_map/all_to_all | solution.py:198
  120.0 3.9 %all-to-all-start.3 = ((bf16[32,12,512]{2,1,0:T(8,128)(2,1)}), bf16[32,12,512]{2,1,0:T(8,128)(2,1)S(1)}, u32[]{:S(2)}, u32[]{:S(2)}) async-start(bf16[32,12,512]{2,1,0:T(8,128)(2,1)} %maximum_maximum_fusion), calls=%async_computation.3 | async-start | bytes 1048576 | tf_op jit(solution)/shard_map/all_to_all | solution.py:198
  123.9 13.4 %all-to-all-done.3 = bf16[32,12,512]{2,1,0:T(8,128)(2,1)S(1)} async-done(((bf16[32,12,512]{2,1,0:T(8,128)(2,1)}), bf16[32,12,512]{2,1,0:T(8,128)(2,1)S(1)}, u32[]{:S(2)}, u32[]{:S(2)}) %all-to-all-start.3) | async-done | bytes 393248 | tf_op jit(solution)/shard_map/all_to_all | solution.py:198
  138.2 45.5 %all_to_all.30.table_ref = bf16[16,288,128]{2,1,0:T(8,128)(2,1)S(1)} all-to-all(bf16[16,288,128]{2,1,0:T(8,128)(2,1)S(1)} %pad_maximum_fusion), channel_id=1, replica_groups=mesh['dom'=32,'y'=8,'core'=2] {'y','core'}, dimensions={0} | all-to-all | bytes 2359296 | tf_op jit(solution)/shard_map/all_to_all | solution.py:211
  183.7 11.0 %edge_sums.3 = f32[512,128]{1,0:T(8,128)S(1)} custom-call(s32[2,16]{1,0:T(2,128)S(1)} %bitcast.51, s32[65536]{0:T(1024)S(1)} %get-tuple-element.24.words_ref, bf16[16,288,128]{2,1,0:T(8,128)(2,1)S(1)} %all_to_all.30.table_ref), custom_call_target="tpu_custom_call" | custom-call | flops 2097152 | bytes 2097152 | tf_op jit(solution)/shard_map/edge_sums/pallas_call | solution.py:138
  194.7 1.9 collective-permute-start.5
  196.7 1.1 collective-permute-done.5
  199.0 7.2 %all-to-all-start.5 = ((bf16[32,20,256]{2,1,0:T(8,128)(2,1)}), bf16[32,20,256]{2,1,0:T(8,128)(2,1)S(1)}, u32[]{:S(2)}, u32[]{:S(2)}) async-start(bf16[32,20,256]{2,1,0:T(8,128)(2,1)} %pad_maximum_fusion.1), calls=%async_computation.5 | async-start | bytes 786432 | tf_op jit(solution)/shard_map/all_to_all | solution.py:198
  207.4 11.0 %all-to-all-done.5 = bf16[32,20,256]{2,1,0:T(8,128)(2,1)S(1)} async-done(((bf16[32,20,256]{2,1,0:T(8,128)(2,1)}), bf16[32,20,256]{2,1,0:T(8,128)(2,1)S(1)}, u32[]{:S(2)}, u32[]{:S(2)}) %all-to-all-start.5) | async-done | bytes 327712 | tf_op jit(solution)/shard_map/all_to_all | solution.py:198
  (90 shorter events, 16.5 us)
Async XLA Ops:
  0.6 117.1 %copy-start = (bf16[256,256]{1,0:T(8,128)(2,1)S(1)}, bf16[256,256]{1,0:T(8,128)(2,1)}, u32[]{:S(2)}) copy-start(bf16[256,256]{1,0:T(8,128)(2,1)} %param.17) | copy-start | bytes 393220
  0.6 40.4 %copy-start.1 = (bf16[256,256]{1,0:T(8,128)(2,1)S(1)}, bf16[256,256]{1,0:T(8,128)(2,1)}, u32[]{:S(2)}) copy-start(bf16[256,256]{1,0:T(8,128)(2,1)} %param.9) | copy-start | bytes 393220
  0.7 40.6 %slice-start = ((bf16[256,256]{1,0:T(8,128)(2,1)}), bf16[192,256]{1,0:T(8,128)(2,1)S(1)}, s32[]{:S(2)}) async-start(bf16[256,256]{1,0:T(8,128)(2,1)} %param.9), calls=%async_computation.6 | async-start | bytes 196608 | tf_op jit(solution)/shard_map/slice | solution.py:273
  10.9 21.2 %collective-permute-start = (s32[2,32,128]{2,1,0:T(8,128)}, s32[2,32,128]{2,1,0:T(8,128)S(1)}, u32[]{:S(2)}, u32[]{:S(2)}) collective-permute-start(s32[2,32,128]{2,1,0:T(8,128)} %sort_lists.1), channel_id=1, source_target_pairs={{0,8},{2,10},{4,12},{6,14},{8,0},{10,2},{12,4},{14,6},{1,9},{3,11}... | collective-permute-start | bytes 98312 | tf_op jit(solution)/shard_map/ppermute | solution.py:226
  19.2 21.8 %all-to-all-start = ((bf16[32,4,256]{2,1,0:T(4,128)(2,1)}), bf16[32,4,256]{2,1,0:T(4,128)(2,1)S(1)}, u32[]{:S(2)}, u32[]{:S(2)}) async-start(bf16[32,4,256]{2,1,0:T(4,128)(2,1)} %reshape.89), calls=%async_computation | async-start | bytes 131072 | tf_op jit(solution)/shard_map/all_to_all | solution.py:198
  32.9 6.9 %collective-permute-start.1 = (s32[2,64,128]{2,1,0:T(8,128)S(1)}, s32[2,64,128]{2,1,0:T(8,128)S(1)}, u32[]{:S(2)}, u32[]{:S(2)}) collective-permute-start(s32[2,64,128]{2,1,0:T(8,128)S(1)} %pad_add_fusion.2), channel_id=1, source_target_pairs={{0,4},{2,6},{4,0},{6,2},{8,12},{10,14},{12,8},{14,10},{1,5},{3,7},... | collective-permute-start | bytes 196616 | tf_op jit(solution)/shard_map/ppermute | solution.py:226
  42.5 36.5 %copy-start.2 = (bf16[256,256]{1,0:T(8,128)(2,1)S(1)}, bf16[256,256]{1,0:T(8,128)(2,1)}, u32[]{:S(2)}) copy-start(bf16[256,256]{1,0:T(8,128)(2,1)} %param.16) | copy-start | bytes 393220
  42.5 33.9 %all-to-all-start.1 = ((bf16[16,256,128]{2,1,0:T(8,128)(2,1)}), bf16[16,256,128]{2,1,0:T(8,128)(2,1)S(1)}, u32[]{:S(2)}, u32[]{:S(2)}) async-start(bf16[16,256,128]{2,1,0:T(8,128)(2,1)} %bitcast.3), calls=%async_computation.1 | async-start | bytes 2097152 | tf_op jit(solution)/shard_map/all_to_all | solution.py:211
  48.5 27.7 %collective-permute-start.2 = (s32[2,128,128]{2,1,0:T(8,128)S(1)}, s32[2,128,128]{2,1,0:T(8,128)S(1)}, u32[]{:S(2)}, u32[]{:S(2)}) collective-permute-start(s32[2,128,128]{2,1,0:T(8,128)S(1)} %pad_add_fusion.1), channel_id=1, source_target_pairs={{0,2},{2,0},{4,6},{6,4},{8,10},{10,8},{12,14},{14,12},{1,3},{3,1},... | collective-permute-start | bytes 393224 | tf_op jit(solution)/shard_map/ppermute | solution.py:226
  76.5 3.7 %collective-permute-start.3 = (s32[2,256,128]{2,1,0:T(8,128)S(1)}, s32[2,256,128]{2,1,0:T(8,128)S(1)}, u32[]{:S(2)}, u32[]{:S(2)}) collective-permute-start(s32[2,256,128]{2,1,0:T(8,128)S(1)} %pad_add_fusion), channel_id=1, source_target_pairs={{0,1},{1,0},{2,3},{3,2},{4,5},{5,4},{6,7},{7,6},{8,9},{9,8},{10,11... | collective-permute-start | bytes 786440 | tf_op jit(solution)/shard_map/ppermute | solution.py:223
  81.0 27.5 %copy-start.3 = (s32[1,1,256]{2,1,0:T(1,128)S(1)}, s32[1,1,256]{2,1,0:T(1,128)}, u32[]{:S(2)}) copy-start(s32[1,1,256]{2,1,0:T(1,128)} %param.15) | copy-start | bytes 3076
  91.7 3.2 %collective-permute-start.4 = (bf16[256,128]{1,0:T(8,128)(2,1)S(1)}, bf16[256,128]{1,0:T(8,128)(2,1)S(1)}, u32[]{:S(2)}, u32[]{:S(2)}) collective-permute-start(bf16[256,128]{1,0:T(8,128)(2,1)S(1)} %dynamic-slice_convert_fusion.1), channel_id=1, source_target_pairs={{0,1},{1,0},{2,3},{3,2},{4,5},{5,4},{6,7},{7,6},{8,9},{9,8},{10,11... | collective-permute-start | bytes 196616 | tf_op jit(solution)/shard_map/ppermute | solution.py:223
  94.0 23.7 %copy-start.4 = (bf16[256,256]{1,0:T(8,128)(2,1)S(1)}, bf16[256,256]{1,0:T(8,128)(2,1)}, u32[]{:S(2)}) copy-start(bf16[256,256]{1,0:T(8,128)(2,1)} %param.10) | copy-start | bytes 393220
  95.8 21.6 %all-to-all-start.2 = ((bf16[32,4,256]{2,1,0:T(4,128)(2,1)}), bf16[32,4,256]{2,1,0:T(4,128)(2,1)S(1)}, u32[]{:S(2)}, u32[]{:S(2)}) async-start(bf16[32,4,256]{2,1,0:T(4,128)(2,1)} %reshape.92), calls=%async_computation.2 | async-start | bytes 131072 | tf_op jit(solution)/shard_map/all_to_all | solution.py:198
  120.0 17.3 %all-to-all-start.3 = ((bf16[32,12,512]{2,1,0:T(8,128)(2,1)}), bf16[32,12,512]{2,1,0:T(8,128)(2,1)S(1)}, u32[]{:S(2)}, u32[]{:S(2)}) async-start(bf16[32,12,512]{2,1,0:T(8,128)(2,1)} %maximum_maximum_fusion), calls=%async_computation.3 | async-start | bytes 1048576 | tf_op jit(solution)/shard_map/all_to_all | solution.py:198
  194.7 3.1 %collective-permute-start.5 = (bf16[256,128]{1,0:T(8,128)(2,1)S(1)}, bf16[256,128]{1,0:T(8,128)(2,1)S(1)}, u32[]{:S(2)}, u32[]{:S(2)}) collective-permute-start(bf16[256,128]{1,0:T(8,128)(2,1)S(1)} %dynamic-slice_convert_fusion), channel_id=1, source_target_pairs={{0,1},{1,0},{2,3},{3,2},{4,5},{5,4},{6,7},{7,6},{8,9},{9,8},{10,11... | collective-permute-start | bytes 196616 | tf_op jit(solution)/shard_map/ppermute | solution.py:223
  199.0 19.4 %all-to-all-start.5 = ((bf16[32,20,256]{2,1,0:T(8,128)(2,1)}), bf16[32,20,256]{2,1,0:T(8,128)(2,1)S(1)}, u32[]{:S(2)}, u32[]{:S(2)}) async-start(bf16[32,20,256]{2,1,0:T(8,128)(2,1)} %pad_maximum_fusion.1), calls=%async_computation.5 | async-start | bytes 786432 | tf_op jit(solution)/shard_map/all_to_all | solution.py:198
